TPU v7x, 32 devices: a whole 2x2x4 slice. The times are simulated.
32 devices in a mesh: cand: 4 (over x, core), seq: 8 (over z, y).
Axes of the slice: x: 2, y: 2, z: 4, core: 2. Of those that a mesh axis runs over, the one named last changes fastest.
Arguments:
- hyena_query: bfloat16 [4, 1024, 4096], P('cand', 'seq'), may hold values from -6 to 6
- hyena_key: bfloat16 [4, 1024, 4096], P('cand', 'seq'), may hold values from -6 to 6
- hyena_value: bfloat16 [4, 1024, 4096], P('cand', 'seq'), may hold values from -6 to 6
- hyena_filters: float32 [128, 256], replicated, may hold values from -0.5 to 0.5
- context_tail: bfloat16 [127, 4096], replicated, may hold values from -6 to 6
- cont_queries: bfloat16 [4, 1024, 32, 128], P('cand', 'seq'), may hold values from -100 to 100
- cont_keys: bfloat16 [4, 1024, 32, 128], P('cand', 'seq'), may hold values from -5 to 5
- cont_values: bfloat16 [4, 1024, 32, 128], P('cand', 'seq'), may hold values from -6 to 6
- context_keys: bfloat16 [768, 32, 128], P('seq'), may hold values from -6 to 6
- context_values: bfloat16 [768, 32, 128], P('seq'), may hold values from -6 to 6
- lengths: int32 [4], P('cand'), may hold values from 256 to 1024, as said below
Outputs:
- hyena_out: bfloat16 [4, 1024, 4096], P('cand', 'seq')
- attention_out: bfloat16 [4, 1024, 32, 128], P('cand', 'seq')
Inputs may be any that keep to these rules, and one draw needn't show every extreme that they name: `lengths`: positions of a candidate at or past its length are padding; some candidate has all 1024 positions valid.
All inputs are finite; a program needn't handle non-finite values.
Results may differ from a plain program's by a relative error of at most 0.0049.
Values may be sent and summed in bfloat16 or wider, within the bound.
No kernel may reach another device: no remote copies, remote signals or barrier semaphores. Data moves between devices by JAX's collectives and lax.ppermute only.
A program may use at most 64 MiB of HBM per device.

v0:
```python
import math

import jax
import jax.numpy as jnp
from jax import lax
from jax.sharding import PartitionSpec as P

CH_GROUP = 16


masked_score = -1e30


def shifted(x, axis, by):
    peers = lax.axis_size(axis)
    pairs = [(i, i + by) for i in range(peers) if 0 <= i + by < peers]
    return lax.ppermute(x, axis, pairs)


def merge_scores(carried, scores, value_rows):
    run_max, run_total, weighted = carried
    new_max = jnp.maximum(run_max, jnp.max(scores, axis=-1))
    weights = jnp.exp(scores - new_max[..., None])
    shrink = jnp.exp(run_max - new_max)
    new_total = run_total * shrink + jnp.sum(weights, axis=-1)
    mixed = jnp.einsum(
        "hqk,khd->hqd", weights.astype(jnp.bfloat16), value_rows, preferred_element_type=jnp.float32
    )
    return (new_max, new_total, weighted * shrink[..., None] + mixed)


def fold_context(carried, queries, key_rows, value_rows):
    scaling = 1.0 / math.sqrt(queries.shape[-1])

    def per_block(operands):
        run_max, run_total, weighted, query_block = operands
        scores = (
            jnp.einsum("hqd,khd->hqk", query_block, key_rows, preferred_element_type=jnp.float32)
            * scaling
        )
        return merge_scores((run_max, run_total, weighted), scores, value_rows)

    return lax.map(per_block, (carried[0], carried[1], carried[2], queries))


def fold_own(carried, queries, key_rows, value_rows):
    scaling = 1.0 / math.sqrt(queries.shape[-1])
    block_rows = queries.shape[2]
    key_places = jnp.arange(key_rows.shape[0])

    def per_block(operands):
        run_max, run_total, weighted, query_block, index = operands
        query_places = index * block_rows + jnp.arange(block_rows)
        scores = (
            jnp.einsum("hqd,khd->hqk", query_block, key_rows, preferred_element_type=jnp.float32)
            * scaling
        )
        allowed = key_places[None, :] <= query_places[:, None]
        scores = jnp.where(allowed[None], scores, masked_score)
        return merge_scores((run_max, run_total, weighted), scores, value_rows)

    return lax.map(
        per_block, (carried[0], carried[1], carried[2], queries, jnp.arange(queries.shape[0]))
    )


def local(
    hyena_query,
    hyena_key,
    hyena_value,
    hyena_filters,
    context_tail,
    cont_queries,
    cont_keys,
    cont_values,
    context_keys,
    context_values,
    lengths,
):
    rows = hyena_key.shape[1]
    taps = hyena_filters.shape[0]
    product = (hyena_key.astype(jnp.float32) * hyena_value.astype(jnp.float32)).astype(jnp.bfloat16)
    received = shifted(product[:, rows - (taps - 1) :, :], "seq", 1)
    is_first = lax.axis_index("seq") == 0
    earlier = jnp.where(is_first, context_tail[None], received)
    extended = jnp.concatenate([earlier, product], axis=1).astype(jnp.float32)
    per_channel = jnp.repeat(hyena_filters, CH_GROUP, axis=1)
    kernel = per_channel[::-1][:, None, :]
    convolved = lax.conv_general_dilated(
        extended,
        kernel,
        (1,),
        "VALID",
        dimension_numbers=("NWC", "WIO", "NWC"),
        feature_group_count=extended.shape[2],
        precision=lax.Precision.HIGHEST,
    )
    places = lax.axis_index("seq") * rows + jnp.arange(rows)
    keep = places[None, :] < lengths[:, None]
    hyena_out = jnp.where(
        keep[:, :, None], hyena_query.astype(jnp.float32) * convolved, 0.0
    ).astype(jnp.bfloat16)
    shared_keys, shared_values = (
        lax.all_to_all(context_keys, "seq", split_axis=1, concat_axis=0, tiled=True),
        lax.all_to_all(context_values, "seq", split_axis=1, concat_axis=0, tiled=True),
    )

    def single(operands):
        query_rows, key_rows, value_rows = operands
        length_all, heads_local, width = query_rows.shape
        block_rows = min(512, length_all)
        count = length_all // block_rows
        queries = query_rows.reshape(count, block_rows, heads_local, width).transpose(0, 2, 1, 3)
        carried = (
            jnp.full((count, heads_local, block_rows), masked_score, jnp.float32),
            jnp.zeros((count, heads_local, block_rows), jnp.float32),
            jnp.zeros((count, heads_local, block_rows, width), jnp.float32),
        )
        carried = fold_context(carried, queries, shared_keys, shared_values)
        carried = fold_own(carried, queries, key_rows, value_rows)
        result = carried[2] / carried[1][..., None]
        return (
            result.transpose(0, 2, 1, 3)
            .reshape(length_all, heads_local, width)
            .astype(jnp.bfloat16)
        )

    attended = lax.map(
        single,
        (
            lax.all_to_all(cont_queries, "seq", split_axis=2, concat_axis=1, tiled=True),
            lax.all_to_all(cont_keys, "seq", split_axis=2, concat_axis=1, tiled=True),
            lax.all_to_all(cont_values, "seq", split_axis=2, concat_axis=1, tiled=True),
        ),
    )
    attention = lax.all_to_all(attended, "seq", split_axis=1, concat_axis=2, tiled=True)
    attention_out = jnp.where(keep[:, :, None, None], attention, jnp.zeros((), jnp.bfloat16))
    return (hyena_out, attention_out)


def solution(mesh):
    placed = (
        P("cand", "seq", None),
        P("cand", "seq", None),
        P("cand", "seq", None),
        P(),
        P(),
        P("cand", "seq", None, None),
        P("cand", "seq", None, None),
        P("cand", "seq", None, None),
        P("seq", None, None),
        P("seq", None, None),
        P("cand"),
    )
    return jax.shard_map(
        local,
        mesh=mesh,
        in_specs=placed,
        out_specs=(P("cand", "seq", None), P("cand", "seq", None, None)),
        check_vma=False,
    )
```

profile of v0, /device:TPU:0, one launch (start us, length us, event | category | flops | bytes accessed | tf_op | source)
XLA Modules:
  0.0 219.9 jit_solution(15558829470086904448)
XLA Ops:
  0.6 2.4 %copy.88 = bf16[96,32,128]{2,0,1:T(8,128)(2,1)} copy(bf16[96,32,128]{2,1,0:T(8,128)(2,1)} %param.23) | data formatting | bytes 1572864 | tf_op args[8]
  3.0 7.3 %all-to-all-start.1 = ((bf16[96,32,128]{2,0,1:T(8,128)(2,1)}), bf16[96,32,128]{2,0,1:T(8,128)(2,1)S(1)}, u32[]{:S(2)}, u32[]{:S(2)}) async-start(bf16[96,32,128]{2,0,1:T(8,128)(2,1)} %copy.88), calls=%async_computation.1 | async-start | bytes 1572864 | tf_op jit(solution)/shard_map/all_to_all | solution.py:104
  11.5 19.0 %all-to-all-done.1 = bf16[96,32,128]{2,0,1:T(8,128)(2,1)S(1)} async-done(((bf16[96,32,128]{2,0,1:T(8,128)(2,1)}), bf16[96,32,128]{2,0,1:T(8,128)(2,1)S(1)}, u32[]{:S(2)}, u32[]{:S(2)}) %all-to-all-start.1) | async-done | bytes 786464 | tf_op jit(solution)/shard_map/all_to_all | solution.py:104
  30.5 3.6 %all-to-all-start.2 = ((bf16[96,32,128]{2,0,1:T(8,128)(2,1)}), bf16[96,32,128]{2,0,1:T(8,128)(2,1)S(1)}, u32[]{:S(2)}, u32[]{:S(2)}) async-start(bf16[96,32,128]{2,0,1:T(8,128)(2,1)} %copy.90), calls=%async_computation.2 | async-start | bytes 1572864 | tf_op jit(solution)/shard_map/all_to_all | solution.py:105
  34.1 2.6 %copy.86 = bf16[1,128,32,128]{3,1,0,2:T(8,128)(2,1)} copy(bf16[1,128,32,128]{3,2,1,0:T(8,128)(2,1)} %param.20) | data formatting | bytes 2097152 | tf_op args[5]
  36.7 17.8 %all-to-all-done.2 = bf16[96,32,128]{2,0,1:T(8,128)(2,1)S(1)} async-done(((bf16[96,32,128]{2,0,1:T(8,128)(2,1)}), bf16[96,32,128]{2,0,1:T(8,128)(2,1)S(1)}, u32[]{:S(2)}, u32[]{:S(2)}) %all-to-all-start.2) | async-done | bytes 786464 | tf_op jit(solution)/shard_map/all_to_all | solution.py:105
  55.3 3.6 %all-to-all-start = ((bf16[1,128,32,128]{3,1,0,2:T(8,128)(2,1)}), bf16[1,128,32,128]{3,1,0,2:T(8,128)(2,1)S(1)}, u32[]{:S(2)}, u32[]{:S(2)}) async-start(bf16[1,128,32,128]{3,1,0,2:T(8,128)(2,1)} %copy.86), calls=%async_computation | async-start | bytes 2097152 | tf_op jit(solution)/shard_map/all_to_all | solution.py:131
  61.7 5.0 %collective-permute-start = (bf16[1,127,4096]{2,1,0:T(8,128)(2,1)}, bf16[1,127,4096]{2,1,0:T(8,128)(2,1)}, u32[]{:S(2)}, u32[]{:S(2)}) collective-permute-start(bf16[1,127,4096]{2,1,0:T(8,128)(2,1)} %slice.4), channel_id=1, source_target_pairs={{0,1},{1,2},{2,3},{3,4},{4,5},{5,6},{6,7},{8,9},{9,10},{10,11},{11... | collective-permute-start | bytes 3121160 | tf_op jit(solution)/shard_map/ppermute | solution.py:17
  68.1 16.7 %all-to-all-done = bf16[1,128,32,128]{3,1,0,2:T(8,128)(2,1)S(1)} async-done(((bf16[1,128,32,128]{3,1,0,2:T(8,128)(2,1)}), bf16[1,128,32,128]{3,1,0,2:T(8,128)(2,1)S(1)}, u32[]{:S(2)}, u32[]{:S(2)}) %all-to-all-start) | async-done | bytes 1048608 | tf_op jit(solution)/shard_map/all_to_all | solution.py:131
  84.8 4.2 %all-to-all-start.3 = ((bf16[1,128,32,128]{3,1,0,2:T(8,128)(2,1)}), bf16[1,128,32,128]{3,1,0,2:T(8,128)(2,1)}, u32[]{:S(2)}, u32[]{:S(2)}) async-start(bf16[1,128,32,128]{3,1,0,2:T(8,128)(2,1)} %copy.93), calls=%async_computation.3 | async-start | bytes 2097152 | tf_op jit(solution)/shard_map/all_to_all | solution.py:132
  91.5 11.4 %rev.3 = f32[128,4096]{0,1:T(8,128)} reverse(f32[128,4096]{0,1:T(8,128)S(1)} %bitcast.120), dimensions={0} | reverse | bytes 4194304 | tf_op jit(solution)/shard_map/rev | solution.py:88
  103.0 5.8 %copy.85 = f32[128,1,4096]{2,1,0:T(1,128)} copy(f32[128,1,4096]{0,2,1:T(8,128)} %bitcast.121) | data formatting | bytes 4194304 | tf_op jit(solution)/shard_map/broadcast_in_dim | solution.py:88
  111.7 3.0 %all-to-all-done.3 = bf16[1,128,32,128]{3,1,0,2:T(8,128)(2,1)} async-done(((bf16[1,128,32,128]{3,1,0,2:T(8,128)(2,1)}), bf16[1,128,32,128]{3,1,0,2:T(8,128)(2,1)}, u32[]{:S(2)}, u32[]{:S(2)}) %all-to-all-start.3) | async-done | bytes 1048608 | tf_op jit(solution)/shard_map/all_to_all | solution.py:132
  114.7 21.7 %all-to-all-start.4 = ((bf16[1,128,32,128]{3,1,0,2:T(8,128)(2,1)}), bf16[1,128,32,128]{3,1,0,2:T(8,128)(2,1)}, u32[]{:S(2)}, u32[]{:S(2)}) async-start(bf16[1,128,32,128]{3,1,0,2:T(8,128)(2,1)} %copy.95), calls=%async_computation.4 | async-start | bytes 2097152 | tf_op jit(solution)/shard_map/all_to_all | solution.py:133
  137.7 10.9 %while.40 = (s32[]{:T(128)}, f32[2,4,512]{2,1,0:T(4,128)S(1)}, f32[2,4,512]{2,1,0:T(4,128)S(1)}, f32[2,4,512,128]{3,2,1,0:T(8,128)}, bf16[2,4,512,128]{3,2,1,0:T...) while((s32[]{:T(128)}, f32[2,4,512]{2,1,0:T(4,128)S(1)}, ...), condition=%wide.region_3.4_spmd, body=%wide.region_0.3_spmd.sunk | while | flops 818161664 | bytes 42041524 | solution.py:43
  148.6 13.9 %all-to-all-done.4 = bf16[1,128,32,128]{3,1,0,2:T(8,128)(2,1)} async-done(((bf16[1,128,32,128]{3,1,0,2:T(8,128)(2,1)}), bf16[1,128,32,128]{3,1,0,2:T(8,128)(2,1)}, u32[]{:S(2)}, u32[]{:S(2)}) %all-to-all-start.4) | async-done | bytes 1048608 | tf_op jit(solution)/shard_map/all_to_all | solution.py:133
  163.8 18.9 %while.41 = (s32[]{:T(128)}, f32[2,4,512]{2,0,1:T(2,128)S(1)}, f32[2,4,512,128]{3,2,0,1:T(8,128)}, f32[2,4,512]{2,1,0:T(4,128)S(1)}, f32[2,4,512]{2,1,0:T(4,128)...) while((s32[]{:T(128)}, f32[2,4,512]{2,0,1:T(2,128)S(1)}, ...), condition=%wide.region_7.8_spmd.clone, body=%wide.region_4.7_spmd.clone.sunk | while | flops 1097867776 | bytes 57299200 | solution.py:62
  167.6 3.0 %fusion.88 = f32[2,4,512,128]{3,2,0,1:T(8,128)S(1)} fusion(f32[2,4,512,128]{3,2,0,1:T(8,128)S(1)} %copy-done.6, s32[]{:T(128)} %get-tuple-element.430, bf16[1024,4,128]{2,0,1:T(8,128)(2,1)S(1)} %get-tuple-element.452, f32[4,512,1024]{2,1,0:T(8,128)S(1)} %get-tuple-element.389, f32[4,512]{1,0:T(4,128)S(1)} %get-tuple-element.391, ...), kind=kOutput, calls=%fused_computation.34.clone.1 | convolution fusion | flops 545783808 | bytes 12075012 | tf_op jit(solution)/shard_map/while/body/eval_jaxpr/while/body/eval_jaxpr/hqk,khd->hqd/dot_general | solution.py:26
  170.6 2.5 %fusion.86 = f32[4,512]{1,0:T(4,128)S(1)} fusion(f32[4,512,1024]{2,1,0:T(8,128)S(1)} %get-tuple-element.389, f32[4,512]{1,0:T(4,128)S(1)} %get-tuple-element.391, pred[512,1024]{1,0:T(8,128)(4,1)S(1)} %iota_compare_fusion.2), kind=kLoop, calls=%fused_computation.28.clone.1 | loop fusion | flops 8386560 | bytes 8929280 | tf_op jit(solution)/shard_map/while/body/eval_jaxpr/while/body/eval_jaxpr/reduce_sum | solution.py:25
  177.1 3.0 %fusion.88 = f32[2,4,512,128]{3,2,0,1:T(8,128)S(1)} fusion(f32[2,4,512,128]{3,2,0,1:T(8,128)S(1)} %copy-done.6, s32[]{:T(128)} %get-tuple-element.430, bf16[1024,4,128]{2,0,1:T(8,128)(2,1)S(1)} %get-tuple-element.452, f32[4,512,1024]{2,1,0:T(8,128)S(1)} %get-tuple-element.389, f32[4,512]{1,0:T(4,128)S(1)} %get-tuple-element.391, ...), kind=kOutput, calls=%fused_computation.34.clone.1 | convolution fusion | flops 545783808 | bytes 12075012 | tf_op jit(solution)/shard_map/while/body/eval_jaxpr/while/body/eval_jaxpr/hqk,khd->hqd/dot_general | solution.py:26
  180.1 2.5 %fusion.86 = f32[4,512]{1,0:T(4,128)S(1)} fusion(f32[4,512,1024]{2,1,0:T(8,128)S(1)} %get-tuple-element.389, f32[4,512]{1,0:T(4,128)S(1)} %get-tuple-element.391, pred[512,1024]{1,0:T(8,128)(4,1)S(1)} %iota_compare_fusion.2), kind=kLoop, calls=%fused_computation.28.clone.1 | loop fusion | flops 8386560 | bytes 8929280 | tf_op jit(solution)/shard_map/while/body/eval_jaxpr/while/body/eval_jaxpr/reduce_sum | solution.py:25
  186.5 3.6 %all-to-all-start.5 = ((bf16[1,1024,4,128]{3,2,0,1:T(4,128)(2,1)}), bf16[1,1024,4,128]{3,2,0,1:T(4,128)(2,1)S(1)}, u32[]{:S(2)}, u32[]{:S(2)}) async-start(bf16[1,1024,4,128]{3,2,0,1:T(4,128)(2,1)} %copy.100), calls=%async_computation.5 | async-start | bytes 2097152 | tf_op jit(solution)/shard_map/all_to_all | solution.py:136
  190.2 25.6 %fusion.53 = bf16[1,128,4096]{2,0,1:T(2,128)(2,1)S(1)} fusion(f32[128,1,4096]{2,1,0:T(1,128)S(1)} %copy-done.8, bf16[1,255,4096]{2,1,0:T(8,128)(2,1)} %pad_maximum_fusion, pred[128]{0:T(512)(128)(4,1)S(1)} %add_compare_fusion, bf16[1,128,4096]{2,1,0:T(8,128)(2,1)} %param.15), kind=kOutput, calls=%fused_computation.53 | convolution fusion | flops 807403520 | bytes 6283392 | tf_op jit(solution)/shard_map/conv_general_dilated | solution.py:89
  215.8 2.1 copy.103
  (106 shorter events, 36.6 us)
Async XLA Ops:
  0.6 9.7 %copy-start.13 = (bf16[96,32,128]{2,1,0:T(8,128)(2,1)S(1)}, bf16[96,32,128]{2,1,0:T(8,128)(2,1)}, u32[]{:S(2)}) copy-start(bf16[96,32,128]{2,1,0:T(8,128)(2,1)} %param.24) | copy-start | bytes 2359300
  3.0 27.5 %all-to-all-start.1 = ((bf16[96,32,128]{2,0,1:T(8,128)(2,1)}), bf16[96,32,128]{2,0,1:T(8,128)(2,1)S(1)}, u32[]{:S(2)}, u32[]{:S(2)}) async-start(bf16[96,32,128]{2,0,1:T(8,128)(2,1)} %copy.88), calls=%async_computation.1 | async-start | bytes 1572864 | tf_op jit(solution)/shard_map/all_to_all | solution.py:104
  11.5 47.4 %copy-start.9 = (bf16[1,128,4096]{2,1,0:T(8,128)(2,1)S(1)}, bf16[1,128,4096]{2,1,0:T(8,128)(2,1)}, u32[]{:S(2)}) copy-start(bf16[1,128,4096]{2,1,0:T(8,128)(2,1)} %param.17) | copy-start | bytes 3145732
  30.5 24.8 %copy-start.2 = (bf16[96,32,128]{2,0,1:T(8,128)(2,1)}, bf16[96,32,128]{2,0,1:T(8,128)(2,1)S(1)}, u32[]{:S(2)}) copy-start(bf16[96,32,128]{2,0,1:T(8,128)(2,1)S(1)} %all-to-all-done.1) | copy-start | bytes 2359300
  30.5 23.9 %all-to-all-start.2 = ((bf16[96,32,128]{2,0,1:T(8,128)(2,1)}), bf16[96,32,128]{2,0,1:T(8,128)(2,1)S(1)}, u32[]{:S(2)}, u32[]{:S(2)}) async-start(bf16[96,32,128]{2,0,1:T(8,128)(2,1)} %copy.90), calls=%async_computation.2 | async-start | bytes 1572864 | tf_op jit(solution)/shard_map/all_to_all | solution.py:105
  55.3 29.5 %all-to-all-start = ((bf16[1,128,32,128]{3,1,0,2:T(8,128)(2,1)}), bf16[1,128,32,128]{3,1,0,2:T(8,128)(2,1)S(1)}, u32[]{:S(2)}, u32[]{:S(2)}) async-start(bf16[1,128,32,128]{3,1,0,2:T(8,128)(2,1)} %copy.86), calls=%async_computation | async-start | bytes 2097152 | tf_op jit(solution)/shard_map/all_to_all | solution.py:131
  58.9 7.8 %copy-start.10 = (bf16[1,128,32,128]{3,2,1,0:T(8,128)(2,1)S(1)}, bf16[1,128,32,128]{3,2,1,0:T(8,128)(2,1)}, u32[]{:S(2)}) copy-start(bf16[1,128,32,128]{3,2,1,0:T(8,128)(2,1)} %param.21) | copy-start | bytes 3145732
  60.5 28.6 %copy-start.11 = (bf16[1,128,32,128]{3,2,1,0:T(8,128)(2,1)S(1)}, bf16[1,128,32,128]{3,2,1,0:T(8,128)(2,1)}, u32[]{:S(2)}) copy-start(bf16[1,128,32,128]{3,2,1,0:T(8,128)(2,1)} %param.22) | copy-start | bytes 3145732
  61.7 29.5 %copy-start.15 = (f32[128,256]{1,0:T(8,128)S(1)}, f32[128,256]{1,0:T(8,128)}, u32[]{:S(2)}) copy-start(f32[128,256]{1,0:T(8,128)} %param.18) | copy-start | bytes 393220
  61.7 47.0 %collective-permute-start = (bf16[1,127,4096]{2,1,0:T(8,128)(2,1)}, bf16[1,127,4096]{2,1,0:T(8,128)(2,1)}, u32[]{:S(2)}, u32[]{:S(2)}) collective-permute-start(bf16[1,127,4096]{2,1,0:T(8,128)(2,1)} %slice.4), channel_id=1, source_target_pairs={{0,1},{1,2},{2,3},{3,4},{4,5},{5,6},{6,7},{8,9},{9,10},{10,11},{11... | collective-permute-start | bytes 3121160 | tf_op jit(solution)/shard_map/ppermute | solution.py:17
  84.8 6.4 %copy-start = (bf16[1,128,32,128]{3,1,0,2:T(8,128)(2,1)}, bf16[1,128,32,128]{3,1,0,2:T(8,128)(2,1)S(1)}, u32[]{:S(2)}) copy-start(bf16[1,128,32,128]{3,1,0,2:T(8,128)(2,1)S(1)} %all-to-all-done) | copy-start | bytes 3145732
  84.8 29.9 %all-to-all-start.3 = ((bf16[1,128,32,128]{3,1,0,2:T(8,128)(2,1)}), bf16[1,128,32,128]{3,1,0,2:T(8,128)(2,1)}, u32[]{:S(2)}, u32[]{:S(2)}) async-start(bf16[1,128,32,128]{3,1,0,2:T(8,128)(2,1)} %copy.93), calls=%async_computation.3 | async-start | bytes 2097152 | tf_op jit(solution)/shard_map/all_to_all | solution.py:132
  103.0 5.8 %copy-start.12 = (bf16[127,4096]{1,0:T(8,128)(2,1)S(1)}, bf16[127,4096]{1,0:T(8,128)(2,1)}, u32[]{:S(2)}) copy-start(bf16[127,4096]{1,0:T(8,128)(2,1)} %param.19) | copy-start | bytes 3121156
  108.9 2.6 %copy-start.1 = (bf16[1,128,32,128]{3,1,0,2:T(8,128)(2,1)S(1)}, bf16[1,128,32,128]{3,1,0,2:T(8,128)(2,1)}, u32[]{:S(2)}) copy-start(bf16[1,128,32,128]{3,1,0,2:T(8,128)(2,1)} %copy-done) | copy-start | bytes 3145732
  114.7 47.7 %all-to-all-start.4 = ((bf16[1,128,32,128]{3,1,0,2:T(8,128)(2,1)}), bf16[1,128,32,128]{3,1,0,2:T(8,128)(2,1)}, u32[]{:S(2)}, u32[]{:S(2)}) async-start(bf16[1,128,32,128]{3,1,0,2:T(8,128)(2,1)} %copy.95), calls=%async_computation.4 | async-start | bytes 2097152 | tf_op jit(solution)/shard_map/all_to_all | solution.py:133
  137.7 1.8 copy-start.16
  143.2 1.8 copy-start.16
  165.4 1.8 copy-start.6
  165.4 2.2 %copy-start.18 = (f32[2,4,512,128]{3,2,1,0:T(8,128)S(1)}, f32[2,4,512,128]{3,2,1,0:T(8,128)}, u32[]{:S(2)}) copy-start(f32[2,4,512,128]{3,2,1,0:T(8,128)} %get-tuple-element.451) | copy-start | bytes 6291460 | tf_op jit(solution)/shard_map/while/body/eval_jaxpr/while
  170.6 2.5 %copy-start.7 = (f32[2,4,512,128]{3,2,0,1:T(8,128)}, f32[2,4,512,128]{3,2,0,1:T(8,128)S(1)}, u32[]{:S(2)}) copy-start(f32[2,4,512,128]{3,2,0,1:T(8,128)S(1)} %fusion.88) | copy-start | bytes 6291460 | tf_op jit(solution)/shard_map/while/body/eval_jaxpr/while
  174.8 2.2 %copy-start.18 = (f32[2,4,512,128]{3,2,1,0:T(8,128)S(1)}, f32[2,4,512,128]{3,2,1,0:T(8,128)}, u32[]{:S(2)}) copy-start(f32[2,4,512,128]{3,2,1,0:T(8,128)} %get-tuple-element.451) | copy-start | bytes 6291460 | tf_op jit(solution)/shard_map/while/body/eval_jaxpr/while
  180.0 2.5 %copy-start.7 = (f32[2,4,512,128]{3,2,0,1:T(8,128)}, f32[2,4,512,128]{3,2,0,1:T(8,128)S(1)}, u32[]{:S(2)}) copy-start(f32[2,4,512,128]{3,2,0,1:T(8,128)S(1)} %fusion.88) | copy-start | bytes 6291460 | tf_op jit(solution)/shard_map/while/body/eval_jaxpr/while
  182.6 7.5 %copy-start.8 = (f32[128,1,4096]{2,1,0:T(1,128)S(1)}, f32[128,1,4096]{2,1,0:T(1,128)}, u32[]{:S(2)}) copy-start(f32[128,1,4096]{2,1,0:T(1,128)} %copy.85) | copy-start | bytes 6291460
  186.5 31.3 %all-to-all-start.5 = ((bf16[1,1024,4,128]{3,2,0,1:T(4,128)(2,1)}), bf16[1,1024,4,128]{3,2,0,1:T(4,128)(2,1)S(1)}, u32[]{:S(2)}, u32[]{:S(2)}) async-start(bf16[1,1024,4,128]{3,2,0,1:T(4,128)(2,1)} %copy.100), calls=%async_computation.5 | async-start | bytes 2097152 | tf_op jit(solution)/shard_map/all_to_all | solution.py:136
  (8 other events, 11.5 us)
where the time goes:
time: 221 us; the launch traced here: 220 us
  waiting for transfers between devices  70.4 us (32%)
  starting transfers between devices  49 us (22%)
  local copies, waits for them, and re-layouts  41.8 us (19%)
  matrix products  41.2 us (19%)
  other arithmetic  14.3 us (6%)
    conv_general_dilated x1, matrix products, local(): lax.conv_general_dilated(extended, kernel, (1,), 'VALID', dimension_numbe...  25.6 us
    all_to_all x1, starting transfers between devices, local(): lax.all_to_all(cont_values, 'seq', split_axis=2, concat_axis=1, tiled=True)  21.7 us
    all_to_all x1, waiting for transfers between devices, local(): lax.all_to_all(context_keys, 'seq', split_axis=1, concat_axis=0, tiled=True)  19 us
    all_to_all x1, waiting for transfers between devices, local(): lax.all_to_all(context_values, 'seq', split_axis=1, concat_axis=0, tiled=...  17.8 us
    all_to_all x1, waiting for transfers between devices, local(): lax.all_to_all(cont_queries, 'seq', split_axis=2, concat_axis=1, tiled=True)  16.7 us
    all_to_all x1, waiting for transfers between devices, local(): lax.all_to_all(cont_values, 'seq', split_axis=2, concat_axis=1, tiled=True)  13.9 us
    unnamed x34, local copies, waits for them, and re-layouts  13.9 us
    rev x1, local copies, waits for them, and re-layouts, local(): kernel = per_channel[::-1][:, None, :]  11.4 us
  transfers between devices with their start and end apart: 7, of which 5 were waited for; matrix products, arithmetic and copies ran while one was open for 31% of the time, Pallas kernels for 0%

commit v1 on v0

v1 whole, which is shorter than its diff:
```python
import functools
import math

import jax
import jax.numpy as jnp
from jax import lax
from jax.experimental import pallas as pl
from jax.experimental.pallas import tpu as pltpu
from jax.sharding import PartitionSpec as P

CH_GROUP = 16
LANES = 128

masked_score = -1e30


def hyena_kernel(length_ref, first_ref, query_ref, key_ref, value_ref, before_ref, tail_ref, wave_ref, out_ref):
    rows, lanes = key_ref.shape[1], key_ref.shape[2]
    product = (key_ref[0].astype(jnp.float32) * value_ref[0].astype(jnp.float32)).astype(jnp.bfloat16)
    first = jnp.broadcast_to(first_ref[0], (rows, lanes)) == 1
    earlier = jnp.where(first, tail_ref[...].astype(jnp.float32), before_ref[0].astype(jnp.float32))
    extended = jnp.concatenate([earlier.astype(jnp.bfloat16), product], axis=0)
    channel = lax.broadcasted_iota(jnp.int32, (rows, lanes), 1) // CH_GROUP
    convolved = jnp.zeros((rows, lanes), jnp.float32)
    for group in range(lanes // CH_GROUP):
        wave = jnp.broadcast_to(wave_ref[group : group + 1, :], (rows, 2 * rows))
        taps = pltpu.roll(wave, 0, 1, stride=1, stride_axis=0)
        high = taps.astype(jnp.bfloat16)
        low = (taps - high.astype(jnp.float32)).astype(jnp.bfloat16)
        term = jnp.dot(high, extended, preferred_element_type=jnp.float32) + jnp.dot(
            low, extended, preferred_element_type=jnp.float32
        )
        convolved = jnp.where(channel == group, term, convolved)
    places = lax.broadcasted_iota(jnp.int32, (rows, lanes), 0)
    gated = query_ref[0].astype(jnp.float32) * convolved
    out_ref[0] = jnp.where(places < length_ref[0], gated, 0.0).astype(jnp.bfloat16)


def hyena(query, key, value, received, tail, filters, left, first):
    _, rows, channels = key.shape
    wave = jnp.pad(filters[::-1], ((1, 2 * rows - filters.shape[0] - 1), (0, 0))).T
    tail = jnp.pad(tail, ((1, 0), (0, 0)))
    groups = LANES // CH_GROUP
    block = pl.BlockSpec((1, rows, LANES), lambda i: (0, 0, i))
    scalar = pl.BlockSpec(memory_space=pltpu.SMEM)
    return pl.pallas_call(
        hyena_kernel,
        grid=(channels // LANES,),
        out_shape=jax.ShapeDtypeStruct(query.shape, jnp.bfloat16),
        in_specs=[
            scalar,
            scalar,
            block,
            block,
            block,
            block,
            pl.BlockSpec((rows, LANES), lambda i: (0, i)),
            pl.BlockSpec((groups, 2 * rows), lambda i: (i, 0)),
        ],
        out_specs=block,
        cost_estimate=pl.CostEstimate(
            flops=2 * 2 * rows * 2 * rows * channels * groups, bytes_accessed=12 * rows * channels, transcendentals=0
        ),
        name="hyena",
    )(left, first, query, key, value, received, tail, wave)


def attend_kernel(block_rows, q_ref, k_ref, v_ref, ck_ref, cv_ref, out_ref):
    sources, _, rows, width = q_ref.shape
    length = sources * rows
    scaling = 1.0 / math.sqrt(width)
    context = ck_ref.shape[1] * ck_ref.shape[3]
    context_keys = ck_ref[0, :, 0].reshape(context, width)
    context_values = cv_ref[0, :, 0].reshape(context, width)
    per = block_rows // rows
    contract = (((1,), (1,)), ((), ()))
    for index in range(length // block_rows):
        queries = q_ref[index * per : (index + 1) * per, 0].reshape(block_rows, width)
        pieces = [
            (lax.dot_general(queries, context_keys, contract, preferred_element_type=jnp.float32), context_values)
        ]
        if index > 0:
            keys = k_ref[: index * per, 0].reshape(index * block_rows, width)
            values = v_ref[: index * per, 0].reshape(index * block_rows, width)
            pieces.append((lax.dot_general(queries, keys, contract, preferred_element_type=jnp.float32), values))
        keys = k_ref[index * per : (index + 1) * per, 0].reshape(block_rows, width)
        values = v_ref[index * per : (index + 1) * per, 0].reshape(block_rows, width)
        scores = lax.dot_general(queries, keys, contract, preferred_element_type=jnp.float32)
        shape = (block_rows, block_rows)
        allowed = lax.broadcasted_iota(jnp.int32, shape, 1) <= lax.broadcasted_iota(jnp.int32, shape, 0)
        pieces.append((jnp.where(allowed, scores, masked_score), values))
        highest = functools.reduce(jnp.maximum, [jnp.max(s, axis=1, keepdims=True) for s, _ in pieces])
        total = jnp.zeros((block_rows, 1), jnp.float32)
        mixed = jnp.zeros((block_rows, width), jnp.float32)
        for scores, values in pieces:
            weights = jnp.exp((scores - highest) * scaling)
            total += jnp.sum(weights, axis=1, keepdims=True)
            mixed += jnp.dot(weights.astype(jnp.bfloat16), values, preferred_element_type=jnp.float32)
        result = (mixed / total).astype(jnp.bfloat16)
        out_ref[index * per : (index + 1) * per, 0] = result.reshape(per, rows, width)


def attend(queries, keys, values, context):
    sources, heads, rows, width = queries.shape
    block_rows = rows * (2 if sources % 2 == 0 and sources * rows <= 2048 else 1)
    own = pl.BlockSpec((sources, 1, rows, width), lambda h: (0, h, 0, 0))

    def shared(which):
        return pl.BlockSpec((1, context.shape[1], 1) + context.shape[3:], lambda h: (h, 0, which, 0, 0))

    length, context_rows = sources * rows, context.shape[1] * context.shape[3]
    pairs = heads * length * (context_rows + (length + block_rows) // 2)
    return pl.pallas_call(
        functools.partial(attend_kernel, block_rows),
        grid=(heads,),
        out_shape=jax.ShapeDtypeStruct(queries.shape, jnp.bfloat16),
        in_specs=[own, own, own, shared(0), shared(1)],
        out_specs=own,
        cost_estimate=pl.CostEstimate(
            flops=4 * pairs * width, bytes_accessed=heads * width * (8 * length + 4 * context_rows), transcendentals=pairs
        ),
        compiler_params=pltpu.CompilerParams(vmem_limit_bytes=48 * 1024 * 1024),
        name="attend",
    )(queries, keys, values, context, context)


def local(
    hyena_query,
    hyena_key,
    hyena_value,
    hyena_filters,
    context_tail,
    cont_queries,
    cont_keys,
    cont_values,
    context_keys,
    context_values,
    lengths,
):
    peers = lax.axis_size("seq")
    cands = lax.axis_size("cand")
    me = lax.axis_index("seq")
    rows = hyena_key.shape[1]
    heads, width = cont_queries.shape[2:]
    share = heads // peers

    def by_owner(x):
        return x.reshape(x.shape[0], peers, share, width).transpose(1, 2, 0, 3)

    def exchange(x):
        return lax.all_to_all(x, "seq", split_axis=0, concat_axis=0, tiled=True)

    if share % cands == 0:
        part = share // cands
        mine = lax.axis_index("cand")

        def picked(x):
            cut = x.reshape(x.shape[0], peers, cands, part, width)
            return lax.dynamic_index_in_dim(cut, mine, 2, keepdims=False).transpose(1, 2, 0, 3)

        pair = jnp.stack([picked(context_keys), picked(context_values)], axis=2)
        pair = exchange(pair)
        context = lax.all_gather(pair.transpose(1, 0, 2, 3, 4), "cand", axis=0, tiled=True)
    else:
        pair = exchange(jnp.stack([by_owner(context_keys), by_owner(context_values)], axis=2))
        context = pair.transpose(1, 0, 2, 3, 4)

    queries = exchange(by_owner(cont_queries[0]))
    keys = exchange(by_owner(cont_keys[0]))
    values = exchange(by_owner(cont_values[0]))

    product = (hyena_key.astype(jnp.float32) * hyena_value.astype(jnp.float32)).astype(jnp.bfloat16)
    received = lax.ppermute(product, "seq", [(i, i + 1) for i in range(peers - 1)])
    left = lengths - me * rows
    first = (me == 0).astype(jnp.int32)[None]
    hyena_out = hyena(hyena_query, hyena_key, hyena_value, received, context_tail, hyena_filters, left, first)

    attended = exchange(attend(queries, keys, values, context))
    attention = attended.transpose(2, 0, 1, 3).reshape(1, rows, heads, width)
    keep = jnp.arange(rows)[None, :, None, None] < left[:, None, None, None]
    attention_out = jnp.where(keep, attention, jnp.zeros((), jnp.bfloat16))
    return (hyena_out, attention_out)


def solution(mesh):
    placed = (
        P("cand", "seq", None),
        P("cand", "seq", None),
        P("cand", "seq", None),
        P(),
        P(),
        P("cand", "seq", None, None),
        P("cand", "seq", None, None),
        P("cand", "seq", None, None),
        P("seq", None, None),
        P("seq", None, None),
        P("cand"),
    )
    return jax.shard_map(
        local,
        mesh=mesh,
        in_specs=placed,
        out_specs=(P("cand", "seq", None), P("cand", "seq", None, None)),
        check_vma=False,
    )
```

time: 221 us -> 216 us (0.977)
  the two profiles are of different devices: /device:TPU:0 before, /device:TPU:19 now
where the time goes in v1:
time: 216 us; the launch traced here: 213 us
  waiting for transfers between devices  88.8 us (41%)
  Pallas kernels  35.3 us (16%)
  blocking collectives  31 us (14%)
  starting transfers between devices  27.1 us (13%)
  between operations  14.8 us (7%)
  local copies, waits for them, and re-layouts  12.5 us (6%)
  other arithmetic  3.63 us (2%)
    all_to_all x4, waiting for transfers between devices, exchange(): return lax.all_to_all(x, 'seq', split_axis=0, concat_axis=0, tiled=True)  49.1 us
    ppermute x1, waiting for transfers between devices, local(): lax.ppermute(product, 'seq', [(i, i + 1) for i in range(peers - 1)])  38.9 us
    all_to_all x1, blocking collectives, exchange(): return lax.all_to_all(x, 'seq', split_axis=0, concat_axis=0, tiled=True)  31 us
    all_to_all x4, starting transfers between devices, exchange(): return lax.all_to_all(x, 'seq', split_axis=0, concat_axis=0, tiled=True)  24 us
    pallas_call x1, Pallas kernels, hyena(): pl.pallas_call(hyena_kernel, grid=(channels // LANES,), out_shape=jax.Sha...  22.9 us
    pallas_call x1, Pallas kernels, attend(): pl.pallas_call(functools.partial(attend_kernel, block_rows), grid=(heads,...  12.3 us
    unnamed x24, local copies, waits for them, and re-layouts  6.79 us
  transfers between devices with their start and end apart: 6, of which 4 were waited for; matrix products, arithmetic and copies ran while one was open for 4% of the time, Pallas kernels for 11%

profile of v1, /device:TPU:19, one launch (start us, length us, event | category | flops | bytes accessed | tf_op | source)
XLA Modules:
  0.0 213.0 jit_solution(5215613668016706256)
XLA Ops:
  7.2 2.2 %constant_dynamic-slice_fusion = (bf16[96,8,1,1,128]{4,2,1,0,3:T(2,128)(2,1)S(1)}, bf16[96,8,1,1,128]{4,2,1,0,3:T(2,128)(2,1)S(1)}) fusion(bf16[96,8,4,1,128]{4,2,1,0,3:T(4,128)(2,1)} %bitcast.40, s32[]{:T(128)S(6)} %select_n.17, bf16[96,8,4,1,128]{4,2,1,0,3:T(4,128)(2,1)} %bitcast.41), kind=kLoop, calls=%fused_computation.7 | loop fusion | bytes 786436 | tf_op jit(solution)/shard_map/jit(dynamic_index_in_dim)/dynamic_slice | solution.py:159
  9.5 0.8 pad_maximum_fusion
  10.3 5.6 %all-to-all-start.3 = ((bf16[8,1,2,96,128]{4,3,2,1,0:T(8,128)(2,1)}), bf16[8,1,2,96,128]{4,3,2,1,0:T(8,128)(2,1)S(1)}, u32[]{:S(2)}, u32[]{:S(2)}) async-start(bf16[8,1,2,96,128]{4,3,2,1,0:T(8,128)(2,1)} %pad_maximum_fusion), calls=%async_computation.3 | async-start | bytes 786432 | tf_op jit(solution)/shard_map/all_to_all | solution.py:151
  15.9 1.4 copy.21
  17.3 8.2 %all-to-all-done.3 = bf16[8,1,2,96,128]{4,3,2,1,0:T(8,128)(2,1)S(1)} async-done(((bf16[8,1,2,96,128]{4,3,2,1,0:T(8,128)(2,1)}), bf16[8,1,2,96,128]{4,3,2,1,0:T(8,128)(2,1)S(1)}, u32[]{:S(2)}, u32[]{:S(2)}) %all-to-all-start.3) | async-done | bytes 393248 | tf_op jit(solution)/shard_map/all_to_all | solution.py:151
  25.5 5.6 %all-to-all-start = ((bf16[8,4,128,128]{3,2,1,0:T(8,128)(2,1)}), bf16[8,4,128,128]{3,2,1,0:T(8,128)(2,1)S(1)}, u32[]{:S(2)}, u32[]{:S(2)}) async-start(bf16[8,4,128,128]{3,2,1,0:T(8,128)(2,1)} %bitcast.5), calls=%async_computation | async-start | bytes 2097152 | tf_op jit(solution)/shard_map/all_to_all | solution.py:151
  31.1 1.4 copy.22
  32.5 20.8 %all-to-all-done.q_ref = bf16[8,4,128,128]{3,2,1,0:T(8,128)(2,1)S(1)} async-done(((bf16[8,4,128,128]{3,2,1,0:T(8,128)(2,1)}), bf16[8,4,128,128]{3,2,1,0:T(8,128)(2,1)S(1)}, u32[]{:S(2)}, u32[]{:S(2)}) %all-to-all-start) | async-done | bytes 1048608 | tf_op jit(solution)/shard_map/all_to_all | solution.py:151
  53.3 7.3 %all-to-all-start.1 = ((bf16[8,4,128,128]{3,2,1,0:T(8,128)(2,1)}), bf16[8,4,128,128]{3,2,1,0:T(8,128)(2,1)S(1)}, u32[]{:S(2)}, u32[]{:S(2)}) async-start(bf16[8,4,128,128]{3,2,1,0:T(8,128)(2,1)} %bitcast.7), calls=%async_computation.1 | async-start | bytes 2097152 | tf_op jit(solution)/shard_map/all_to_all | solution.py:151
  60.7 0.7 all-gather.3.cloned.1.call-update
  61.4 1.4 copy.23
  62.8 20.1 %all-to-all-done.1.k_ref = bf16[8,4,128,128]{3,2,1,0:T(8,128)(2,1)S(1)} async-done(((bf16[8,4,128,128]{3,2,1,0:T(8,128)(2,1)}), bf16[8,4,128,128]{3,2,1,0:T(8,128)(2,1)S(1)}, u32[]{:S(2)}, u32[]{:S(2)}) %all-to-all-start.1) | async-done | bytes 1048608 | tf_op jit(solution)/shard_map/all_to_all | solution.py:151
  82.9 31.0 %all_to_all.25.v_ref = bf16[8,4,128,128]{3,2,1,0:T(8,128)(2,1)S(1)} all-to-all(bf16[8,4,128,128]{3,2,1,0:T(8,128)(2,1)} %bitcast.37), channel_id=1, replica_groups=mesh['cand'=4,'seq'=8] {'seq'}, dimensions={0} | all-to-all | bytes 2097152 | tf_op jit(solution)/shard_map/all_to_all | solution.py:151
  113.9 1.4 copy-done
  115.4 12.3 %attend.1 = bf16[8,4,128,128]{3,2,1,0:T(8,128)(2,1)} custom-call(bf16[8,4,128,128]{3,2,1,0:T(8,128)(2,1)S(1)} %all-to-all-done.q_ref, bf16[8,4,128,128]{3,2,1,0:T(8,128)(2,1)S(1)} %all-to-all-done.1.k_ref, bf16[8,4,128,128]{3,2,1,0:T(8,128)(2,1)S(1)} %all_to_all.25.v_ref, bf16[4,8,2,96,128]{4,3,2,1,0:T(8,128)(2,1)S(1)} %bitcast.34, ...), custom_call_target="tpu_custom_call" | custom-call | flops 2952790016 | bytes 5767168 | tf_op jit(solution)/shard_map/attend/pallas_call | solution.py:113
  127.7 5.4 %all-to-all-start.4 = ((bf16[8,4,128,128]{3,2,1,0:T(8,128)(2,1)}), bf16[8,4,128,128]{3,2,1,0:T(8,128)(2,1)S(1)}, u32[]{:S(2)}, u32[]{:S(2)}) async-start(bf16[8,4,128,128]{3,2,1,0:T(8,128)(2,1)} %attend.1), calls=%async_computation.4 | async-start | bytes 2097152 | tf_op jit(solution)/shard_map/all_to_all | solution.py:151
  133.1 1.2 multiply_convert_fusion
  134.4 3.1 %collective-permute-start = (bf16[1,128,4096]{2,1,0:T(8,128)(2,1)}, bf16[1,128,4096]{2,1,0:T(8,128)(2,1)S(1)}, u32[]{:S(2)}, u32[]{:S(2)}) collective-permute-start(bf16[1,128,4096]{2,1,0:T(8,128)(2,1)} %multiply_convert_fusion), channel_id=1, source_target_pairs={{0,1},{1,2},{2,3},{3,4},{4,5},{5,6},{6,7},{8,9},{9,10},{10,11},{11... | collective-permute-start | bytes 3145736 | tf_op jit(solution)/shard_map/ppermute | solution.py:173
  138.4 2.5 %pad.8.tail_ref = bf16[128,4096]{1,0:T(8,128)(2,1)} pad(bf16[127,4096]{1,0:T(8,128)(2,1)} %param.15, bf16[]{:T(256)} %constant.20.clone.1), padding=1_0x0_0 | pad | bytes 2088962 | tf_op jit(solution)/shard_map/jit(_pad)/pad | solution.py:42
  140.9 0.8 pad_bitcast_fusion.wave_ref
  141.7 38.9 %collective-permute-done.before_ref = bf16[1,128,4096]{2,1,0:T(8,128)(2,1)S(1)} collective-permute-done((bf16[1,128,4096]{2,1,0:T(8,128)(2,1)}, bf16[1,128,4096]{2,1,0:T(8,128)(2,1)S(1)}, u32[]{:S(2)}, u32[]{:S(2)}) %collective-permute-start) | collective-permute-done | bytes 1048608 | tf_op jit(solution)/shard_map/ppermute | solution.py:173
  180.6 1.0 copy-done.8
  181.6 22.9 %hyena.1 = bf16[1,128,4096]{2,1,0:T(8,128)(2,1)} custom-call(s32[1]{0:T(128)} %sub.7.length_ref, s32[1]{0:T(128)} %bitcast.1.first_ref, bf16[1,128,4096]{2,1,0:T(8,128)(2,1)} %query_ref.1, bf16[1,128,4096]{2,1,0:T(8,128)(2,1)} %key_ref.1, bf16[1,128,4096]{2,1,0:T(8,128)(2,1)} %value_ref.1, bf16[1,128,4096]{2,1,0:T(8,128)(2,1)} %copy-done.8, ...), custom_call_target="tpu_custom_call" | custom-call | flops 4294967296 | bytes 6291456 | tf_op jit(solution)/shard_map/hyena/pallas_call | solution.py:46
  204.5 1.6 copy_select_fusion
  (24 shorter events, 0.5 us)
Async XLA Ops:
  9.4 6.6 %copy-start.4 = (bf16[1,128,32,128]{3,2,1,0:T(8,128)(2,1)S(1)}, bf16[1,128,32,128]{3,2,1,0:T(8,128)(2,1)}, u32[]{:S(2)}) copy-start(bf16[1,128,32,128]{3,2,1,0:T(8,128)(2,1)} %param.16) | copy-start | bytes 3145732
  10.3 15.2 %all-to-all-start.3 = ((bf16[8,1,2,96,128]{4,3,2,1,0:T(8,128)(2,1)}), bf16[8,1,2,96,128]{4,3,2,1,0:T(8,128)(2,1)S(1)}, u32[]{:S(2)}, u32[]{:S(2)}) async-start(bf16[8,1,2,96,128]{4,3,2,1,0:T(8,128)(2,1)} %pad_maximum_fusion), calls=%async_computation.3 | async-start | bytes 786432 | tf_op jit(solution)/shard_map/all_to_all | solution.py:151
  17.3 13.8 %copy-start.5 = (bf16[1,128,32,128]{3,2,1,0:T(8,128)(2,1)S(1)}, bf16[1,128,32,128]{3,2,1,0:T(8,128)(2,1)}, u32[]{:S(2)}) copy-start(bf16[1,128,32,128]{3,2,1,0:T(8,128)(2,1)} %param.17) | copy-start | bytes 3145732
  25.5 7.0 %copy-start.1 = (bf16[8,1,2,96,128]{4,3,2,1,0:T(8,128)(2,1)}, bf16[8,1,2,96,128]{4,3,2,1,0:T(8,128)(2,1)S(1)}, u32[]{:S(2)}) copy-start(bf16[8,1,2,96,128]{4,3,2,1,0:T(8,128)(2,1)S(1)} %all-to-all-done.3) | copy-start | bytes 1179652
  25.5 27.8 %all-to-all-start = ((bf16[8,4,128,128]{3,2,1,0:T(8,128)(2,1)}), bf16[8,4,128,128]{3,2,1,0:T(8,128)(2,1)S(1)}, u32[]{:S(2)}, u32[]{:S(2)}) async-start(bf16[8,4,128,128]{3,2,1,0:T(8,128)(2,1)} %bitcast.5), calls=%async_computation | async-start | bytes 2097152 | tf_op jit(solution)/shard_map/all_to_all | solution.py:151
  32.5 28.9 %copy-start.6 = (bf16[1,128,32,128]{3,2,1,0:T(8,128)(2,1)S(1)}, bf16[1,128,32,128]{3,2,1,0:T(8,128)(2,1)}, u32[]{:S(2)}) copy-start(bf16[1,128,32,128]{3,2,1,0:T(8,128)(2,1)} %param.18) | copy-start | bytes 3145732
  53.3 29.6 %all-to-all-start.1 = ((bf16[8,4,128,128]{3,2,1,0:T(8,128)(2,1)}), bf16[8,4,128,128]{3,2,1,0:T(8,128)(2,1)S(1)}, u32[]{:S(2)}, u32[]{:S(2)}) async-start(bf16[8,4,128,128]{3,2,1,0:T(8,128)(2,1)} %bitcast.7), calls=%async_computation.1 | async-start | bytes 2097152 | tf_op jit(solution)/shard_map/all_to_all | solution.py:151
  60.7 53.3 %all-gather.3.cloned.1.call-start = ((), (), s32[]{:S(2)}) async-start(), calls=%async_computation.5 | async-start | bytes 1966080 | tf_op jit(solution)/shard_map/all_gather | solution.py:163
  113.9 1.4 copy-start
  127.7 5.4 %copy-start.2 = (bf16[1,128,4096]{2,1,0:T(8,128)(2,1)S(1)}, bf16[1,128,4096]{2,1,0:T(8,128)(2,1)}, u32[]{:S(2)}) copy-start(bf16[1,128,4096]{2,1,0:T(8,128)(2,1)} %key_ref.1) | copy-start | bytes 3145732
  127.7 5.4 %copy-start.3 = (bf16[1,128,4096]{2,1,0:T(8,128)(2,1)S(1)}, bf16[1,128,4096]{2,1,0:T(8,128)(2,1)}, u32[]{:S(2)}) copy-start(bf16[1,128,4096]{2,1,0:T(8,128)(2,1)} %value_ref.1) | copy-start | bytes 3145732
  127.7 76.9 %all-to-all-start.4 = ((bf16[8,4,128,128]{3,2,1,0:T(8,128)(2,1)}), bf16[8,4,128,128]{3,2,1,0:T(8,128)(2,1)S(1)}, u32[]{:S(2)}, u32[]{:S(2)}) async-start(bf16[8,4,128,128]{3,2,1,0:T(8,128)(2,1)} %attend.1), calls=%async_computation.4 | async-start | bytes 2097152 | tf_op jit(solution)/shard_map/all_to_all | solution.py:151
  133.1 5.0 %copy-start.7 = (f32[128,256]{1,0:T(8,128)S(1)}, f32[128,256]{1,0:T(8,128)}, u32[]{:S(2)}) copy-start(f32[128,256]{1,0:T(8,128)} %param.14) | copy-start | bytes 393220
  134.4 46.3 %collective-permute-start = (bf16[1,128,4096]{2,1,0:T(8,128)(2,1)}, bf16[1,128,4096]{2,1,0:T(8,128)(2,1)S(1)}, u32[]{:S(2)}, u32[]{:S(2)}) collective-permute-start(bf16[1,128,4096]{2,1,0:T(8,128)(2,1)} %multiply_convert_fusion), channel_id=1, source_target_pairs={{0,1},{1,2},{2,3},{3,4},{4,5},{5,6},{6,7},{8,9},{9,10},{10,11},{11... | collective-permute-start | bytes 3145736 | tf_op jit(solution)/shard_map/ppermute | solution.py:173
  180.6 1.0 copy-start.8
Sparse Core Ops, SparseCore 0:
  63.0 20.3 all-gather.2

commit v2 on v1

v2 whole, which is shorter than its diff:
```python
import functools
import math

import jax
import jax.numpy as jnp
from jax import lax
from jax.experimental import pallas as pl
from jax.experimental.pallas import tpu as pltpu
from jax.sharding import PartitionSpec as P

CH_GROUP = 16
LANES = 128
VMEM = 56 * 1024 * 1024
WAVES = 2

masked_score = -1e30

bf16 = jnp.bfloat16
f32 = jnp.float32


def hyena_kernel(place_ref, query_ref, key_ref, value_ref, before_ref, tail_ref, wave_ref, out_ref):
    rows, lanes = key_ref.shape[1], key_ref.shape[2]
    product = (key_ref[0].astype(f32) * value_ref[0].astype(f32)).astype(bf16)
    first = jnp.broadcast_to(place_ref[0], (rows, lanes)) == 0
    earlier = jnp.where(first, tail_ref[...].astype(f32), before_ref[...].astype(f32))
    extended = jnp.concatenate([earlier.astype(bf16), product], axis=0)
    channel = lax.broadcasted_iota(jnp.int32, (rows, lanes), 1) // CH_GROUP
    convolved = jnp.zeros((rows, lanes), f32)
    for group in range(lanes // CH_GROUP):
        wave = jnp.broadcast_to(wave_ref[group : group + 1, :], (rows, 2 * rows))
        taps = pltpu.roll(wave, 0, 1, stride=1, stride_axis=0)
        high = taps.astype(bf16)
        low = (taps - high.astype(f32)).astype(bf16)
        term = jnp.dot(high, extended, preferred_element_type=f32) + jnp.dot(
            low, extended, preferred_element_type=f32
        )
        convolved = jnp.where(channel == group, term, convolved)
    places = lax.broadcasted_iota(jnp.int32, (rows, lanes), 0)
    gated = query_ref[0].astype(f32) * convolved
    out_ref[0] = jnp.where(places < place_ref[1], gated, 0.0).astype(bf16)


def hyena(query, key, value, received, tail, filters, place):
    _, rows, channels = key.shape
    wave = jnp.pad(filters[::-1], ((1, 2 * rows - filters.shape[0] - 1), (0, 0))).T
    tail = jnp.pad(tail, ((1, 0), (0, 0)))
    groups = LANES // CH_GROUP
    block = pl.BlockSpec((1, rows, LANES), lambda i: (0, 0, i))
    flat = pl.BlockSpec((rows, LANES), lambda i: (0, i))
    return pl.pallas_call(
        hyena_kernel,
        grid=(channels // LANES,),
        out_shape=jax.ShapeDtypeStruct(query.shape, bf16),
        in_specs=[
            pl.BlockSpec(memory_space=pltpu.SMEM),
            block,
            block,
            block,
            flat,
            flat,
            pl.BlockSpec((groups, 2 * rows), lambda i: (i, 0)),
        ],
        out_specs=block,
        cost_estimate=pl.CostEstimate(
            flops=2 * 2 * rows * 2 * rows * channels * groups, bytes_accessed=12 * rows * channels, transcendentals=0
        ),
        name="hyena",
    )(place, query, key, value, received, tail, wave)


def attend_kernel(block_rows, q_ref, k_ref, v_ref, ck_ref, cv_ref, out_ref):
    sources, _, rows, width = k_ref.shape
    index = pl.program_id(1)
    scaling = 1.0 / math.sqrt(width)
    context = ck_ref.shape[1] * ck_ref.shape[3]
    contract = (((1,), (1,)), ((), ()))
    queries = q_ref[...].reshape(block_rows, width)
    per = block_rows // rows

    def fold(carried, scores, values):
        run_max, run_total, mixed = carried
        highest = jnp.maximum(run_max, jnp.max(scores, axis=1, keepdims=True))
        weights = jnp.exp((scores - highest) * scaling)
        shrink = jnp.exp((run_max - highest) * scaling)
        total = run_total * shrink + jnp.sum(weights, axis=1, keepdims=True)
        mixed = mixed * shrink + jnp.dot(weights.astype(bf16), values, preferred_element_type=f32)
        return highest, total, mixed

    def own(block):
        keys = k_ref[pl.ds(block * per, per), 0].reshape(block_rows, width)
        values = v_ref[pl.ds(block * per, per), 0].reshape(block_rows, width)
        return lax.dot_general(queries, keys, contract, preferred_element_type=f32), values

    scores, values = own(index)
    shape = (block_rows, block_rows)
    allowed = lax.broadcasted_iota(jnp.int32, shape, 1) <= lax.broadcasted_iota(jnp.int32, shape, 0)
    scores = jnp.where(allowed, scores, masked_score)
    start = (
        jnp.full((block_rows, 1), masked_score, f32),
        jnp.zeros((block_rows, 1), f32),
        jnp.zeros((block_rows, width), f32),
    )
    carried = fold(start, scores, values)
    carried = lax.fori_loop(0, index, lambda i, c: fold(c, *own(i)), carried)
    context_keys = ck_ref[0, :, 0].reshape(context, width)
    context_values = cv_ref[0, :, 0].reshape(context, width)
    scores = lax.dot_general(queries, context_keys, contract, preferred_element_type=f32)
    _, total, mixed = fold(carried, scores, context_values)
    out_ref[...] = (mixed / total).astype(bf16).reshape(out_ref.shape)


def attend(queries, keys, values, context):
    sources, heads, rows, width = queries.shape
    per = 2 if sources % 2 == 0 else 1
    whole = pl.BlockSpec((sources, 1, rows, width), lambda h, i: (0, h, 0, 0))
    part = pl.BlockSpec((per, 1, rows, width), lambda h, i: (i, h, 0, 0))

    def shared(which):
        return pl.BlockSpec((1, context.shape[1], 1) + context.shape[3:], lambda h, i: (h, 0, which, 0, 0))

    length, context_rows = sources * rows, context.shape[1] * context.shape[3]
    pairs = heads * length * (context_rows + (length + rows * per) // 2)
    return pl.pallas_call(
        functools.partial(attend_kernel, rows * per),
        grid=(heads, sources // per),
        out_shape=jax.ShapeDtypeStruct(queries.shape, bf16),
        in_specs=[part, whole, whole, shared(0), shared(1)],
        out_specs=part,
        cost_estimate=pl.CostEstimate(
            flops=4 * pairs * width, bytes_accessed=heads * width * (8 * length + 4 * context_rows), transcendentals=pairs
        ),
        compiler_params=pltpu.CompilerParams(vmem_limit_bytes=VMEM),
        name="attend",
    )(queries, keys, values, context, context)


def attention_by_heads(cont_queries, cont_keys, cont_values, context_keys, context_values, left):
    peers = lax.axis_size("seq")
    rows, heads, width = cont_queries.shape
    share = heads // peers

    def by_owner(x):
        return x.reshape(x.shape[0], peers, share, width).transpose(1, 2, 0, 3)

    def exchange(x):
        return lax.all_to_all(x, "seq", split_axis=0, concat_axis=0, tiled=True)

    pair = exchange(jnp.stack([by_owner(context_keys), by_owner(context_values)], axis=2))
    context = pair.transpose(1, 0, 2, 3, 4)
    queries = exchange(by_owner(cont_queries))
    keys = exchange(by_owner(cont_keys))
    values = exchange(by_owner(cont_values))
    attended = exchange(attend(queries, keys, values, context))
    attention = attended.transpose(2, 0, 1, 3).reshape(rows, heads, width)
    keep = jnp.arange(rows)[:, None, None] < left
    return jnp.where(keep, attention, jnp.zeros((), bf16))


SIDE = 4


def pack_kernel(*refs):
    count = 3 * SIDE
    sources, outs = refs[1 : 1 + count], refs[1 + count :]
    group = sources[0].shape[1]
    each = group // WAVES
    for partner in range(SIDE):
        for which in range(3):
            x = jnp.transpose(sources[3 * partner + which][...].astype(f32), (1, 0, 2)).astype(bf16)
            outs[partner][which * group : (which + 1) * group] = x
            if which == 0:
                for wave in range(WAVES):
                    outs[SIDE + wave * SIDE + partner][...] = x[wave * each : (wave + 1) * each]


def pack(queries, keys, values, side):
    rows, heads, width = queries.shape
    group = heads // SIDE
    step = 32

    def taken(partner):
        return pl.BlockSpec((step, group, width), lambda i, s: (i, s[0] ^ partner, 0))

    sizes = [3 * group] * SIDE + [group // WAVES] * (SIDE * WAVES)
    return pl.pallas_call(
        pack_kernel,
        grid_spec=pltpu.PrefetchScalarGridSpec(
            num_scalar_prefetch=1,
            grid=(rows // step,),
            in_specs=[taken(partner) for partner in range(SIDE) for _ in range(3)],
            out_specs=[pl.BlockSpec((n, step, width), lambda i, s: (0, i, 0)) for n in sizes],
        ),
        out_shape=[jax.ShapeDtypeStruct((n, rows, width), bf16) for n in sizes],
        compiler_params=pltpu.CompilerParams(vmem_limit_bytes=VMEM),
        name="pack",
    )(side, *([queries, keys, values] * SIDE))


def pack_context_kernel(*refs):
    sources, outs = refs[1 : 1 + 2 * SIDE], refs[1 + 2 * SIDE :]
    part = outs[0].shape[0]
    start = refs[0][1] * part
    for partner in range(SIDE):
        for which in range(2):
            x = sources[2 * partner + which]
            for head in range(part):
                outs[partner][head, which] = x[:, pl.ds(start + head, 1), :][:, 0, :].astype(bf16)


def pack_context(keys, values, side, part):
    rows, heads, width = keys.shape
    group = heads // SIDE

    def taken(partner):
        return pl.BlockSpec((rows, group, width), lambda i, s: (0, s[0] ^ partner, 0))

    shape = (part, 2, rows, width)
    return pl.pallas_call(
        pack_context_kernel,
        grid_spec=pltpu.PrefetchScalarGridSpec(
            num_scalar_prefetch=1,
            grid=(1,),
            in_specs=[taken(partner) for partner in range(SIDE) for _ in range(2)],
            out_specs=[pl.BlockSpec(shape, lambda i, s: (0, 0, 0, 0))] * SIDE,
        ),
        out_shape=[jax.ShapeDtypeStruct(shape, bf16)] * SIDE,
        compiler_params=pltpu.CompilerParams(vmem_limit_bytes=VMEM),
        name="pack_context",
    )(side, *([keys.astype(f32), values.astype(f32)] * SIDE))


def softmax_columns(pieces, scaling):
    highest = functools.reduce(jnp.maximum, [jnp.max(s, axis=0, keepdims=True) for s, _ in pieces])
    total = mixed = 0.0
    for scores, values in pieces:
        weights = jnp.exp((scores - highest) * scaling)
        total += jnp.sum(weights, axis=0, keepdims=True)
        mixed += lax.dot_general(values, weights.astype(bf16), (((0,), (0,)), ((), ())), preferred_element_type=f32)
    return mixed / total, highest * scaling + jnp.log(total)


def thirds(x):
    first = x.astype(bf16).astype(f32)
    second = (x - first).astype(bf16).astype(f32)
    return first, second, x - first - second


def products(keys, queries):
    return lax.dot_general(keys, queries, (((1,), (1,)), ((), ())), preferred_element_type=f32)


def visit_kernel(wave, side_ref, *refs):
    q_refs, kv_refs, outs = refs[:SIDE], refs[SIDE : 2 * SIDE], refs[2 * SIDE :]
    each, rows, width = q_refs[0].shape
    group = kv_refs[0].shape[0] // 3
    scaling = 1.0 / math.sqrt(width)

    @pl.when(side_ref[2] == 0)
    def _():
        stats = [[], [], []]
        for head in range(each):
            place = wave * each + head
            queries = jnp.concatenate([q[head] for q in q_refs], axis=0)
            keys = jnp.concatenate([r[group + place] for r in kv_refs], axis=0)
            values = jnp.concatenate([r[2 * group + place] for r in kv_refs], axis=0)
            mixed, level = softmax_columns([(products(keys, queries), values)], scaling)
            result = mixed.T.astype(bf16)
            for partner in range(SIDE):
                outs[partner][head * rows : (head + 1) * rows] = result[partner * rows : (partner + 1) * rows]
            for third, value in enumerate(thirds(level)):
                stats[third].append(value)
        pad = outs[0].shape[0] - each * rows - 3 * each
        lines = stats[0] + stats[1] + stats[2]
        if pad > 0:
            lines.append(jnp.zeros((pad, SIDE * rows), f32))
        block = jnp.concatenate(lines, axis=0).astype(bf16)
        for partner in range(SIDE):
            outs[partner][each * rows :] = block[:, partner * rows : (partner + 1) * rows]


def stat_rows(heads):
    return -(-3 * heads // 16) * 16


def visit(wave, queries, packs, side):
    each, rows, width = queries[0].shape
    out = (each * rows + stat_rows(each), width)
    pairs = each * (SIDE * rows) ** 2
    whole = pl.BlockSpec(memory_space=pltpu.VMEM)
    return pl.pallas_call(
        functools.partial(visit_kernel, wave),
        in_specs=[pl.BlockSpec(memory_space=pltpu.SMEM)] + [whole] * (2 * SIDE),
        out_specs=[whole] * SIDE,
        out_shape=[jax.ShapeDtypeStruct(out, bf16)] * SIDE,
        cost_estimate=pl.CostEstimate(flops=4 * pairs * width, bytes_accessed=4 << 20, transcendentals=pairs),
        compiler_params=pltpu.CompilerParams(vmem_limit_bytes=VMEM),
        name="visit",
    )(side, *queries, *packs)


def own_kernel(parts, side_ref, *refs):
    qkv_refs, refs = refs[: 3 * SIDE], refs[3 * SIDE :]
    context_refs, refs = refs[:parts], refs[parts:]
    outs, (qs, ks, vs, os, ck, cv, level_ref, stat_ref) = refs[:SIDE], refs[SIDE:]
    _, rows, width = qkv_refs[0].shape
    side = side_ref[0]
    step = pl.program_id(0)
    each = context_refs[0].shape[1]
    group = pl.num_programs(0)
    head = ((step // each) ^ side_ref[1]) * each + step % each
    scaling = 1.0 / math.sqrt(width)
    length = SIDE * rows

    for partner in range(SIDE):
        place = pl.ds(pl.multiple_of((side ^ partner) * rows, rows), rows)
        qs[place] = qkv_refs[3 * partner][0]
        ks[place] = qkv_refs[3 * partner + 1][0]
        vs[place] = qkv_refs[3 * partner + 2][0]
    for part in range(parts):

        @pl.when(step // each == part)
        def _():
            ck[...] = context_refs[part][:, pl.ds(step % each, 1), 0].reshape(ck.shape)
            cv[...] = context_refs[part][:, pl.ds(step % each, 1), 1].reshape(cv.shape)

    block = 2 * rows
    for index in range(length // block):
        here = slice(index * block, (index + 1) * block)
        queries = qs[here]
        pieces = [(products(ck[...], queries), cv[...])]
        if index > 0:
            pieces.append((products(ks[: index * block], queries), vs[: index * block]))
        scores = products(ks[here], queries)
        allowed = lax.broadcasted_iota(jnp.int32, scores.shape, 0) <= lax.broadcasted_iota(jnp.int32, scores.shape, 1)
        pieces.append((jnp.where(allowed, scores, masked_score), vs[here]))
        mixed, level = softmax_columns(pieces, scaling)
        os[here] = mixed.T.astype(bf16)
        for part in range(block // rows):
            level_ref[index * (block // rows) + part, 0:1] = level[:, part * rows : (part + 1) * rows]
    at = pl.ds(pl.multiple_of(head * rows, rows), rows)
    for partner in range(SIDE):
        place = side ^ partner
        outs[partner][at] = os[pl.ds(pl.multiple_of(place * rows, rows), rows)]
        for third, value in enumerate(thirds(level_ref[place, 0:1])):
            stat_ref[partner, pl.ds(third * group + head, 1)] = value

    @pl.when(step == group - 1)
    def _():
        for partner in range(SIDE):
            outs[partner][group * rows :] = stat_ref[partner].astype(bf16)


def own(packs, contexts, side):
    triple, rows, width = packs[0].shape
    group = triple // 3
    parts = len(contexts)
    each = contexts[0].shape[1]
    sources, context_rows = contexts[0].shape[0], contexts[0].shape[3]
    stats = stat_rows(group)

    def taken(which):
        return pl.BlockSpec(
            (1, rows, width), lambda i, s: (which * group + ((i // each) ^ s[1]) * each + i % each, 0, 0)
        )

    def whole(shape):
        return pl.BlockSpec(shape, lambda i, s: (0,) * len(shape))

    out = (group * rows + stats, width)
    pairs = group * SIDE * rows * (sources * context_rows + SIDE * rows * 3 // 4)
    operands = [p for p in packs for _ in range(3)]
    return pl.pallas_call(
        functools.partial(own_kernel, parts),
        grid_spec=pltpu.PrefetchScalarGridSpec(
            num_scalar_prefetch=1,
            grid=(group,),
            in_specs=[taken(which) for _ in packs for which in range(3)] + [whole(c.shape) for c in contexts],
            out_specs=[whole(out)] * SIDE,
            scratch_shapes=[pltpu.VMEM((SIDE * rows, width), bf16)] * 4
            + [pltpu.VMEM((sources * context_rows, width), bf16)] * 2
            + [pltpu.VMEM((SIDE, 8, rows), f32), pltpu.VMEM((SIDE, stats, rows), f32)],
        ),
        out_shape=[jax.ShapeDtypeStruct(out, bf16)] * SIDE,
        cost_estimate=pl.CostEstimate(flops=4 * pairs * width, bytes_accessed=10 << 20, transcendentals=pairs),
        compiler_params=pltpu.CompilerParams(vmem_limit_bytes=VMEM),
        name="own",
    )(side, *operands, *contexts)


def merge_kernel(side_ref, *refs):
    mine, visits, out = refs[:SIDE], refs[SIDE : SIDE + SIDE * WAVES], refs[-1]
    step, group, width = out.shape
    rows = mine[0].shape[1]
    each = group // WAVES
    second = jnp.full((rows, group), side_ref[2], jnp.int32) == 1
    place = lax.broadcasted_iota(jnp.int32, (step, group, width), 0)

    def levels(ref, heads):
        lines = ref[heads * rows : heads * rows + stat_rows(heads)].astype(f32)
        return lines[:heads] + lines[heads : 2 * heads] + lines[2 * heads : 3 * heads]

    for partner in range(SIDE):

        @pl.when(pl.program_id(0) == partner)
        def _():
            here = levels(mine[partner], group)
            there = jnp.concatenate([levels(visits[w * SIDE + partner], each) for w in range(WAVES)], axis=0)
            gap = (there - here).T
            first_share = jnp.where(second, 1.0 / (1.0 + jnp.exp(gap)), 1.0)
            other_share = jnp.where(second, 1.0 / (1.0 + jnp.exp(-gap)), 0.0)
            heads = []
            for head in range(group):
                a = mine[partner][head * rows : (head + 1) * rows].astype(f32)
                local = head % each
                b = visits[head // each * SIDE + partner][local * rows : (local + 1) * rows].astype(f32)
                heads.append(a * first_share[:, head : head + 1] + b * other_share[:, head : head + 1])
            result = jnp.transpose(jnp.stack(heads), (1, 0, 2))
            out[...] = jnp.where(place < side_ref[3], result, 0.0).astype(bf16)


def merge(mine, visits, side, heads):
    rows = mine[0].shape[1]
    width = mine[0].shape[1]
    group = heads // SIDE

    def whole(x):
        return pl.BlockSpec(x.shape, lambda i, s: (0, 0))

    return pl.pallas_call(
        merge_kernel,
        grid_spec=pltpu.PrefetchScalarGridSpec(
            num_scalar_prefetch=1,
            grid=(SIDE,),
            in_specs=[whole(x) for x in (*mine, *visits)],
            out_specs=pl.BlockSpec((rows, group, width), lambda i, s: (0, s[0] ^ i, 0)),
        ),
        out_shape=jax.ShapeDtypeStruct((rows, heads, width), bf16),
        compiler_params=pltpu.CompilerParams(vmem_limit_bytes=VMEM),
        name="merge",
    )(side, *mine, *visits)


def attention_by_halves(cont_queries, cont_keys, cont_values, context_keys, context_values, left):
    heads = cont_queries.shape[1]
    cands = lax.axis_size("cand")
    me, mine = lax.axis_index("seq"), lax.axis_index("cand")
    peers = 2 * SIDE
    side = jnp.stack([me % SIDE, mine, me // SIDE, left]).astype(jnp.int32)

    def within(x, k):
        return lax.ppermute(x, "seq", [(i, i ^ k) for i in range(peers)])

    def down(x, k):
        return lax.ppermute(x, "seq", [(i, i ^ (SIDE + k)) for i in range(SIDE, peers)])

    def up(x, k):
        return lax.ppermute(x, "seq", [(i, i ^ (SIDE + k)) for i in range(SIDE)])

    def swap(x, k):
        return lax.ppermute(x, "cand", [(i, i ^ k) for i in range(cands)])

    packed = pack(cont_queries, cont_keys, cont_values, side)
    own_packs, crossing = packed[:SIDE], packed[SIDE:]
    visitors = [[down(crossing[w * SIDE + k], k) for k in range(SIDE)] for w in range(WAVES)]
    packs = [own_packs[0]] + [within(own_packs[k], k) for k in range(1, SIDE)]

    part = heads // SIDE // cands
    sent = pack_context(context_keys, context_values, side, part)
    context = jnp.stack([within(sent[k % SIDE], k) if k else sent[0] for k in range(peers)])
    across = swap(context, 2)
    contexts = [context, swap(context, 1), across, swap(across, 1)]

    visits = []
    for w in range(WAVES):
        parts = visit(w, visitors[w], packs, side)
        visits += [up(parts[k], k) for k in range(SIDE)]
    results = own(packs, contexts, side)
    results = [results[0]] + [within(results[k], k) for k in range(1, SIDE)]
    return merge(results, visits, side, heads)


def local(
    hyena_query,
    hyena_key,
    hyena_value,
    hyena_filters,
    context_tail,
    cont_queries,
    cont_keys,
    cont_values,
    context_keys,
    context_values,
    lengths,
):
    peers = lax.axis_size("seq")
    me = lax.axis_index("seq")
    rows = hyena_key.shape[1]
    heads = cont_queries.shape[2]
    left = (lengths[0] - me * rows).astype(jnp.int32)

    product = (hyena_key[0].astype(f32) * hyena_value[0].astype(f32)).astype(bf16)
    received = lax.ppermute(product, "seq", [(i, i + 1) for i in range(peers - 1)])
    place = jnp.stack([me.astype(jnp.int32), left])

    halves = peers == 2 * SIDE and lax.axis_size("cand") == 4 and heads % 32 == 0 and rows == LANES
    attention = attention_by_halves if halves else attention_by_heads
    attention_out = attention(
        cont_queries[0], cont_keys[0], cont_values[0], context_keys, context_values, left
    )[None]
    hyena_out = hyena(hyena_query, hyena_key, hyena_value, received, context_tail, hyena_filters, place)
    return (hyena_out, attention_out)


def solution(mesh):
    placed = (
        P("cand", "seq", None),
        P("cand", "seq", None),
        P("cand", "seq", None),
        P(),
        P(),
        P("cand", "seq", None, None),
        P("cand", "seq", None, None),
        P("cand", "seq", None, None),
        P("seq", None, None),
        P("seq", None, None),
        P("cand"),
    )
    return jax.shard_map(
        local,
        mesh=mesh,
        in_specs=placed,
        out_specs=(P("cand", "seq", None), P("cand", "seq", None, None)),
        check_vma=False,
    )
```

time: 216 us -> 210 us (0.972)
  the two profiles are of different devices: /device:TPU:19 before, /device:TPU:0 now
where the time goes in v2:
time: 210 us; the launch traced here: 206 us
  starting transfers between devices  75.8 us (36%)
  Pallas kernels  68.1 us (32%)
  waiting for transfers between devices  43 us (20%)
  local copies, waits for them, and re-layouts  11 us (5%)
  other arithmetic  6.4 us (3%)
    ppermute x8, starting transfers between devices, up(): return lax.ppermute(x, 'seq', [(i, i ^ SIDE + k) for i in range(SIDE)])  39.5 us
    pallas_call x1, Pallas kernels, hyena(): pl.pallas_call(hyena_kernel, grid=(channels // LANES,), out_shape=jax.Sha...  23 us
    ppermute x8, waiting for transfers between devices, down(): lax.ppermute(x, 'seq', [(i, i ^ SIDE + k) for i in range(SIDE, peers)])  21.5 us
    ppermute x13, starting transfers between devices, within(): return lax.ppermute(x, 'seq', [(i, i ^ k) for i in range(peers)])  20.4 us
    pallas_call x1, Pallas kernels, own(): pl.pallas_call(functools.partial(own_kernel, parts), grid_spec=pltpu.Pref...  18.9 us
    ppermute x13, waiting for transfers between devices, within(): return lax.ppermute(x, 'seq', [(i, i ^ k) for i in range(peers)])  14.1 us
    pallas_call x2, Pallas kernels, visit(): pl.pallas_call(functools.partial(visit_kernel, wave), in_specs=[pl.BlockS...  10.8 us
    ppermute x8, starting transfers between devices, down(): lax.ppermute(x, 'seq', [(i, i ^ SIDE + k) for i in range(SIDE, peers)])  10.4 us
  transfers between devices with their start and end apart: 33, of which 9 were waited for; matrix products, arithmetic and copies ran while one was open for 6% of the time, Pallas kernels for 29%

profile of v2, /device:TPU:0, one launch (start us, length us, event | category | flops | bytes accessed | tf_op | source)
XLA Modules:
  0.0 206.1 jit_solution(4628242488729054806)
XLA Ops:
  1.4 2.5 %convert_element_type.28.refs_1_.refs_3_.refs_5_.refs_7_ = f32[96,32,128]{2,1,0:T(8,128)} convert(bf16[96,32,128]{2,1,0:T(8,128)(2,1)} %param.19) | non-fusion elementwise | flops 393216 | bytes 2359296 | tf_op jit(solution)/shard_map/convert_element_type | solution.py:230
  5.9 4.0 %pack_context.1 = (bf16[2,2,96,128]{3,2,1,0:T(8,128)(2,1)}, bf16[2,2,96,128]{3,2,1,0:T(8,128)(2,1)}, bf16[2,2,96,128]{3,2,1,0:T(8,128)(2,1)}, bf16[2,2,96,128]{3,2,1,0:T(8,128)(2,1)}) custom-call(s32[4]{0:T(128)} %pad_add_fusion.1.refs_0_.side_ref, f32[96,32,128]{2,1,0:T(8,128)} %convert_element_type.28.refs_1_.refs_3_.refs_5_.refs_7_, ...), custom_call_target="tpu_custom_call" | custom-call | tf_op jit(solution)/shard_map/pack_context/pallas_call | solution.py:219
  9.9 3.0 %collective-permute-start.4 = (bf16[2,2,96,128]{3,2,1,0:T(8,128)(2,1)}, bf16[2,2,96,128]{3,2,1,0:T(8,128)(2,1)S(1)}, u32[]{:S(2)}, u32[]{:S(2)}) collective-permute-start(bf16[2,2,96,128]{3,2,1,0:T(8,128)(2,1)} %get-tuple-element.35), channel_id=1, source_target_pairs={{0,1},{1,0},{2,3},{3,2},{4,5},{5,4},{6,7},{7,6},{8,9},{9,8},{10,11... | collective-permute-start | bytes 294920 | tf_op jit(solution)/shard_map/ppermute | solution.py:452
  12.9 2.5 %collective-permute-start.8 = (bf16[2,2,96,128]{3,2,1,0:T(8,128)(2,1)}, bf16[2,2,96,128]{3,2,1,0:T(8,128)(2,1)S(1)}, u32[]{:S(2)}, u32[]{:S(2)}) collective-permute-start(bf16[2,2,96,128]{3,2,1,0:T(8,128)(2,1)} %get-tuple-element.35), channel_id=1, source_target_pairs={{0,5},{1,4},{2,7},{3,6},{4,1},{5,0},{6,3},{7,2},{8,13},{9,12},{10,... | collective-permute-start | bytes 294920 | tf_op jit(solution)/shard_map/ppermute | solution.py:452
  20.5 6.1 %pack.1 = (bf16[24,128,128]{2,1,0:T(8,128)(2,1)}, bf16[24,128,128]{2,1,0:T(8,128)(2,1)}, bf16[24,128,128]{2,1,0:T(8,128)(2,1)}, bf16[24,128,128]{2,1,0:T(8,128)(...) custom-call(s32[4]{0:T(128)} %pad_add_fusion.1.refs_0_.side_ref, ...), custom_call_target="tpu_custom_call" | custom-call | tf_op jit(solution)/shard_map/pack/pallas_call | solution.py:186
  26.6 3.5 %collective-permute-start.6 = (bf16[2,2,96,128]{3,2,1,0:T(8,128)(2,1)S(1)}, bf16[2,2,96,128]{3,2,1,0:T(8,128)(2,1)S(1)}, u32[]{:S(2)}, u32[]{:S(2)}) collective-permute-start(bf16[2,2,96,128]{3,2,1,0:T(8,128)(2,1)S(1)} %copy-done.33), channel_id=1, source_target_pairs={{0,3},{1,2},{2,1},{3,0},{4,7},{5,6},{6,5},{7,4},{8,11},{9,10},{10,... | collective-permute-start | bytes 294920 | tf_op jit(solution)/shard_map/ppermute | solution.py:452
  42.4 12.4 %collective-permute-done.25.refs_0_ = bf16[4,128,128]{2,1,0:T(8,128)(2,1)S(1)} collective-permute-done((bf16[4,128,128]{2,1,0:T(8,128)(2,1)}, bf16[4,128,128]{2,1,0:T(8,128)(2,1)S(1)}, u32[]{:S(2)}, u32[]{:S(2)}) %collective-permute-start.25) | collective-permute-done | bytes 131104 | tf_op jit(solution)/shard_map/ppermute | solution.py:455
  55.8 2.2 %collective-permute-done.26.refs_1_ = bf16[4,128,128]{2,1,0:T(8,128)(2,1)S(1)} collective-permute-done((bf16[4,128,128]{2,1,0:T(8,128)(2,1)}, bf16[4,128,128]{2,1,0:T(8,128)(2,1)S(1)}, u32[]{:S(2)}, u32[]{:S(2)}) %collective-permute-start.26) | collective-permute-done | bytes 131104 | tf_op jit(solution)/shard_map/ppermute | solution.py:455
  58.1 3.4 %collective-permute-start.3 = (bf16[24,128,128]{2,1,0:T(8,128)(2,1)}, bf16[24,128,128]{2,1,0:T(8,128)(2,1)S(1)}, u32[]{:S(2)}, u32[]{:S(2)}) collective-permute-start(bf16[24,128,128]{2,1,0:T(8,128)(2,1)} %get-tuple-element.33), channel_id=1, source_target_pairs={{0,3},{1,2},{2,1},{3,0},{4,7},{5,6},{6,5},{7,4},{8,11},{9,10},{10,... | collective-permute-start | bytes 2359304 | tf_op jit(solution)/shard_map/ppermute | solution.py:452
  62.9 2.5 %collective-permute-done.17.refs_0_ = bf16[4,128,128]{2,1,0:T(8,128)(2,1)S(1)} collective-permute-done((bf16[4,128,128]{2,1,0:T(8,128)(2,1)}, bf16[4,128,128]{2,1,0:T(8,128)(2,1)S(1)}, u32[]{:S(2)}, u32[]{:S(2)}) %collective-permute-start.17) | collective-permute-done | bytes 131104 | tf_op jit(solution)/shard_map/ppermute | solution.py:455
  68.1 2.5 %collective-permute-done.18.refs_1_ = bf16[4,128,128]{2,1,0:T(8,128)(2,1)S(1)} collective-permute-done((bf16[4,128,128]{2,1,0:T(8,128)(2,1)}, bf16[4,128,128]{2,1,0:T(8,128)(2,1)S(1)}, u32[]{:S(2)}, u32[]{:S(2)}) %collective-permute-start.18) | collective-permute-done | bytes 131104 | tf_op jit(solution)/shard_map/ppermute | solution.py:455
  70.6 3.9 %collective-permute-start = (bf16[128,4096]{1,0:T(8,128)(2,1)}, bf16[128,4096]{1,0:T(8,128)(2,1)}, u32[]{:S(2)}, u32[]{:S(2)}) collective-permute-start(bf16[128,4096]{1,0:T(8,128)(2,1)} %fusion), channel_id=1, source_target_pairs={{0,1},{1,2},{2,3},{3,4},{4,5},{5,6},{6,7},{8,9},{9,10},{10,11},{11... | collective-permute-start | bytes 3145736 | tf_op jit(solution)/shard_map/ppermute | solution.py:503
  74.5 2.4 %collective-permute-done.1.refs_3_.refs_4_.refs_5_ = bf16[24,128,128]{2,1,0:T(8,128)(2,1)S(1)} collective-permute-done((bf16[24,128,128]{2,1,0:T(8,128)(2,1)}, bf16[24,128,128]{2,1,0:T(8,128)(2,1)S(1)}, u32[]{:S(2)}, u32[]{:S(2)}) %collective-permute-start.1) | collective-permute-done | bytes 786464 | tf_op jit(solution)/shard_map/ppermute | solution.py:452
  76.9 7.4 %collective-permute-done.12.refs_14_ = bf16[8,2,2,96,128]{4,3,2,1,0:T(8,128)(2,1)} collective-permute-done((bf16[8,2,2,96,128]{4,3,2,1,0:T(8,128)(2,1)}, bf16[8,2,2,96,128]{4,3,2,1,0:T(8,128)(2,1)}, u32[]{:S(2)}, u32[]{:S(2)}) %collective-permute-start.12) | collective-permute-done | bytes 786464 | tf_op jit(solution)/shard_map/ppermute | solution.py:461
  88.7 10.4 %collective-permute-done.3.refs_9_.refs_10_.refs_11_.refs_7_ = bf16[24,128,128]{2,1,0:T(8,128)(2,1)S(1)} collective-permute-done((bf16[24,128,128]{2,1,0:T(8,128)(2,1)}, bf16[24,128,128]{2,1,0:T(8,128)(2,1)S(1)}, u32[]{:S(2)}, u32[]{:S(2)}) %collective-permute-start.3) | collective-permute-done | bytes 786464 | tf_op jit(solution)/shard_map/ppermute | solution.py:452
  101.2 5.4 %visit.3 = (bf16[528,128]{1,0:T(8,128)(2,1)}, bf16[528,128]{1,0:T(8,128)(2,1)}, bf16[528,128]{1,0:T(8,128)(2,1)}, bf16[528,128]{1,0:T(8,128)(2,1)}) custom-call(s32[4]{0:T(128)} %pad_add_fusion.1.refs_0_.side_ref, bf16[4,128,128]{2,1,0:T(8,128)(2,1)} %copy-done.18, bf16[4,128,128]{2,1,0:T(8,128)(2,1)} %copy-done.19, bf16[4,128,128]{2,1,0:T(8,128)(2,1)} %copy-done.21, ...), custom_call_target="tpu_custom_call" | custom-call | flops 536870912 | bytes 4194304 | tf_op jit(solution)/shard_map/visit/pallas_call | solution.py:291
  106.6 6.5 %collective-permute-start.29 = (bf16[528,128]{1,0:T(8,128)(2,1)}, bf16[528,128]{1,0:T(8,128)(2,1)S(1)}, u32[]{:S(2)}, u32[]{:S(2)}) collective-permute-start(bf16[528,128]{1,0:T(8,128)(2,1)} %get-tuple-element.54), channel_id=1, source_target_pairs={{0,4},{1,5},{2,6},{3,7},{8,12},{9,13},{10,14},{11,15},{16,20},{17,... | collective-permute-start | bytes 405512 | tf_op jit(solution)/shard_map/ppermute | solution.py:458
  115.0 5.4 %collective-permute-start.30 = (bf16[528,128]{1,0:T(8,128)(2,1)}, bf16[528,128]{1,0:T(8,128)(2,1)S(1)}, u32[]{:S(2)}, u32[]{:S(2)}) collective-permute-start(bf16[528,128]{1,0:T(8,128)(2,1)} %get-tuple-element.55), channel_id=1, source_target_pairs={{0,5},{1,4},{2,7},{3,6},{8,13},{9,12},{10,15},{11,14},{16,21},{17,... | collective-permute-start | bytes 405512 | tf_op jit(solution)/shard_map/ppermute | solution.py:458
  121.0 5.4 %visit.2 = (bf16[528,128]{1,0:T(8,128)(2,1)}, bf16[528,128]{1,0:T(8,128)(2,1)}, bf16[528,128]{1,0:T(8,128)(2,1)}, bf16[528,128]{1,0:T(8,128)(2,1)}) custom-call(s32[4]{0:T(128)} %pad_add_fusion.1.refs_0_.side_ref, bf16[4,128,128]{2,1,0:T(8,128)(2,1)} %copy-done.20, bf16[4,128,128]{2,1,0:T(8,128)(2,1)} %copy-done.23, bf16[4,128,128]{2,1,0:T(8,128)(2,1)} %copy-done.24, ...), custom_call_target="tpu_custom_call" | custom-call | flops 536870912 | bytes 4194304 | tf_op jit(solution)/shard_map/visit/pallas_call | solution.py:291
  127.7 19.2 %collective-permute-start.32 = (bf16[528,128]{1,0:T(8,128)(2,1)S(1)}, bf16[528,128]{1,0:T(8,128)(2,1)S(1)}, u32[]{:S(2)}, u32[]{:S(2)}) collective-permute-start(bf16[528,128]{1,0:T(8,128)(2,1)S(1)} %copy-done.29), channel_id=1, source_target_pairs={{0,7},{1,6},{2,5},{3,4},{8,15},{9,14},{10,13},{11,12},{16,23},{17,... | collective-permute-start | bytes 405512 | tf_op jit(solution)/shard_map/ppermute | solution.py:458
  149.8 18.9 %own.1 = (bf16[1056,128]{1,0:T(8,128)(2,1)}, bf16[1056,128]{1,0:T(8,128)(2,1)}, bf16[1056,128]{1,0:T(8,128)(2,1)}, bf16[1056,128]{1,0:T(8,128)(2,1)}) custom-call(s32[4]{0:T(128)} %pad_add_fusion.1.refs_0_.side_ref, bf16[24,128,128]{2,1,0:T(8,128)(2,1)} %get-tuple-element.30.refs_0_.refs_1_.refs_2_.refs_4_, ...), custom_call_target="tpu_custom_call" | custom-call | flops 2415919104 | bytes 10485760 | tf_op jit(solution)/shard_map/own/pallas_call | solution.py:373
  168.7 2.9 %collective-permute-start.23 = (bf16[528,128]{1,0:T(8,128)(2,1)S(1)}, bf16[528,128]{1,0:T(8,128)(2,1)S(1)}, u32[]{:S(2)}, u32[]{:S(2)}) collective-permute-start(bf16[528,128]{1,0:T(8,128)(2,1)S(1)} %copy-done.28), channel_id=1, source_target_pairs={{0,6},{1,7},{2,4},{3,5},{8,14},{9,15},{10,12},{11,13},{16,22},{17,... | collective-permute-start | bytes 405512 | tf_op jit(solution)/shard_map/ppermute | solution.py:458
  176.7 23.0 %hyena.1 = bf16[1,128,4096]{2,1,0:T(8,128)(2,1)} custom-call(s32[2]{0:T(128)} %pad_add_fusion.place_ref, bf16[1,128,4096]{2,1,0:T(8,128)(2,1)} %query_ref.1, bf16[1,128,4096]{2,1,0:T(8,128)(2,1)} %key_ref.1, bf16[1,128,4096]{2,1,0:T(8,128)(2,1)} %value_ref.1, bf16[128,4096]{1,0:T(8,128)(2,1)} %collective-permute-done.before_ref, ...), custom_call_target="tpu_custom_call" | custom-call | flops 4294967296 | bytes 6291456 | tf_op jit(solution)/shard_map/hyena/pallas_call | solution.py:51
  200.8 5.3 %merge.1 = bf16[128,32,128]{2,1,0:T(8,128)(2,1)} custom-call(s32[4]{0:T(128)} %pad_add_fusion.1.refs_0_.side_ref, bf16[1056,128]{1,0:T(8,128)(2,1)} %get-tuple-element.38.refs_0_, bf16[1056,128]{1,0:T(8,128)(2,1)} %copy-done.7, bf16[1056,128]{1,0:T(8,128)(2,1)} %copy-done.8, bf16[1056,128]{1,0:T(8,128)(2,1)} %copy-done.9, bf16[528,128]{1,0:T(8,128)(2,1)} %copy-done.14, ...), custom_call_target="tpu_custom_call" | custom-call | tf_op jit(solution)/shard_map/merge/pallas_call | solution.py:430
  (134 shorter events, 43.5 us)
Async XLA Ops:
  12.9 23.7 %collective-permute-start.8 = (bf16[2,2,96,128]{3,2,1,0:T(8,128)(2,1)}, bf16[2,2,96,128]{3,2,1,0:T(8,128)(2,1)S(1)}, u32[]{:S(2)}, u32[]{:S(2)}) collective-permute-start(bf16[2,2,96,128]{3,2,1,0:T(8,128)(2,1)} %get-tuple-element.35), channel_id=1, source_target_pairs={{0,5},{1,4},{2,7},{3,6},{4,1},{5,0},{6,3},{7,2},{8,13},{9,12},{10,... | collective-permute-start | bytes 294920 | tf_op jit(solution)/shard_map/ppermute | solution.py:452
  17.0 21.6 %collective-permute-start.9 = (bf16[2,2,96,128]{3,2,1,0:T(8,128)(2,1)}, bf16[2,2,96,128]{3,2,1,0:T(8,128)(2,1)S(1)}, u32[]{:S(2)}, u32[]{:S(2)}) collective-permute-start(bf16[2,2,96,128]{3,2,1,0:T(8,128)(2,1)} %get-tuple-element.36), channel_id=1, source_target_pairs={{0,6},{1,7},{2,4},{3,5},{4,2},{5,3},{6,0},{7,1},{8,14},{9,15},{10,... | collective-permute-start | bytes 294920 | tf_op jit(solution)/shard_map/ppermute | solution.py:452
  32.7 22.1 %collective-permute-start.25 = (bf16[4,128,128]{2,1,0:T(8,128)(2,1)}, bf16[4,128,128]{2,1,0:T(8,128)(2,1)S(1)}, u32[]{:S(2)}, u32[]{:S(2)}) collective-permute-start(bf16[4,128,128]{2,1,0:T(8,128)(2,1)} %get-tuple-element.50), channel_id=1, source_target_pairs={{4,0},{5,1},{6,2},{7,3},{12,8},{13,9},{14,10},{15,11},{20,16},{21,... | collective-permute-start | bytes 393224 | tf_op jit(solution)/shard_map/ppermute | solution.py:455
  34.7 23.4 %collective-permute-start.26 = (bf16[4,128,128]{2,1,0:T(8,128)(2,1)}, bf16[4,128,128]{2,1,0:T(8,128)(2,1)S(1)}, u32[]{:S(2)}, u32[]{:S(2)}) collective-permute-start(bf16[4,128,128]{2,1,0:T(8,128)(2,1)} %get-tuple-element.51), channel_id=1, source_target_pairs={{4,1},{5,0},{6,3},{7,2},{12,9},{13,8},{14,11},{15,10},{20,17},{21,... | collective-permute-start | bytes 393224 | tf_op jit(solution)/shard_map/ppermute | solution.py:455
  36.6 21.4 %collective-permute-start.27 = (bf16[4,128,128]{2,1,0:T(8,128)(2,1)}, bf16[4,128,128]{2,1,0:T(8,128)(2,1)S(1)}, u32[]{:S(2)}, u32[]{:S(2)}) collective-permute-start(bf16[4,128,128]{2,1,0:T(8,128)(2,1)} %get-tuple-element.52), channel_id=1, source_target_pairs={{4,2},{5,3},{6,0},{7,1},{12,10},{13,11},{14,8},{15,9},{20,18},{21,... | collective-permute-start | bytes 393224 | tf_op jit(solution)/shard_map/ppermute | solution.py:455
  38.5 22.9 %collective-permute-start.28 = (bf16[4,128,128]{2,1,0:T(8,128)(2,1)}, bf16[4,128,128]{2,1,0:T(8,128)(2,1)S(1)}, u32[]{:S(2)}, u32[]{:S(2)}) collective-permute-start(bf16[4,128,128]{2,1,0:T(8,128)(2,1)} %get-tuple-element.53), channel_id=1, source_target_pairs={{4,3},{5,2},{6,1},{7,0},{12,11},{13,10},{14,9},{15,8},{20,19},{21,... | collective-permute-start | bytes 393224 | tf_op jit(solution)/shard_map/ppermute | solution.py:455
  40.5 24.9 %collective-permute-start.17 = (bf16[4,128,128]{2,1,0:T(8,128)(2,1)}, bf16[4,128,128]{2,1,0:T(8,128)(2,1)S(1)}, u32[]{:S(2)}, u32[]{:S(2)}) collective-permute-start(bf16[4,128,128]{2,1,0:T(8,128)(2,1)} %get-tuple-element.42), channel_id=1, source_target_pairs={{4,0},{5,1},{6,2},{7,3},{12,8},{13,9},{14,10},{15,11},{20,16},{21,... | collective-permute-start | bytes 393224 | tf_op jit(solution)/shard_map/ppermute | solution.py:455
  54.8 22.1 %collective-permute-start.1 = (bf16[24,128,128]{2,1,0:T(8,128)(2,1)}, bf16[24,128,128]{2,1,0:T(8,128)(2,1)S(1)}, u32[]{:S(2)}, u32[]{:S(2)}) collective-permute-start(bf16[24,128,128]{2,1,0:T(8,128)(2,1)} %get-tuple-element.31), channel_id=1, source_target_pairs={{0,1},{1,0},{2,3},{3,2},{4,5},{5,4},{6,7},{7,6},{8,9},{9,8},{10,11... | collective-permute-start | bytes 2359304 | tf_op jit(solution)/shard_map/ppermute | solution.py:452
  58.0 29.4 %collective-permute-start.2 = (bf16[24,128,128]{2,1,0:T(8,128)(2,1)}, bf16[24,128,128]{2,1,0:T(8,128)(2,1)S(1)}, u32[]{:S(2)}, u32[]{:S(2)}) collective-permute-start(bf16[24,128,128]{2,1,0:T(8,128)(2,1)} %get-tuple-element.32), channel_id=1, source_target_pairs={{0,2},{1,3},{2,0},{3,1},{4,6},{5,7},{6,4},{7,5},{8,10},{9,11},{10,... | collective-permute-start | bytes 2359304 | tf_op jit(solution)/shard_map/ppermute | solution.py:452
  58.1 41.0 %collective-permute-start.3 = (bf16[24,128,128]{2,1,0:T(8,128)(2,1)}, bf16[24,128,128]{2,1,0:T(8,128)(2,1)S(1)}, u32[]{:S(2)}, u32[]{:S(2)}) collective-permute-start(bf16[24,128,128]{2,1,0:T(8,128)(2,1)} %get-tuple-element.33), channel_id=1, source_target_pairs={{0,3},{1,2},{2,1},{3,0},{4,7},{5,6},{6,5},{7,4},{8,11},{9,10},{10,... | collective-permute-start | bytes 2359304 | tf_op jit(solution)/shard_map/ppermute | solution.py:452
  70.6 104.6 %collective-permute-start = (bf16[128,4096]{1,0:T(8,128)(2,1)}, bf16[128,4096]{1,0:T(8,128)(2,1)}, u32[]{:S(2)}, u32[]{:S(2)}) collective-permute-start(bf16[128,4096]{1,0:T(8,128)(2,1)} %fusion), channel_id=1, source_target_pairs={{0,1},{1,2},{2,3},{3,4},{4,5},{5,6},{6,7},{8,9},{9,10},{10,11},{11... | collective-permute-start | bytes 3145736 | tf_op jit(solution)/shard_map/ppermute | solution.py:503
  76.9 49.5 %collective-permute-start.11 = (bf16[8,2,2,96,128]{4,3,2,1,0:T(8,128)(2,1)}, bf16[8,2,2,96,128]{4,3,2,1,0:T(8,128)(2,1)}, u32[]{:S(2)}, u32[]{:S(2)}) collective-permute-start(bf16[8,2,2,96,128]{4,3,2,1,0:T(8,128)(2,1)} %bitcast_dynamic-update-slice_fusion.refs_12_), channel_id=1, source_target_pairs={{0,8},{8,0},{16,24},{24,16},{1,9},{9,1},{17,25},{25,17},{2,10},{10... | collective-permute-start | bytes 2359304 | tf_op jit(solution)/shard_map/ppermute | solution.py:461
  84.4 64.0 %collective-permute-start.13 = (bf16[8,2,2,96,128]{4,3,2,1,0:T(8,128)(2,1)}, bf16[8,2,2,96,128]{4,3,2,1,0:T(8,128)(2,1)}, u32[]{:S(2)}, u32[]{:S(2)}) collective-permute-start(bf16[8,2,2,96,128]{4,3,2,1,0:T(8,128)(2,1)} %collective-permute-done.12.refs_14_), channel_id=1, source_target_pairs={{0,8},{8,0},{16,24},{24,16},{1,9},{9,1},{17,25},{25,17},{2,10},{10... | collective-permute-start | bytes 2359304 | tf_op jit(solution)/shard_map/ppermute | solution.py:461
  106.6 21.1 %collective-permute-start.29 = (bf16[528,128]{1,0:T(8,128)(2,1)}, bf16[528,128]{1,0:T(8,128)(2,1)S(1)}, u32[]{:S(2)}, u32[]{:S(2)}) collective-permute-start(bf16[528,128]{1,0:T(8,128)(2,1)} %get-tuple-element.54), channel_id=1, source_target_pairs={{0,4},{1,5},{2,6},{3,7},{8,12},{9,13},{10,14},{11,15},{16,20},{17,... | collective-permute-start | bytes 405512 | tf_op jit(solution)/shard_map/ppermute | solution.py:458
  115.0 32.0 %collective-permute-start.30 = (bf16[528,128]{1,0:T(8,128)(2,1)}, bf16[528,128]{1,0:T(8,128)(2,1)S(1)}, u32[]{:S(2)}, u32[]{:S(2)}) collective-permute-start(bf16[528,128]{1,0:T(8,128)(2,1)} %get-tuple-element.55), channel_id=1, source_target_pairs={{0,5},{1,4},{2,7},{3,6},{8,13},{9,12},{10,15},{11,14},{16,21},{17,... | collective-permute-start | bytes 405512 | tf_op jit(solution)/shard_map/ppermute | solution.py:458
  126.4 42.3 %collective-permute-start.31 = (bf16[528,128]{1,0:T(8,128)(2,1)S(1)}, bf16[528,128]{1,0:T(8,128)(2,1)S(1)}, u32[]{:S(2)}, u32[]{:S(2)}) collective-permute-start(bf16[528,128]{1,0:T(8,128)(2,1)S(1)} %copy-done.30), channel_id=1, source_target_pairs={{0,6},{1,7},{2,4},{3,5},{8,14},{9,15},{10,12},{11,13},{16,22},{17,... | collective-permute-start | bytes 405512 | tf_op jit(solution)/shard_map/ppermute | solution.py:458
  127.7 43.8 %collective-permute-start.32 = (bf16[528,128]{1,0:T(8,128)(2,1)S(1)}, bf16[528,128]{1,0:T(8,128)(2,1)S(1)}, u32[]{:S(2)}, u32[]{:S(2)}) collective-permute-start(bf16[528,128]{1,0:T(8,128)(2,1)S(1)} %copy-done.29), channel_id=1, source_target_pairs={{0,7},{1,6},{2,5},{3,4},{8,15},{9,14},{10,13},{11,12},{16,23},{17,... | collective-permute-start | bytes 405512 | tf_op jit(solution)/shard_map/ppermute | solution.py:458
  147.0 26.1 %collective-permute-start.21 = (bf16[528,128]{1,0:T(8,128)(2,1)}, bf16[528,128]{1,0:T(8,128)(2,1)S(1)}, u32[]{:S(2)}, u32[]{:S(2)}) collective-permute-start(bf16[528,128]{1,0:T(8,128)(2,1)} %get-tuple-element.46), channel_id=1, source_target_pairs={{0,4},{1,5},{2,6},{3,7},{8,12},{9,13},{10,14},{11,15},{16,20},{17,... | collective-permute-start | bytes 405512 | tf_op jit(solution)/shard_map/ppermute | solution.py:458
  148.4 26.3 %collective-permute-start.22 = (bf16[528,128]{1,0:T(8,128)(2,1)}, bf16[528,128]{1,0:T(8,128)(2,1)S(1)}, u32[]{:S(2)}, u32[]{:S(2)}) collective-permute-start(bf16[528,128]{1,0:T(8,128)(2,1)} %get-tuple-element.47), channel_id=1, source_target_pairs={{0,5},{1,4},{2,7},{3,6},{8,13},{9,12},{10,15},{11,14},{16,21},{17,... | collective-permute-start | bytes 405512 | tf_op jit(solution)/shard_map/ppermute | solution.py:458
  168.7 31.1 %collective-permute-start.23 = (bf16[528,128]{1,0:T(8,128)(2,1)S(1)}, bf16[528,128]{1,0:T(8,128)(2,1)S(1)}, u32[]{:S(2)}, u32[]{:S(2)}) collective-permute-start(bf16[528,128]{1,0:T(8,128)(2,1)S(1)} %copy-done.28), channel_id=1, source_target_pairs={{0,6},{1,7},{2,4},{3,5},{8,14},{9,15},{10,12},{11,13},{16,22},{17,... | collective-permute-start | bytes 405512 | tf_op jit(solution)/shard_map/ppermute | solution.py:458
  171.6 28.2 %collective-permute-start.24 = (bf16[528,128]{1,0:T(8,128)(2,1)S(1)}, bf16[528,128]{1,0:T(8,128)(2,1)S(1)}, u32[]{:S(2)}, u32[]{:S(2)}) collective-permute-start(bf16[528,128]{1,0:T(8,128)(2,1)S(1)} %copy-done.27), channel_id=1, source_target_pairs={{0,7},{1,6},{2,5},{3,4},{8,15},{9,14},{10,13},{11,12},{16,23},{17,... | collective-permute-start | bytes 405512 | tf_op jit(solution)/shard_map/ppermute | solution.py:458
  173.1 26.7 %collective-permute-start.14 = (bf16[1056,128]{1,0:T(8,128)(2,1)}, bf16[1056,128]{1,0:T(8,128)(2,1)S(1)}, u32[]{:S(2)}, u32[]{:S(2)}) collective-permute-start(bf16[1056,128]{1,0:T(8,128)(2,1)} %get-tuple-element.39), channel_id=1, source_target_pairs={{0,1},{1,0},{2,3},{3,2},{4,5},{5,4},{6,7},{7,6},{8,9},{9,8},{10,11... | collective-permute-start | bytes 811016 | tf_op jit(solution)/shard_map/ppermute | solution.py:452
  174.7 25.2 %collective-permute-start.15 = (bf16[1056,128]{1,0:T(8,128)(2,1)}, bf16[1056,128]{1,0:T(8,128)(2,1)S(1)}, u32[]{:S(2)}, u32[]{:S(2)}) collective-permute-start(bf16[1056,128]{1,0:T(8,128)(2,1)} %get-tuple-element.40), channel_id=1, source_target_pairs={{0,2},{1,3},{2,0},{3,1},{4,6},{5,7},{6,4},{7,5},{8,10},{9,11},{10,... | collective-permute-start | bytes 811016 | tf_op jit(solution)/shard_map/ppermute | solution.py:452
  175.2 24.6 %collective-permute-start.16 = (bf16[1056,128]{1,0:T(8,128)(2,1)}, bf16[1056,128]{1,0:T(8,128)(2,1)S(1)}, u32[]{:S(2)}, u32[]{:S(2)}) collective-permute-start(bf16[1056,128]{1,0:T(8,128)(2,1)} %get-tuple-element.41), channel_id=1, source_target_pairs={{0,3},{1,2},{2,1},{3,0},{4,7},{5,6},{6,5},{7,4},{8,11},{9,10},{10,... | collective-permute-start | bytes 811016 | tf_op jit(solution)/shard_map/ppermute | solution.py:452
  (43 other events, 623.0 us)

commit v3 on v1

v3 whole, which is shorter than its diff:
```python
import functools
import math

import jax
import jax.numpy as jnp
from jax import lax
from jax.experimental import pallas as pl
from jax.experimental.pallas import tpu as pltpu
from jax.sharding import PartitionSpec as P

CH_GROUP = 16
LANES = 128
VMEM = 56 * 1024 * 1024
WAVES = 2
SIDE = 4
BLOCK = 256
EARLY = 2

masked_score = -1e30
TINY = pl.CostEstimate(flops=1, bytes_accessed=1, transcendentals=0)

bf16 = jnp.bfloat16
f32 = jnp.float32


def hyena_kernel(place_ref, query_ref, key_ref, value_ref, near_ref, even_ref, odd_ref, tail_ref, wave_ref, *refs):
    rows, lanes = key_ref.shape[1], key_ref.shape[2]
    out_ref = refs[-1]
    groups = LANES // CH_GROUP
    product = (key_ref[0].astype(f32) * value_ref[0].astype(f32)).astype(bf16)
    shape = (rows, lanes)
    first = jnp.broadcast_to(place_ref[0], shape) == 0
    even = jnp.broadcast_to(place_ref[0] % 2, shape) == 0
    lower = jnp.broadcast_to(pl.program_id(0), shape) < pl.num_programs(0) // 2
    earlier = jnp.where(even, even_ref[...].astype(f32), odd_ref[...].astype(f32))
    earlier = jnp.where(lower, near_ref[...].astype(f32), earlier)
    earlier = jnp.where(first, tail_ref[...].astype(f32), earlier)
    extended = jnp.concatenate([earlier.astype(bf16), product], axis=0)
    channel = lax.broadcasted_iota(jnp.int32, (rows, LANES), 1) // CH_GROUP
    tiles = []
    for tile in range(lanes // LANES):
        columns = extended[:, tile * LANES : (tile + 1) * LANES]
        convolved = jnp.zeros((rows, LANES), f32)
        for group in range(groups):
            line = tile * groups + group
            wave = jnp.broadcast_to(wave_ref[line : line + 1, :], (rows, 2 * rows))
            taps = pltpu.roll(wave, 0, 1, stride=1, stride_axis=0)
            high = taps.astype(bf16)
            low = (taps - high.astype(f32)).astype(bf16)
            term = jnp.dot(high, columns, preferred_element_type=f32) + jnp.dot(
                low, columns, preferred_element_type=f32
            )
            convolved = jnp.where(channel == group, term, convolved)
        tiles.append(convolved)
    convolved = jnp.concatenate(tiles, axis=1)
    places = lax.broadcasted_iota(jnp.int32, (rows, lanes), 0)
    gated = query_ref[0].astype(f32) * convolved
    out_ref[0] = jnp.where(places < place_ref[1], gated, 0.0).astype(bf16)


def hyena(query, key, value, received, constants, place, after):
    _, rows, channels = key.shape
    wave, tail = constants
    groups = LANES // CH_GROUP
    lanes = math.gcd(channels // 2, 8 * LANES)
    steps = channels // lanes // 2
    block = pl.BlockSpec((1, rows, lanes), lambda i: (0, 0, i))
    flat = pl.BlockSpec((rows, lanes), lambda i: (0, i))
    return pl.pallas_call(
        hyena_kernel,
        grid=(channels // lanes,),
        out_shape=jax.ShapeDtypeStruct(query.shape, bf16),
        in_specs=[
            pl.BlockSpec(memory_space=pltpu.SMEM),
            block,
            block,
            block,
            pl.BlockSpec((rows, lanes), lambda i: (0, jnp.minimum(i, steps - 1))),
            pl.BlockSpec((rows, lanes), lambda i: (0, jnp.maximum(i - steps, 0))),
            pl.BlockSpec((rows, lanes), lambda i: (0, jnp.maximum(i - steps, 0))),
            flat,
            pl.BlockSpec((lanes // CH_GROUP, 2 * rows), lambda i: (i, 0)),
        ]
        + [pl.BlockSpec(memory_space=pl.ANY)] * len(after),
        out_specs=block,
        cost_estimate=TINY,
        name="hyena",
    )(place, query, key, value, *received, tail, wave, *after)


def attend_kernel(block_rows, q_ref, k_ref, v_ref, ck_ref, cv_ref, out_ref):
    sources, _, rows, width = k_ref.shape
    index = pl.program_id(1)
    scaling = 1.0 / math.sqrt(width)
    context = ck_ref.shape[1] * ck_ref.shape[3]
    contract = (((1,), (1,)), ((), ()))
    queries = q_ref[...].reshape(block_rows, width)
    per = block_rows // rows

    def fold(carried, scores, values):
        run_max, run_total, mixed = carried
        highest = jnp.maximum(run_max, jnp.max(scores, axis=1, keepdims=True))
        weights = jnp.exp((scores - highest) * scaling)
        shrink = jnp.exp((run_max - highest) * scaling)
        total = run_total * shrink + jnp.sum(weights, axis=1, keepdims=True)
        mixed = mixed * shrink + jnp.dot(weights.astype(bf16), values, preferred_element_type=f32)
        return highest, total, mixed

    def own(block):
        keys = k_ref[pl.ds(block * per, per), 0].reshape(block_rows, width)
        values = v_ref[pl.ds(block * per, per), 0].reshape(block_rows, width)
        return lax.dot_general(queries, keys, contract, preferred_element_type=f32), values

    scores, values = own(index)
    shape = (block_rows, block_rows)
    allowed = lax.broadcasted_iota(jnp.int32, shape, 1) <= lax.broadcasted_iota(jnp.int32, shape, 0)
    scores = jnp.where(allowed, scores, masked_score)
    start = (
        jnp.full((block_rows, 1), masked_score, f32),
        jnp.zeros((block_rows, 1), f32),
        jnp.zeros((block_rows, width), f32),
    )
    carried = fold(start, scores, values)
    carried = lax.fori_loop(0, index, lambda i, c: fold(c, *own(i)), carried)
    context_keys = ck_ref[0, :, 0].reshape(context, width)
    context_values = cv_ref[0, :, 0].reshape(context, width)
    scores = lax.dot_general(queries, context_keys, contract, preferred_element_type=f32)
    _, total, mixed = fold(carried, scores, context_values)
    out_ref[...] = (mixed / total).astype(bf16).reshape(out_ref.shape)


def attend(queries, keys, values, context):
    sources, heads, rows, width = queries.shape
    per = 2 if sources % 2 == 0 else 1
    whole = pl.BlockSpec((sources, 1, rows, width), lambda h, i: (0, h, 0, 0))
    part = pl.BlockSpec((per, 1, rows, width), lambda h, i: (i, h, 0, 0))

    def shared(which):
        return pl.BlockSpec((1, context.shape[1], 1) + context.shape[3:], lambda h, i: (h, 0, which, 0, 0))

    length, context_rows = sources * rows, context.shape[1] * context.shape[3]
    pairs = heads * length * (context_rows + (length + rows * per) // 2)
    return pl.pallas_call(
        functools.partial(attend_kernel, rows * per),
        grid=(heads, sources // per),
        out_shape=jax.ShapeDtypeStruct(queries.shape, bf16),
        in_specs=[part, whole, whole, shared(0), shared(1)],
        out_specs=part,
        cost_estimate=TINY,
        compiler_params=pltpu.CompilerParams(vmem_limit_bytes=VMEM),
        name="attend",
    )(queries, keys, values, context, context)


def attention_by_heads(cont_queries, cont_keys, cont_values, context_keys, context_values, left):
    peers = lax.axis_size("seq")
    rows, heads, width = cont_queries.shape
    share = heads // peers

    def by_owner(x):
        return x.reshape(x.shape[0], peers, share, width).transpose(1, 2, 0, 3)

    def exchange(x):
        return lax.all_to_all(x, "seq", split_axis=0, concat_axis=0, tiled=True)

    pair = exchange(jnp.stack([by_owner(context_keys), by_owner(context_values)], axis=2))
    context = pair.transpose(1, 0, 2, 3, 4)
    queries = exchange(by_owner(cont_queries))
    keys = exchange(by_owner(cont_keys))
    values = exchange(by_owner(cont_values))
    attended = exchange(attend(queries, keys, values, context))
    attention = attended.transpose(2, 0, 1, 3).reshape(rows, heads, width)
    keep = jnp.arange(rows)[:, None, None] < left
    return jnp.where(keep, attention, jnp.zeros((), bf16))


def pack_kernel(peers, side_ref, *refs):
    sources, outs, (heads_first, context_first) = refs[:5], refs[5:-2], refs[-2:]
    rows, heads, _ = sources[0].shape
    share = heads // peers
    each = share // WAVES
    for which, ref in enumerate(sources[:3]):
        heads_first[...] = jnp.transpose(ref[...], (1, 0, 2))
        for index, out in enumerate(outs):
            wave, partner = divmod(index, peers)
            start = (side_ref[2] ^ partner) * share + wave * each
            taken = heads_first[pl.ds(start, each)]
            for head in range(each):
                at = (which * each + head) * rows
                out[at : at + rows] = taken[head]
    for which, ref in enumerate(sources[3:]):
        context_first[...] = jnp.transpose(ref[...], (1, 0, 2))
        for partner, out in enumerate(outs[:peers]):
            start = (side_ref[2] ^ partner) * share + side_ref[1]
            at = 3 * each * rows + which * ref.shape[0]
            out[at : at + ref.shape[0]] = context_first[pl.ds(start, 1)][0]


def pack(arrays, side, peers):
    rows, heads, width = arrays[0].shape
    context_rows = arrays[3].shape[0]
    size = 3 * heads // peers // WAVES * rows
    sizes = [size + 2 * context_rows] * peers + [size] * (peers * (WAVES - 1))
    packed = pl.pallas_call(
        functools.partial(pack_kernel, peers),
        grid_spec=pltpu.PrefetchScalarGridSpec(
            num_scalar_prefetch=1,
            grid=(1,),
            in_specs=[pl.BlockSpec(x.shape, lambda i, s: (0, 0, 0)) for x in arrays],
            out_specs=[pl.BlockSpec((n, width), lambda i, s: (0, 0)) for n in sizes],
            scratch_shapes=[pltpu.VMEM((heads, rows, width), bf16), pltpu.VMEM((heads, context_rows, width), bf16)],
        ),
        out_shape=[jax.ShapeDtypeStruct((n, width), bf16) for n in sizes],
        cost_estimate=TINY,
        compiler_params=pltpu.CompilerParams(vmem_limit_bytes=VMEM),
        name="pack",
    )(side, *arrays)
    return [list(packed[wave * peers : (wave + 1) * peers]) for wave in range(WAVES)]


def gate_kernel(*refs):
    pass


def gate(x, after):
    anywhere = pl.BlockSpec(memory_space=pl.ANY)
    return pl.pallas_call(
        gate_kernel,
        in_specs=[anywhere] * (1 + len(after)),
        out_specs=anywhere,
        out_shape=jax.ShapeDtypeStruct(x.shape, x.dtype),
        input_output_aliases={0: 0},
        cost_estimate=TINY,
        name="gate",
    )(x, *after)


def gather_kernel(*refs):
    for index in range(refs[-1].shape[0]):
        refs[-1][index] = refs[index][...]


def gather(arrays, size, after):
    last = arrays[0].shape[0] // size - 1
    shape = (len(arrays), size, arrays[0].shape[1])
    return pl.pallas_call(
        gather_kernel,
        grid=(1,),
        in_specs=[pl.BlockSpec(shape[1:], lambda i: (last, 0))] * len(arrays)
        + [pl.BlockSpec(memory_space=pl.ANY)] * len(after),
        out_specs=pl.BlockSpec(shape, lambda i: (0, 0, 0)),
        out_shape=jax.ShapeDtypeStruct(shape, bf16),
        cost_estimate=TINY,
        name="gather",
    )(*arrays, *after)


def softmax_columns(pieces, scaling):
    highest = functools.reduce(jnp.maximum, [jnp.max(s, axis=0, keepdims=True) for s, _ in pieces])
    total = mixed = 0.0
    for scores, values in pieces:
        weights = jnp.exp((scores - highest) * scaling)
        total += jnp.sum(weights, axis=0, keepdims=True)
        mixed += lax.dot_general(values, weights.astype(bf16), (((0,), (0,)), ((), ())), preferred_element_type=f32)
    return mixed / total


def products(keys, queries):
    return lax.dot_general(keys, queries, (((1,), (1,)), ((), ())), preferred_element_type=f32)


def wave_kernel(wave, peers, side_ref, *refs):
    arrived, contexts, refs = refs[: 3 * peers], refs[3 * peers : 3 * peers + SIDE], refs[-peers - 6 :]
    outs, (qs, ks, vs, os, slots, sems) = refs[:peers], refs[peers:]
    rows, width = arrived[0].shape
    step = pl.program_id(0)
    each = slots.shape[0]
    scaling = 1.0 / math.sqrt(width)
    context_rows = slots.shape[2] // 2

    def each_copy(head, act):
        part = (wave * each + head) ^ side_ref[1]
        for number in range(SIDE):

            @pl.when(part == number)
            def _():
                act(pltpu.make_async_copy(contexts[number], slots.at[head], sems.at[head]))

    @pl.when(step == 0)
    def _():
        for head in range(each):
            each_copy(head, lambda copy: copy.start())

    places = [pl.ds(pl.multiple_of((side_ref[2] ^ partner) * rows, rows), rows) for partner in range(peers)]
    for partner, place in enumerate(places):
        qs[place] = arrived[3 * partner][...]
        ks[place] = arrived[3 * partner + 1][...]
        vs[place] = arrived[3 * partner + 2][...]

    for head in range(each):

        @pl.when(step == head)
        def _():
            each_copy(head, lambda copy: copy.wait())

    context_keys = slots[step, :, :context_rows].reshape(peers * context_rows, width)
    context_values = slots[step, :, context_rows:].reshape(peers * context_rows, width)
    block = min(BLOCK, peers * rows)
    for index in range(peers * rows // block):
        here = slice(index * block, (index + 1) * block)
        queries = qs[here]
        pieces = [(products(context_keys, queries), context_values)]
        if index > 0:
            before = slice(0, index * block)
            pieces.append((products(ks[before], queries), vs[before]))
        scores = products(ks[here], queries)
        allowed = lax.broadcasted_iota(jnp.int32, scores.shape, 0) <= lax.broadcasted_iota(
            jnp.int32, scores.shape, 1
        )
        pieces.append((jnp.where(allowed, scores, masked_score), vs[here]))
        os[here] = softmax_columns(pieces, scaling).T.astype(bf16)
    for partner, place in enumerate(places):
        outs[partner][0] = os[place]


def attend_wave(wave, arrived, contexts, side, after):
    peers = len(arrived)
    rows, width = LANES, arrived[0].shape[1]
    each = arrived[0].shape[0] // rows // 3

    def taken(which):
        return pl.BlockSpec((rows, width), lambda i, s: (which * each + i, 0))

    result = pl.BlockSpec((1, rows, width), lambda i, s: (i, 0, 0))
    return pl.pallas_call(
        functools.partial(wave_kernel, wave, peers),
        grid_spec=pltpu.PrefetchScalarGridSpec(
            num_scalar_prefetch=1,
            grid=(each,),
            in_specs=[taken(which) for _ in arrived for which in range(3)]
            + [pl.BlockSpec(memory_space=pl.ANY)] * (SIDE + len(after)),
            out_specs=[result] * peers,
            scratch_shapes=[pltpu.VMEM((peers * rows, width), bf16)] * 4
            + [pltpu.VMEM((each,) + contexts[0].shape, bf16), pltpu.SemaphoreType.DMA((each,))],
        ),
        out_shape=[jax.ShapeDtypeStruct((each, rows, width), bf16)] * peers,
        cost_estimate=TINY,
        compiler_params=pltpu.CompilerParams(vmem_limit_bytes=VMEM),
        name="attend_wave",
    )(side, *[x for x in arrived for _ in range(3)], *contexts, *after)


def unpack_kernel(peers, side_ref, *refs):
    arrived, (out, heads_first) = refs[:-2], refs[-2:]
    each = arrived[0].shape[0]
    for index, ref in enumerate(arrived):
        wave, partner = divmod(index, peers)
        heads_first[pl.ds((side_ref[2] ^ partner) * each * WAVES + wave * each, each)] = ref[...].astype(f32)
    result = jnp.transpose(heads_first[...], (1, 0, 2))
    place = lax.broadcasted_iota(jnp.int32, result.shape, 0) + pl.program_id(0) * result.shape[0]
    out[...] = jnp.where(place < side_ref[0], result, 0.0).astype(bf16)


def unpack(arrived, side):
    each, rows, width = arrived[0].shape
    heads = each * len(arrived)
    step = rows // 4
    return pl.pallas_call(
        functools.partial(unpack_kernel, len(arrived) // WAVES),
        grid_spec=pltpu.PrefetchScalarGridSpec(
            num_scalar_prefetch=1,
            grid=(rows // step,),
            in_specs=[pl.BlockSpec((each, step, width), lambda i, s: (0, i, 0))] * len(arrived),
            out_specs=pl.BlockSpec((step, heads, width), lambda i, s: (i, 0, 0)),
            scratch_shapes=[pltpu.VMEM((heads, step, width), f32)],
        ),
        out_shape=jax.ShapeDtypeStruct((rows, heads, width), bf16),
        cost_estimate=TINY,
        compiler_params=pltpu.CompilerParams(vmem_limit_bytes=VMEM),
        name="unpack",
    )(side, *arrived)


def in_waves(arrays, left, key, value, constants, finish):
    peers = lax.axis_size("seq")
    cands = lax.axis_size("cand")
    side = jnp.stack([left, lax.axis_index("cand"), lax.axis_index("seq")]).astype(jnp.int32)

    def exchange(parts, chosen):
        parts = list(parts)
        for k in chosen:
            parts[k] = lax.ppermute(parts[k], "seq", [(i, i ^ k) for i in range(peers)])
        return parts

    def swap(x, k):
        return lax.ppermute(x, "cand", [(i, i ^ k) for i in range(cands)])

    everyone, near_by, across_half = range(1, peers), range(1, peers // 2), range(peers // 2, peers)
    one, two = pack(arrays, side, peers)
    one = exchange(one, everyone)
    two = exchange(two, across_half)
    received = brought((key.astype(f32) * value.astype(f32)).astype(bf16))
    context = gather(one, 2 * arrays[3].shape[0], constants)
    across = swap(context, 2)
    contexts = [context, swap(context, 1), across, swap(across, 1)]

    first = attend_wave(0, one, contexts, side, tuple(two[k] for k in across_half[:EARLY]))
    two = [gate(x, (first[0],)) if k in near_by else x for k, x in enumerate(two)]
    two = exchange(two, near_by)
    hyena_out = finish(received, (first[0],))
    second = attend_wave(1, two, contexts, side, (hyena_out,))
    return unpack(exchange(first, everyone) + exchange(second, everyone), side), hyena_out


def brought(product):
    peers = lax.axis_size("seq")
    half = product.shape[1] // 2
    near, far = product[:, :half], product[:, half:]
    near = lax.ppermute(near, "seq", [(i, i + 1) for i in range(peers - 1)])
    odd = lax.ppermute(far, "seq", [(i, i ^ 1) for i in range(peers)])
    even = lax.ppermute(odd, "seq", [(i, i + 2) for i in range(0, peers - 2, 2)])
    return near, even, odd


def local(
    hyena_query,
    hyena_key,
    hyena_value,
    hyena_filters,
    context_tail,
    cont_queries,
    cont_keys,
    cont_values,
    context_keys,
    context_values,
    lengths,
):
    peers = lax.axis_size("seq")
    me = lax.axis_index("seq")
    rows = hyena_key.shape[1]
    heads = cont_queries.shape[2]
    left = (lengths[0] - me * rows).astype(jnp.int32)

    place = jnp.stack([me.astype(jnp.int32), left])

    wave = jnp.pad(hyena_filters[::-1], ((1, 2 * rows - hyena_filters.shape[0] - 1), (0, 0))).T
    constants = (wave, jnp.pad(context_tail, ((1, 0), (0, 0))))

    def finish(received, after):
        return hyena(hyena_query, hyena_key, hyena_value, received, constants, place, after)

    share = heads // peers
    waves = share == SIDE and lax.axis_size("cand") == SIDE and peers & (peers - 1) == 0
    arrays = (cont_queries[0], cont_keys[0], cont_values[0], context_keys, context_values)
    key, value = hyena_key[0], hyena_value[0]
    if waves:
        attention_out, hyena_out = in_waves(arrays, left, key, value, constants, finish)
    else:
        attention_out = attention_by_heads(*arrays, left)
        hyena_out = finish(brought((key.astype(f32) * value.astype(f32)).astype(bf16)), ())
    return (hyena_out, attention_out[None])


def solution(mesh):
    placed = (
        P("cand", "seq", None),
        P("cand", "seq", None),
        P("cand", "seq", None),
        P(),
        P(),
        P("cand", "seq", None, None),
        P("cand", "seq", None, None),
        P("cand", "seq", None, None),
        P("seq", None, None),
        P("seq", None, None),
        P("cand"),
    )
    return jax.shard_map(
        local,
        mesh=mesh,
        in_specs=placed,
        out_specs=(P("cand", "seq", None), P("cand", "seq", None, None)),
        check_vma=False,
    )
```

time: 216 us -> 167 us (0.77)
  the two profiles are of different devices: /device:TPU:19 before, /device:TPU:0 now
where the time goes in v3:
time: 167 us
  starting transfers between devices  79.1 us (47%)
  Pallas kernels  45.4 us (27%)
  waiting for transfers between devices  32.8 us (20%)
  local copies, waits for them, and re-layouts  5.98 us (4%)
  between operations  1.89 us (1%)
    ppermute x28, starting transfers between devices, exchange(): parts[k] = lax.ppermute(parts[k], 'seq', [(i, i ^ k) for i in range(peers)])  68.9 us
    ppermute x28, waiting for transfers between devices, exchange(): parts[k] = lax.ppermute(parts[k], 'seq', [(i, i ^ k) for i in range(peers)])  32.8 us
    pallas_call x2, Pallas kernels, attend_wave(): pl.pallas_call(functools.partial(wave_kernel, wave, peers), grid_spec=plt...  19.5 us
    pallas_call x1, Pallas kernels, hyena(): pl.pallas_call(hyena_kernel, grid=(channels // lanes,), out_shape=jax.Sha...  12.4 us
    pallas_call x1, Pallas kernels, pack(): pl.pallas_call(functools.partial(pack_kernel, peers), grid_spec=pltpu.Pre...  7.29 us
    pallas_call x1, Pallas kernels, unpack(): pl.pallas_call(functools.partial(unpack_kernel, len(arrived) // WAVES), g...  4.31 us
    ppermute x1, starting transfers between devices, brought(): near = lax.ppermute(near, 'seq', [(i, i + 1) for i in range(peers - 1)])  3.45 us
  transfers between devices with their start and end apart: 34, of which 8 were waited for; matrix products, arithmetic and copies ran while one was open for 3% of the time, Pallas kernels for 20%

profile of v3, /device:TPU:0, one launch (start us, length us, event | category | flops | bytes accessed | tf_op | source)
XLA Modules:
  0.0 166.6 jit_solution(14584705375349309633)
XLA Ops:
  1.8 7.3 %pack.1 = (bf16[960,128]{1,0:T(8,128)(2,1)}, bf16[960,128]{1,0:T(8,128)(2,1)}, bf16[960,128]{1,0:T(8,128)(2,1)}, bf16[960,128]{1,0:T(8,128)(2,1)}, bf16[960,128]...) custom-call(s32[3]{0:T(128)} %pad_add_fusion.1.side_ref, ...), custom_call_target="tpu_custom_call" | custom-call | flops 1 | bytes 1 | tf_op jit(solution)/shard_map/pack/pallas_call | solution.py:204
  9.1 3.0 %collective-permute-start.3 = (bf16[960,128]{1,0:T(8,128)(2,1)}, bf16[960,128]{1,0:T(8,128)(2,1)S(1)}, u32[]{:S(2)}, u32[]{:S(2)}) collective-permute-start(bf16[960,128]{1,0:T(8,128)(2,1)} %get-tuple-element.35), channel_id=1, source_target_pairs={{0,1},{1,0},{2,3},{3,2},{4,5},{5,4},{6,7},{7,6},{8,9},{9,8},{10,11... | collective-permute-start | bytes 737288 | tf_op jit(solution)/shard_map/ppermute | solution.py:392
  13.8 3.0 %collective-permute-start.6 = (bf16[960,128]{1,0:T(8,128)(2,1)}, bf16[960,128]{1,0:T(8,128)(2,1)S(1)}, u32[]{:S(2)}, u32[]{:S(2)}) collective-permute-start(bf16[960,128]{1,0:T(8,128)(2,1)} %get-tuple-element.38), channel_id=1, source_target_pairs={{0,4},{1,5},{2,6},{3,7},{4,0},{5,1},{6,2},{7,3},{8,12},{9,13},{10,... | collective-permute-start | bytes 737288 | tf_op jit(solution)/shard_map/ppermute | solution.py:392
  18.3 3.8 %collective-permute-start.8 = (bf16[960,128]{1,0:T(8,128)(2,1)}, bf16[960,128]{1,0:T(8,128)(2,1)S(1)}, u32[]{:S(2)}, u32[]{:S(2)}) collective-permute-start(bf16[960,128]{1,0:T(8,128)(2,1)} %get-tuple-element.40), channel_id=1, source_target_pairs={{0,6},{1,7},{2,4},{3,5},{4,2},{5,3},{6,0},{7,1},{8,14},{9,15},{10,... | collective-permute-start | bytes 737288 | tf_op jit(solution)/shard_map/ppermute | solution.py:392
  22.2 8.7 %collective-permute-done.4.refs_2_.refs_6_.refs_7_.refs_8_ = bf16[960,128]{1,0:T(8,128)(2,1)S(1)} collective-permute-done((bf16[960,128]{1,0:T(8,128)(2,1)}, bf16[960,128]{1,0:T(8,128)(2,1)S(1)}, u32[]{:S(2)}, u32[]{:S(2)}) %collective-permute-start.4) | collective-permute-done | bytes 245792 | tf_op jit(solution)/shard_map/ppermute | solution.py:392
  34.5 2.6 %collective-permute-start.1 = (bf16[128,2048]{1,0:T(8,128)(2,1)S(1)}, bf16[128,2048]{1,0:T(8,128)(2,1)S(1)}, u32[]{:S(2)}, u32[]{:S(2)}) collective-permute-start(bf16[128,2048]{1,0:T(8,128)(2,1)S(1)} %copy-done.23), channel_id=1, source_target_pairs={{0,1},{1,0},{2,3},{3,2},{4,5},{5,4},{6,7},{7,6},{8,9},{9,8},{10,11... | collective-permute-start | bytes 1572872 | tf_op jit(solution)/shard_map/ppermute | solution.py:420
  37.9 13.5 %collective-permute-done.7.refs_5_.refs_15_.refs_16_.refs_17_ = bf16[960,128]{1,0:T(8,128)(2,1)S(1)} collective-permute-done((bf16[960,128]{1,0:T(8,128)(2,1)}, bf16[960,128]{1,0:T(8,128)(2,1)S(1)}, u32[]{:S(2)}, u32[]{:S(2)}) %collective-permute-start.7) | collective-permute-done | bytes 245792 | tf_op jit(solution)/shard_map/ppermute | solution.py:392
  55.7 11.1 %collective-permute-start.13 = (bf16[768,128]{1,0:T(8,128)(2,1)}, bf16[768,128]{1,0:T(8,128)(2,1)S(1)}, u32[]{:S(2)}, u32[]{:S(2)}) collective-permute-start(bf16[768,128]{1,0:T(8,128)(2,1)} %get-tuple-element.42), channel_id=1, source_target_pairs={{0,4},{1,5},{2,6},{3,7},{4,0},{5,1},{6,2},{7,3},{8,12},{9,13},{10,... | collective-permute-start | bytes 589832 | tf_op jit(solution)/shard_map/ppermute | solution.py:392
  67.2 7.3 %collective-permute-start.14 = (bf16[768,128]{1,0:T(8,128)(2,1)}, bf16[768,128]{1,0:T(8,128)(2,1)S(1)}, u32[]{:S(2)}, u32[]{:S(2)}) collective-permute-start(bf16[768,128]{1,0:T(8,128)(2,1)} %get-tuple-element.43), channel_id=1, source_target_pairs={{0,5},{1,4},{2,7},{3,6},{4,1},{5,0},{6,3},{7,2},{8,13},{9,12},{10,... | collective-permute-start | bytes 589832 | tf_op jit(solution)/shard_map/ppermute | solution.py:392
  74.5 3.5 %collective-permute-start = (bf16[128,2048]{1,0:T(8,128)(2,1)S(1)}, bf16[128,2048]{1,0:T(8,128)(2,1)S(1)}, u32[]{:S(2)}, u32[]{:S(2)}) collective-permute-start(bf16[128,2048]{1,0:T(8,128)(2,1)S(1)} %copy-done.22), channel_id=1, source_target_pairs={{0,1},{1,2},{2,3},{3,4},{4,5},{5,6},{6,7},{8,9},{9,10},{10,11},{11... | collective-permute-start | bytes 1572872 | tf_op jit(solution)/shard_map/ppermute | solution.py:419
  78.0 2.1 %collective-permute-start.2 = (bf16[128,2048]{1,0:T(8,128)(2,1)S(1)}, bf16[128,2048]{1,0:T(8,128)(2,1)}, u32[]{:S(2)}, u32[]{:S(2)}) collective-permute-start(bf16[128,2048]{1,0:T(8,128)(2,1)S(1)} %collective-permute-done.1.odd_ref), channel_id=1, source_target_pairs={{0,2},{2,4},{4,6},{8,10},{10,12},{12,14},{16,18},{18,20},{20,22},{... | collective-permute-start | bytes 1572872 | tf_op jit(solution)/shard_map/ppermute | solution.py:421
  80.1 4.4 %collective-permute-done.14.refs_29_.refs_15_.refs_16_.refs_17_ = bf16[768,128]{1,0:T(8,128)(2,1)S(1)} collective-permute-done((bf16[768,128]{1,0:T(8,128)(2,1)}, bf16[768,128]{1,0:T(8,128)(2,1)S(1)}, u32[]{:S(2)}, u32[]{:S(2)}) %collective-permute-start.14) | collective-permute-done | bytes 196640 | tf_op jit(solution)/shard_map/ppermute | solution.py:392
  85.3 4.2 %collective-permute-start.26 = (bf16[768,128]{1,0:T(8,128)(2,1)S(1)}, bf16[768,128]{1,0:T(8,128)(2,1)S(1)}, u32[]{:S(2)}, u32[]{:S(2)}) collective-permute-start(bf16[768,128]{1,0:T(8,128)(2,1)S(1)} %copy-done.39), channel_id=1, source_target_pairs={{0,7},{1,6},{2,5},{3,4},{4,3},{5,2},{6,1},{7,0},{8,15},{9,14},{10,... | collective-permute-start | bytes 589832 | tf_op jit(solution)/shard_map/ppermute | solution.py:392
  90.3 9.7 %attend_wave.2 = (bf16[2,128,128]{2,1,0:T(8,128)(2,1)}, bf16[2,128,128]{2,1,0:T(8,128)(2,1)}, bf16[2,128,128]{2,1,0:T(8,128)(2,1)}, bf16[2,128,128]{2,1,0:T(8,12...) custom-call(s32[3]{0:T(128)} %pad_add_fusion.1.side_ref, ...), custom_call_target="tpu_custom_call" | custom-call | flops 1 | bytes 1 | tf_op jit(solution)/shard_map/attend_wave/pallas_call | solution.py:335
  100.2 5.9 %collective-permute-start.23 = (bf16[768,128]{1,0:T(8,128)(2,1)}, bf16[768,128]{1,0:T(8,128)(2,1)S(1)}, u32[]{:S(2)}, u32[]{:S(2)}) collective-permute-start(bf16[768,128]{1,0:T(8,128)(2,1)} %gate.4), channel_id=1, source_target_pairs={{0,2},{1,3},{2,0},{3,1},{4,6},{5,7},{6,4},{7,5},{8,10},{9,11},{10,... | collective-permute-start | bytes 589832 | tf_op jit(solution)/shard_map/ppermute | solution.py:392
  108.2 4.0 %collective-permute-start.16 = (bf16[2,128,128]{2,1,0:T(8,128)(2,1)S(1)}, bf16[2,128,128]{2,1,0:T(8,128)(2,1)S(1)}, u32[]{:S(2)}, u32[]{:S(2)}) collective-permute-start(bf16[2,128,128]{2,1,0:T(8,128)(2,1)S(1)} %copy-done.46), channel_id=1, source_target_pairs={{0,2},{1,3},{2,0},{3,1},{4,6},{5,7},{6,4},{7,5},{8,10},{9,11},{10,... | collective-permute-start | bytes 196616 | tf_op jit(solution)/shard_map/ppermute | solution.py:392
  112.6 4.5 %collective-permute-start.18 = (bf16[2,128,128]{2,1,0:T(8,128)(2,1)S(1)}, bf16[2,128,128]{2,1,0:T(8,128)(2,1)S(1)}, u32[]{:S(2)}, u32[]{:S(2)}) collective-permute-start(bf16[2,128,128]{2,1,0:T(8,128)(2,1)S(1)} %copy-done.44), channel_id=1, source_target_pairs={{0,4},{1,5},{2,6},{3,7},{4,0},{5,1},{6,2},{7,3},{8,12},{9,13},{10,... | collective-permute-start | bytes 196616 | tf_op jit(solution)/shard_map/ppermute | solution.py:392
  117.8 12.4 %hyena.1.refs_28_ = bf16[1,128,4096]{2,1,0:T(8,128)(2,1)} custom-call(s32[2]{0:T(128)} %pad_add_fusion.place_ref, bf16[1,128,4096]{2,1,0:T(8,128)(2,1)} %query_ref.1, bf16[1,128,4096]{2,1,0:T(8,128)(2,1)} %key_ref.1, bf16[1,128,4096]{2,1,0:T(8,128)(2,1)} %value_ref.1, bf16[128,2048]{1,0:T(8,128)(2,1)} %copy-done.21, ...), custom_call_target="tpu_custom_call" | custom-call | flops 1 | bytes 1 | tf_op jit(solution)/shard_map/hyena/pallas_call | solution.py:69
  130.9 9.8 %attend_wave.3 = (bf16[2,128,128]{2,1,0:T(8,128)(2,1)}, bf16[2,128,128]{2,1,0:T(8,128)(2,1)}, bf16[2,128,128]{2,1,0:T(8,128)(2,1)}, bf16[2,128,128]{2,1,0:T(8,12...) custom-call(s32[3]{0:T(128)} %pad_add_fusion.1.side_ref, ...), custom_call_target="tpu_custom_call" | custom-call | flops 1 | bytes 1 | tf_op jit(solution)/shard_map/attend_wave/pallas_call | solution.py:335
  140.8 2.2 %collective-permute-start.20 = (bf16[2,128,128]{2,1,0:T(8,128)(2,1)S(1)}, bf16[2,128,128]{2,1,0:T(8,128)(2,1)S(1)}, u32[]{:S(2)}, u32[]{:S(2)}) collective-permute-start(bf16[2,128,128]{2,1,0:T(8,128)(2,1)S(1)} %copy-done.42), channel_id=1, source_target_pairs={{0,6},{1,7},{2,4},{3,5},{4,2},{5,3},{6,0},{7,1},{8,14},{9,15},{10,... | collective-permute-start | bytes 196616 | tf_op jit(solution)/shard_map/ppermute | solution.py:392
  146.2 2.3 %collective-permute-start.29 = (bf16[2,128,128]{2,1,0:T(8,128)(2,1)}, bf16[2,128,128]{2,1,0:T(8,128)(2,1)S(1)}, u32[]{:S(2)}, u32[]{:S(2)}) collective-permute-start(bf16[2,128,128]{2,1,0:T(8,128)(2,1)} %get-tuple-element.61), channel_id=1, source_target_pairs={{0,3},{1,2},{2,1},{3,0},{4,7},{5,6},{6,5},{7,4},{8,11},{9,10},{10,... | collective-permute-start | bytes 196616 | tf_op jit(solution)/shard_map/ppermute | solution.py:392
  152.1 2.1 %collective-permute-start.32 = (bf16[2,128,128]{2,1,0:T(8,128)(2,1)}, bf16[2,128,128]{2,1,0:T(8,128)(2,1)S(1)}, u32[]{:S(2)}, u32[]{:S(2)}) collective-permute-start(bf16[2,128,128]{2,1,0:T(8,128)(2,1)} %get-tuple-element.64), channel_id=1, source_target_pairs={{0,6},{1,7},{2,4},{3,5},{4,2},{5,3},{6,0},{7,1},{8,14},{9,15},{10,... | collective-permute-start | bytes 196616 | tf_op jit(solution)/shard_map/ppermute | solution.py:392
  157.5 2.6 %collective-permute-done.31.refs_13_ = bf16[2,128,128]{2,1,0:T(8,128)(2,1)S(1)} collective-permute-done((bf16[2,128,128]{2,1,0:T(8,128)(2,1)}, bf16[2,128,128]{2,1,0:T(8,128)(2,1)S(1)}, u32[]{:S(2)}, u32[]{:S(2)}) %collective-permute-start.31) | collective-permute-done | bytes 65568 | tf_op jit(solution)/shard_map/ppermute | solution.py:392
  162.1 4.3 %unpack.1 = bf16[128,32,128]{2,1,0:T(8,128)(2,1)} custom-call(s32[3]{0:T(128)} %pad_add_fusion.1.side_ref, bf16[2,128,128]{2,1,0:T(8,128)(2,1)} %get-tuple-element.44.refs_0_.refs_1_, bf16[2,128,128]{2,1,0:T(8,128)(2,1)} %copy-done.25, bf16[2,128,128]{2,1,0:T(8,128)(2,1)} %copy-done.26, bf16[2,128,128]{2,1,0:T(8,128)(2,1)} %copy-done.27, ...), custom_call_target="tpu_custom_call" | custom-call | flops 1 | bytes 1 | tf_op jit(solution)/shard_map/unpack/pallas_call | solution.py:368
  (157 shorter events, 30.4 us)
Async XLA Ops:
  12.2 18.7 %collective-permute-start.4 = (bf16[960,128]{1,0:T(8,128)(2,1)}, bf16[960,128]{1,0:T(8,128)(2,1)S(1)}, u32[]{:S(2)}, u32[]{:S(2)}) collective-permute-start(bf16[960,128]{1,0:T(8,128)(2,1)} %get-tuple-element.36), channel_id=1, source_target_pairs={{0,2},{1,3},{2,0},{3,1},{4,6},{5,7},{6,4},{7,5},{8,10},{9,11},{10,... | collective-permute-start | bytes 737288 | tf_op jit(solution)/shard_map/ppermute | solution.py:392
  13.8 20.8 %collective-permute-start.5 = (bf16[960,128]{1,0:T(8,128)(2,1)}, bf16[960,128]{1,0:T(8,128)(2,1)S(1)}, u32[]{:S(2)}, u32[]{:S(2)}) collective-permute-start(bf16[960,128]{1,0:T(8,128)(2,1)} %get-tuple-element.37), channel_id=1, source_target_pairs={{0,3},{1,2},{2,1},{3,0},{4,7},{5,6},{6,5},{7,4},{8,11},{9,10},{10,... | collective-permute-start | bytes 737288 | tf_op jit(solution)/shard_map/ppermute | solution.py:392
  13.8 24.2 %collective-permute-start.6 = (bf16[960,128]{1,0:T(8,128)(2,1)}, bf16[960,128]{1,0:T(8,128)(2,1)S(1)}, u32[]{:S(2)}, u32[]{:S(2)}) collective-permute-start(bf16[960,128]{1,0:T(8,128)(2,1)} %get-tuple-element.38), channel_id=1, source_target_pairs={{0,4},{1,5},{2,6},{3,7},{4,0},{5,1},{6,2},{7,3},{8,12},{9,13},{10,... | collective-permute-start | bytes 737288 | tf_op jit(solution)/shard_map/ppermute | solution.py:392
  16.7 34.7 %collective-permute-start.7 = (bf16[960,128]{1,0:T(8,128)(2,1)}, bf16[960,128]{1,0:T(8,128)(2,1)S(1)}, u32[]{:S(2)}, u32[]{:S(2)}) collective-permute-start(bf16[960,128]{1,0:T(8,128)(2,1)} %get-tuple-element.39), channel_id=1, source_target_pairs={{0,5},{1,4},{2,7},{3,6},{4,1},{5,0},{6,3},{7,2},{8,13},{9,12},{10,... | collective-permute-start | bytes 737288 | tf_op jit(solution)/shard_map/ppermute | solution.py:392
  18.3 33.1 %collective-permute-start.8 = (bf16[960,128]{1,0:T(8,128)(2,1)}, bf16[960,128]{1,0:T(8,128)(2,1)S(1)}, u32[]{:S(2)}, u32[]{:S(2)}) collective-permute-start(bf16[960,128]{1,0:T(8,128)(2,1)} %get-tuple-element.40), channel_id=1, source_target_pairs={{0,6},{1,7},{2,4},{3,5},{4,2},{5,3},{6,0},{7,1},{8,14},{9,15},{10,... | collective-permute-start | bytes 737288 | tf_op jit(solution)/shard_map/ppermute | solution.py:392
  30.9 20.6 %collective-permute-start.9 = (bf16[960,128]{1,0:T(8,128)(2,1)}, bf16[960,128]{1,0:T(8,128)(2,1)S(1)}, u32[]{:S(2)}, u32[]{:S(2)}) collective-permute-start(bf16[960,128]{1,0:T(8,128)(2,1)} %get-tuple-element.41), channel_id=1, source_target_pairs={{0,7},{1,6},{2,5},{3,4},{4,3},{5,2},{6,1},{7,0},{8,15},{9,14},{10,... | collective-permute-start | bytes 737288 | tf_op jit(solution)/shard_map/ppermute | solution.py:392
  34.5 43.5 %collective-permute-start.1 = (bf16[128,2048]{1,0:T(8,128)(2,1)S(1)}, bf16[128,2048]{1,0:T(8,128)(2,1)S(1)}, u32[]{:S(2)}, u32[]{:S(2)}) collective-permute-start(bf16[128,2048]{1,0:T(8,128)(2,1)S(1)} %copy-done.23), channel_id=1, source_target_pairs={{0,1},{1,0},{2,3},{3,2},{4,5},{5,4},{6,7},{7,6},{8,9},{9,8},{10,11... | collective-permute-start | bytes 1572872 | tf_op jit(solution)/shard_map/ppermute | solution.py:420
  54.2 12.6 %collective-permute-start.11 = (bf16[8,192,128]{2,1,0:T(8,128)(2,1)}, bf16[8,192,128]{2,1,0:T(8,128)(2,1)S(1)}, u32[]{:S(2)}, u32[]{:S(2)}) collective-permute-start(bf16[8,192,128]{2,1,0:T(8,128)(2,1)} %gather.1.refs_24_), channel_id=1, source_target_pairs={{0,16},{8,24},{16,0},{24,8},{1,17},{9,25},{17,1},{25,9},{2,18},{10... | collective-permute-start | bytes 1179656 | tf_op jit(solution)/shard_map/ppermute | solution.py:396
  55.7 18.9 %collective-permute-start.13 = (bf16[768,128]{1,0:T(8,128)(2,1)}, bf16[768,128]{1,0:T(8,128)(2,1)S(1)}, u32[]{:S(2)}, u32[]{:S(2)}) collective-permute-start(bf16[768,128]{1,0:T(8,128)(2,1)} %get-tuple-element.42), channel_id=1, source_target_pairs={{0,4},{1,5},{2,6},{3,7},{4,0},{5,1},{6,2},{7,3},{8,12},{9,13},{10,... | collective-permute-start | bytes 589832 | tf_op jit(solution)/shard_map/ppermute | solution.py:392
  66.7 18.6 %collective-permute-start.10 = (bf16[8,192,128]{2,1,0:T(8,128)(2,1)}, bf16[8,192,128]{2,1,0:T(8,128)(2,1)S(1)}, u32[]{:S(2)}, u32[]{:S(2)}) collective-permute-start(bf16[8,192,128]{2,1,0:T(8,128)(2,1)} %gather.1.refs_24_), channel_id=1, source_target_pairs={{0,8},{8,0},{16,24},{24,16},{1,9},{9,1},{17,25},{25,17},{2,10},{10... | collective-permute-start | bytes 1179656 | tf_op jit(solution)/shard_map/ppermute | solution.py:396
  66.7 22.8 %collective-permute-start.12 = (bf16[8,192,128]{2,1,0:T(8,128)(2,1)S(1)}, bf16[8,192,128]{2,1,0:T(8,128)(2,1)S(1)}, u32[]{:S(2)}, u32[]{:S(2)}) collective-permute-start(bf16[8,192,128]{2,1,0:T(8,128)(2,1)S(1)} %collective-permute-done.11.refs_26_), channel_id=1, source_target_pairs={{0,8},{8,0},{16,24},{24,16},{1,9},{9,1},{17,25},{25,17},{2,10},{10... | collective-permute-start | bytes 1179656 | tf_op jit(solution)/shard_map/ppermute | solution.py:396
  67.2 17.3 %collective-permute-start.14 = (bf16[768,128]{1,0:T(8,128)(2,1)}, bf16[768,128]{1,0:T(8,128)(2,1)S(1)}, u32[]{:S(2)}, u32[]{:S(2)}) collective-permute-start(bf16[768,128]{1,0:T(8,128)(2,1)} %get-tuple-element.43), channel_id=1, source_target_pairs={{0,5},{1,4},{2,7},{3,6},{4,1},{5,0},{6,3},{7,2},{8,13},{9,12},{10,... | collective-permute-start | bytes 589832 | tf_op jit(solution)/shard_map/ppermute | solution.py:392
  74.5 32.4 %collective-permute-start = (bf16[128,2048]{1,0:T(8,128)(2,1)S(1)}, bf16[128,2048]{1,0:T(8,128)(2,1)S(1)}, u32[]{:S(2)}, u32[]{:S(2)}) collective-permute-start(bf16[128,2048]{1,0:T(8,128)(2,1)S(1)} %copy-done.22), channel_id=1, source_target_pairs={{0,1},{1,2},{2,3},{3,4},{4,5},{5,6},{6,7},{8,9},{9,10},{10,11},{11... | collective-permute-start | bytes 1572872 | tf_op jit(solution)/shard_map/ppermute | solution.py:419
  78.0 30.1 %collective-permute-start.2 = (bf16[128,2048]{1,0:T(8,128)(2,1)S(1)}, bf16[128,2048]{1,0:T(8,128)(2,1)}, u32[]{:S(2)}, u32[]{:S(2)}) collective-permute-start(bf16[128,2048]{1,0:T(8,128)(2,1)S(1)} %collective-permute-done.1.odd_ref), channel_id=1, source_target_pairs={{0,2},{2,4},{4,6},{8,10},{10,12},{12,14},{16,18},{18,20},{20,22},{... | collective-permute-start | bytes 1572872 | tf_op jit(solution)/shard_map/ppermute | solution.py:421
  84.5 15.6 %collective-permute-start.25 = (bf16[768,128]{1,0:T(8,128)(2,1)S(1)}, bf16[768,128]{1,0:T(8,128)(2,1)S(1)}, u32[]{:S(2)}, u32[]{:S(2)}) collective-permute-start(bf16[768,128]{1,0:T(8,128)(2,1)S(1)} %copy-done.40), channel_id=1, source_target_pairs={{0,6},{1,7},{2,4},{3,5},{4,2},{5,3},{6,0},{7,1},{8,14},{9,15},{10,... | collective-permute-start | bytes 589832 | tf_op jit(solution)/shard_map/ppermute | solution.py:392
  85.3 20.7 %collective-permute-start.26 = (bf16[768,128]{1,0:T(8,128)(2,1)S(1)}, bf16[768,128]{1,0:T(8,128)(2,1)S(1)}, u32[]{:S(2)}, u32[]{:S(2)}) collective-permute-start(bf16[768,128]{1,0:T(8,128)(2,1)S(1)} %copy-done.39), channel_id=1, source_target_pairs={{0,7},{1,6},{2,5},{3,4},{4,3},{5,2},{6,1},{7,0},{8,15},{9,14},{10,... | collective-permute-start | bytes 589832 | tf_op jit(solution)/shard_map/ppermute | solution.py:392
  100.0 12.1 %collective-permute-start.24 = (bf16[768,128]{1,0:T(8,128)(2,1)}, bf16[768,128]{1,0:T(8,128)(2,1)S(1)}, u32[]{:S(2)}, u32[]{:S(2)}) collective-permute-start(bf16[768,128]{1,0:T(8,128)(2,1)} %gate.5), channel_id=1, source_target_pairs={{0,3},{1,2},{2,1},{3,0},{4,7},{5,6},{6,5},{7,4},{8,11},{9,10},{10,... | collective-permute-start | bytes 589832 | tf_op jit(solution)/shard_map/ppermute | solution.py:392
  100.2 12.5 %collective-permute-start.23 = (bf16[768,128]{1,0:T(8,128)(2,1)}, bf16[768,128]{1,0:T(8,128)(2,1)S(1)}, u32[]{:S(2)}, u32[]{:S(2)}) collective-permute-start(bf16[768,128]{1,0:T(8,128)(2,1)} %gate.4), channel_id=1, source_target_pairs={{0,2},{1,3},{2,0},{3,1},{4,6},{5,7},{6,4},{7,5},{8,10},{9,11},{10,... | collective-permute-start | bytes 589832 | tf_op jit(solution)/shard_map/ppermute | solution.py:392
  106.0 24.2 %collective-permute-start.22 = (bf16[768,128]{1,0:T(8,128)(2,1)}, bf16[768,128]{1,0:T(8,128)(2,1)S(1)}, u32[]{:S(2)}, u32[]{:S(2)}) collective-permute-start(bf16[768,128]{1,0:T(8,128)(2,1)} %gate.3), channel_id=1, source_target_pairs={{0,1},{1,0},{2,3},{3,2},{4,5},{5,4},{6,7},{7,6},{8,9},{9,8},{10,11... | collective-permute-start | bytes 589832 | tf_op jit(solution)/shard_map/ppermute | solution.py:392
  107.0 33.8 %collective-permute-start.15 = (bf16[2,128,128]{2,1,0:T(8,128)(2,1)S(1)}, bf16[2,128,128]{2,1,0:T(8,128)(2,1)S(1)}, u32[]{:S(2)}, u32[]{:S(2)}) collective-permute-start(bf16[2,128,128]{2,1,0:T(8,128)(2,1)S(1)} %copy-done.47), channel_id=1, source_target_pairs={{0,1},{1,0},{2,3},{3,2},{4,5},{5,4},{6,7},{7,6},{8,9},{9,8},{10,11... | collective-permute-start | bytes 196616 | tf_op jit(solution)/shard_map/ppermute | solution.py:392
  108.2 34.8 %collective-permute-start.16 = (bf16[2,128,128]{2,1,0:T(8,128)(2,1)S(1)}, bf16[2,128,128]{2,1,0:T(8,128)(2,1)S(1)}, u32[]{:S(2)}, u32[]{:S(2)}) collective-permute-start(bf16[2,128,128]{2,1,0:T(8,128)(2,1)S(1)} %copy-done.46), channel_id=1, source_target_pairs={{0,2},{1,3},{2,0},{3,1},{4,6},{5,7},{6,4},{7,5},{8,10},{9,11},{10,... | collective-permute-start | bytes 196616 | tf_op jit(solution)/shard_map/ppermute | solution.py:392
  112.2 32.9 %collective-permute-start.17 = (bf16[2,128,128]{2,1,0:T(8,128)(2,1)S(1)}, bf16[2,128,128]{2,1,0:T(8,128)(2,1)S(1)}, u32[]{:S(2)}, u32[]{:S(2)}) collective-permute-start(bf16[2,128,128]{2,1,0:T(8,128)(2,1)S(1)} %copy-done.45), channel_id=1, source_target_pairs={{0,3},{1,2},{2,1},{3,0},{4,7},{5,6},{6,5},{7,4},{8,11},{9,10},{10,... | collective-permute-start | bytes 196616 | tf_op jit(solution)/shard_map/ppermute | solution.py:392
  112.6 33.6 %collective-permute-start.18 = (bf16[2,128,128]{2,1,0:T(8,128)(2,1)S(1)}, bf16[2,128,128]{2,1,0:T(8,128)(2,1)S(1)}, u32[]{:S(2)}, u32[]{:S(2)}) collective-permute-start(bf16[2,128,128]{2,1,0:T(8,128)(2,1)S(1)} %copy-done.44), channel_id=1, source_target_pairs={{0,4},{1,5},{2,6},{3,7},{4,0},{5,1},{6,2},{7,3},{8,12},{9,13},{10,... | collective-permute-start | bytes 196616 | tf_op jit(solution)/shard_map/ppermute | solution.py:392
  130.3 16.0 %collective-permute-start.19 = (bf16[2,128,128]{2,1,0:T(8,128)(2,1)S(1)}, bf16[2,128,128]{2,1,0:T(8,128)(2,1)S(1)}, u32[]{:S(2)}, u32[]{:S(2)}) collective-permute-start(bf16[2,128,128]{2,1,0:T(8,128)(2,1)S(1)} %copy-done.43), channel_id=1, source_target_pairs={{0,5},{1,4},{2,7},{3,6},{4,1},{5,0},{6,3},{7,2},{8,13},{9,12},{10,... | collective-permute-start | bytes 196616 | tf_op jit(solution)/shard_map/ppermute | solution.py:392
  (58 other events, 643.9 us)

commit v4 on v3

--- a/solution.py
+++ b/solution.py
@@ -13,7 +13,7 @@
 VMEM = 56 * 1024 * 1024
 WAVES = 2
 SIDE = 4
-BLOCK = 256
+BLOCK = 512
 EARLY = 2
 
 masked_score = -1e30
@@ -355,8 +355,8 @@
     each = arrived[0].shape[0]
     for index, ref in enumerate(arrived):
         wave, partner = divmod(index, peers)
-        heads_first[pl.ds((side_ref[2] ^ partner) * each * WAVES + wave * each, each)] = ref[...].astype(f32)
-    result = jnp.transpose(heads_first[...], (1, 0, 2))
+        heads_first[pl.ds((side_ref[2] ^ partner) * each * WAVES + wave * each, each)] = ref[...]
+    result = jnp.transpose(heads_first[...], (1, 0, 2)).astype(f32)
     place = lax.broadcasted_iota(jnp.int32, result.shape, 0) + pl.program_id(0) * result.shape[0]
     out[...] = jnp.where(place < side_ref[0], result, 0.0).astype(bf16)
 
@@ -364,7 +364,7 @@
 def unpack(arrived, side):
     each, rows, width = arrived[0].shape
     heads = each * len(arrived)
-    step = rows // 4
+    step = rows // 2
     return pl.pallas_call(
         functools.partial(unpack_kernel, len(arrived) // WAVES),
         grid_spec=pltpu.PrefetchScalarGridSpec(
@@ -372,7 +372,7 @@
             grid=(rows // step,),
             in_specs=[pl.BlockSpec((each, step, width), lambda i, s: (0, i, 0))] * len(arrived),
             out_specs=pl.BlockSpec((step, heads, width), lambda i, s: (i, 0, 0)),
-            scratch_shapes=[pltpu.VMEM((heads, step, width), f32)],
+            scratch_shapes=[pltpu.VMEM((heads, step, width), bf16)],
         ),
         out_shape=jax.ShapeDtypeStruct((rows, heads, width), bf16),
         cost_estimate=TINY,

time: 167 us -> 165 us (0.988)
  Pallas kernels: 45.4 us -> 42.7 us
where the time goes in v4:
time: 165 us
  starting transfers between devices  79.9 us (48%)
  Pallas kernels  42.7 us (26%)
  waiting for transfers between devices  32.8 us (20%)
  local copies, waits for them, and re-layouts  5.98 us (4%)
  between operations  1.89 us (1%)
    ppermute x28, starting transfers between devices, exchange(): parts[k] = lax.ppermute(parts[k], 'seq', [(i, i ^ k) for i in range(peers)])  69.8 us
    ppermute x28, waiting for transfers between devices, exchange(): parts[k] = lax.ppermute(parts[k], 'seq', [(i, i ^ k) for i in range(peers)])  32.8 us
    pallas_call x2, Pallas kernels, attend_wave(): pl.pallas_call(functools.partial(wave_kernel, wave, peers), grid_spec=plt...  17.9 us
    pallas_call x1, Pallas kernels, hyena(): pl.pallas_call(hyena_kernel, grid=(channels // lanes,), out_shape=jax.Sha...  12.4 us
    pallas_call x1, Pallas kernels, pack(): pl.pallas_call(functools.partial(pack_kernel, peers), grid_spec=pltpu.Pre...  7.29 us
    ppermute x1, starting transfers between devices, brought(): near = lax.ppermute(near, 'seq', [(i, i + 1) for i in range(peers - 1)])  3.45 us
  transfers between devices with their start and end apart: 34, of which 8 were waited for; matrix products, arithmetic and copies ran while one was open for 3% of the time, Pallas kernels for 20%

profile of v4, /device:TPU:0, one launch (start us, length us, event | category | flops | bytes accessed | tf_op | source)
XLA Modules:
  0.0 164.7 jit_solution(1667214830215862795)
XLA Ops:
  1.8 7.3 %pack.1 = (bf16[960,128]{1,0:T(8,128)(2,1)}, bf16[960,128]{1,0:T(8,128)(2,1)}, bf16[960,128]{1,0:T(8,128)(2,1)}, bf16[960,128]{1,0:T(8,128)(2,1)}, bf16[960,128]...) custom-call(s32[3]{0:T(128)} %pad_add_fusion.1.side_ref, ...), custom_call_target="tpu_custom_call" | custom-call | flops 1 | bytes 1 | tf_op jit(solution)/shard_map/pack/pallas_call | solution.py:204
  9.1 3.0 %collective-permute-start.3 = (bf16[960,128]{1,0:T(8,128)(2,1)}, bf16[960,128]{1,0:T(8,128)(2,1)S(1)}, u32[]{:S(2)}, u32[]{:S(2)}) collective-permute-start(bf16[960,128]{1,0:T(8,128)(2,1)} %get-tuple-element.35), channel_id=1, source_target_pairs={{0,1},{1,0},{2,3},{3,2},{4,5},{5,4},{6,7},{7,6},{8,9},{9,8},{10,11... | collective-permute-start | bytes 737288 | tf_op jit(solution)/shard_map/ppermute | solution.py:392
  13.8 3.0 %collective-permute-start.6 = (bf16[960,128]{1,0:T(8,128)(2,1)}, bf16[960,128]{1,0:T(8,128)(2,1)S(1)}, u32[]{:S(2)}, u32[]{:S(2)}) collective-permute-start(bf16[960,128]{1,0:T(8,128)(2,1)} %get-tuple-element.38), channel_id=1, source_target_pairs={{0,4},{1,5},{2,6},{3,7},{4,0},{5,1},{6,2},{7,3},{8,12},{9,13},{10,... | collective-permute-start | bytes 737288 | tf_op jit(solution)/shard_map/ppermute | solution.py:392
  18.3 3.8 %collective-permute-start.8 = (bf16[960,128]{1,0:T(8,128)(2,1)}, bf16[960,128]{1,0:T(8,128)(2,1)S(1)}, u32[]{:S(2)}, u32[]{:S(2)}) collective-permute-start(bf16[960,128]{1,0:T(8,128)(2,1)} %get-tuple-element.40), channel_id=1, source_target_pairs={{0,6},{1,7},{2,4},{3,5},{4,2},{5,3},{6,0},{7,1},{8,14},{9,15},{10,... | collective-permute-start | bytes 737288 | tf_op jit(solution)/shard_map/ppermute | solution.py:392
  22.2 8.7 %collective-permute-done.4.refs_2_.refs_6_.refs_7_.refs_8_ = bf16[960,128]{1,0:T(8,128)(2,1)S(1)} collective-permute-done((bf16[960,128]{1,0:T(8,128)(2,1)}, bf16[960,128]{1,0:T(8,128)(2,1)S(1)}, u32[]{:S(2)}, u32[]{:S(2)}) %collective-permute-start.4) | collective-permute-done | bytes 245792 | tf_op jit(solution)/shard_map/ppermute | solution.py:392
  34.5 2.6 %collective-permute-start.1 = (bf16[128,2048]{1,0:T(8,128)(2,1)S(1)}, bf16[128,2048]{1,0:T(8,128)(2,1)S(1)}, u32[]{:S(2)}, u32[]{:S(2)}) collective-permute-start(bf16[128,2048]{1,0:T(8,128)(2,1)S(1)} %copy-done.23), channel_id=1, source_target_pairs={{0,1},{1,0},{2,3},{3,2},{4,5},{5,4},{6,7},{7,6},{8,9},{9,8},{10,11... | collective-permute-start | bytes 1572872 | tf_op jit(solution)/shard_map/ppermute | solution.py:420
  37.9 13.5 %collective-permute-done.7.refs_5_.refs_15_.refs_16_.refs_17_ = bf16[960,128]{1,0:T(8,128)(2,1)S(1)} collective-permute-done((bf16[960,128]{1,0:T(8,128)(2,1)}, bf16[960,128]{1,0:T(8,128)(2,1)S(1)}, u32[]{:S(2)}, u32[]{:S(2)}) %collective-permute-start.7) | collective-permute-done | bytes 245792 | tf_op jit(solution)/shard_map/ppermute | solution.py:392
  55.7 11.1 %collective-permute-start.13 = (bf16[768,128]{1,0:T(8,128)(2,1)}, bf16[768,128]{1,0:T(8,128)(2,1)S(1)}, u32[]{:S(2)}, u32[]{:S(2)}) collective-permute-start(bf16[768,128]{1,0:T(8,128)(2,1)} %get-tuple-element.42), channel_id=1, source_target_pairs={{0,4},{1,5},{2,6},{3,7},{4,0},{5,1},{6,2},{7,3},{8,12},{9,13},{10,... | collective-permute-start | bytes 589832 | tf_op jit(solution)/shard_map/ppermute | solution.py:392
  67.2 7.3 %collective-permute-start.14 = (bf16[768,128]{1,0:T(8,128)(2,1)}, bf16[768,128]{1,0:T(8,128)(2,1)S(1)}, u32[]{:S(2)}, u32[]{:S(2)}) collective-permute-start(bf16[768,128]{1,0:T(8,128)(2,1)} %get-tuple-element.43), channel_id=1, source_target_pairs={{0,5},{1,4},{2,7},{3,6},{4,1},{5,0},{6,3},{7,2},{8,13},{9,12},{10,... | collective-permute-start | bytes 589832 | tf_op jit(solution)/shard_map/ppermute | solution.py:392
  74.5 3.5 %collective-permute-start = (bf16[128,2048]{1,0:T(8,128)(2,1)S(1)}, bf16[128,2048]{1,0:T(8,128)(2,1)S(1)}, u32[]{:S(2)}, u32[]{:S(2)}) collective-permute-start(bf16[128,2048]{1,0:T(8,128)(2,1)S(1)} %copy-done.22), channel_id=1, source_target_pairs={{0,1},{1,2},{2,3},{3,4},{4,5},{5,6},{6,7},{8,9},{9,10},{10,11},{11... | collective-permute-start | bytes 1572872 | tf_op jit(solution)/shard_map/ppermute | solution.py:419
  78.0 2.1 %collective-permute-start.2 = (bf16[128,2048]{1,0:T(8,128)(2,1)S(1)}, bf16[128,2048]{1,0:T(8,128)(2,1)}, u32[]{:S(2)}, u32[]{:S(2)}) collective-permute-start(bf16[128,2048]{1,0:T(8,128)(2,1)S(1)} %collective-permute-done.1.odd_ref), channel_id=1, source_target_pairs={{0,2},{2,4},{4,6},{8,10},{10,12},{12,14},{16,18},{18,20},{20,22},{... | collective-permute-start | bytes 1572872 | tf_op jit(solution)/shard_map/ppermute | solution.py:421
  80.1 4.4 %collective-permute-done.14.refs_29_.refs_15_.refs_16_.refs_17_ = bf16[768,128]{1,0:T(8,128)(2,1)S(1)} collective-permute-done((bf16[768,128]{1,0:T(8,128)(2,1)}, bf16[768,128]{1,0:T(8,128)(2,1)S(1)}, u32[]{:S(2)}, u32[]{:S(2)}) %collective-permute-start.14) | collective-permute-done | bytes 196640 | tf_op jit(solution)/shard_map/ppermute | solution.py:392
  85.3 4.2 %collective-permute-start.26 = (bf16[768,128]{1,0:T(8,128)(2,1)S(1)}, bf16[768,128]{1,0:T(8,128)(2,1)S(1)}, u32[]{:S(2)}, u32[]{:S(2)}) collective-permute-start(bf16[768,128]{1,0:T(8,128)(2,1)S(1)} %copy-done.39), channel_id=1, source_target_pairs={{0,7},{1,6},{2,5},{3,4},{4,3},{5,2},{6,1},{7,0},{8,15},{9,14},{10,... | collective-permute-start | bytes 589832 | tf_op jit(solution)/shard_map/ppermute | solution.py:392
  90.3 8.9 %attend_wave.2 = (bf16[2,128,128]{2,1,0:T(8,128)(2,1)}, bf16[2,128,128]{2,1,0:T(8,128)(2,1)}, bf16[2,128,128]{2,1,0:T(8,128)(2,1)}, bf16[2,128,128]{2,1,0:T(8,12...) custom-call(s32[3]{0:T(128)} %pad_add_fusion.1.side_ref, ...), custom_call_target="tpu_custom_call" | custom-call | flops 1 | bytes 1 | tf_op jit(solution)/shard_map/attend_wave/pallas_call | solution.py:335
  99.3 6.7 %collective-permute-start.23 = (bf16[768,128]{1,0:T(8,128)(2,1)}, bf16[768,128]{1,0:T(8,128)(2,1)S(1)}, u32[]{:S(2)}, u32[]{:S(2)}) collective-permute-start(bf16[768,128]{1,0:T(8,128)(2,1)} %gate.4), channel_id=1, source_target_pairs={{0,2},{1,3},{2,0},{3,1},{4,6},{5,7},{6,4},{7,5},{8,10},{9,11},{10,... | collective-permute-start | bytes 589832 | tf_op jit(solution)/shard_map/ppermute | solution.py:392
  108.2 4.0 %collective-permute-start.16 = (bf16[2,128,128]{2,1,0:T(8,128)(2,1)S(1)}, bf16[2,128,128]{2,1,0:T(8,128)(2,1)S(1)}, u32[]{:S(2)}, u32[]{:S(2)}) collective-permute-start(bf16[2,128,128]{2,1,0:T(8,128)(2,1)S(1)} %copy-done.46), channel_id=1, source_target_pairs={{0,2},{1,3},{2,0},{3,1},{4,6},{5,7},{6,4},{7,5},{8,10},{9,11},{10,... | collective-permute-start | bytes 196616 | tf_op jit(solution)/shard_map/ppermute | solution.py:392
  112.6 4.5 %collective-permute-start.18 = (bf16[2,128,128]{2,1,0:T(8,128)(2,1)S(1)}, bf16[2,128,128]{2,1,0:T(8,128)(2,1)S(1)}, u32[]{:S(2)}, u32[]{:S(2)}) collective-permute-start(bf16[2,128,128]{2,1,0:T(8,128)(2,1)S(1)} %copy-done.44), channel_id=1, source_target_pairs={{0,4},{1,5},{2,6},{3,7},{4,0},{5,1},{6,2},{7,3},{8,12},{9,13},{10,... | collective-permute-start | bytes 196616 | tf_op jit(solution)/shard_map/ppermute | solution.py:392
  117.8 12.4 %hyena.1.refs_28_ = bf16[1,128,4096]{2,1,0:T(8,128)(2,1)} custom-call(s32[2]{0:T(128)} %pad_add_fusion.place_ref, bf16[1,128,4096]{2,1,0:T(8,128)(2,1)} %query_ref.1, bf16[1,128,4096]{2,1,0:T(8,128)(2,1)} %key_ref.1, bf16[1,128,4096]{2,1,0:T(8,128)(2,1)} %value_ref.1, bf16[128,2048]{1,0:T(8,128)(2,1)} %copy-done.21, ...), custom_call_target="tpu_custom_call" | custom-call | flops 1 | bytes 1 | tf_op jit(solution)/shard_map/hyena/pallas_call | solution.py:69
  130.9 9.0 %attend_wave.3 = (bf16[2,128,128]{2,1,0:T(8,128)(2,1)}, bf16[2,128,128]{2,1,0:T(8,128)(2,1)}, bf16[2,128,128]{2,1,0:T(8,128)(2,1)}, bf16[2,128,128]{2,1,0:T(8,12...) custom-call(s32[3]{0:T(128)} %pad_add_fusion.1.side_ref, ...), custom_call_target="tpu_custom_call" | custom-call | flops 1 | bytes 1 | tf_op jit(solution)/shard_map/attend_wave/pallas_call | solution.py:335
  139.9 2.2 %collective-permute-start.20 = (bf16[2,128,128]{2,1,0:T(8,128)(2,1)S(1)}, bf16[2,128,128]{2,1,0:T(8,128)(2,1)S(1)}, u32[]{:S(2)}, u32[]{:S(2)}) collective-permute-start(bf16[2,128,128]{2,1,0:T(8,128)(2,1)S(1)} %copy-done.42), channel_id=1, source_target_pairs={{0,6},{1,7},{2,4},{3,5},{4,2},{5,3},{6,0},{7,1},{8,14},{9,15},{10,... | collective-permute-start | bytes 196616 | tf_op jit(solution)/shard_map/ppermute | solution.py:392
  145.4 2.3 %collective-permute-start.29 = (bf16[2,128,128]{2,1,0:T(8,128)(2,1)}, bf16[2,128,128]{2,1,0:T(8,128)(2,1)S(1)}, u32[]{:S(2)}, u32[]{:S(2)}) collective-permute-start(bf16[2,128,128]{2,1,0:T(8,128)(2,1)} %get-tuple-element.61), channel_id=1, source_target_pairs={{0,3},{1,2},{2,1},{3,0},{4,7},{5,6},{6,5},{7,4},{8,11},{9,10},{10,... | collective-permute-start | bytes 196616 | tf_op jit(solution)/shard_map/ppermute | solution.py:392
  151.2 2.1 %collective-permute-start.32 = (bf16[2,128,128]{2,1,0:T(8,128)(2,1)}, bf16[2,128,128]{2,1,0:T(8,128)(2,1)S(1)}, u32[]{:S(2)}, u32[]{:S(2)}) collective-permute-start(bf16[2,128,128]{2,1,0:T(8,128)(2,1)} %get-tuple-element.64), channel_id=1, source_target_pairs={{0,6},{1,7},{2,4},{3,5},{4,2},{5,3},{6,0},{7,1},{8,14},{9,15},{10,... | collective-permute-start | bytes 196616 | tf_op jit(solution)/shard_map/ppermute | solution.py:392
  156.6 2.6 %collective-permute-done.31.refs_13_ = bf16[2,128,128]{2,1,0:T(8,128)(2,1)S(1)} collective-permute-done((bf16[2,128,128]{2,1,0:T(8,128)(2,1)}, bf16[2,128,128]{2,1,0:T(8,128)(2,1)S(1)}, u32[]{:S(2)}, u32[]{:S(2)}) %collective-permute-start.31) | collective-permute-done | bytes 65568 | tf_op jit(solution)/shard_map/ppermute | solution.py:392
  161.3 3.3 %unpack.1 = bf16[128,32,128]{2,1,0:T(8,128)(2,1)} custom-call(s32[3]{0:T(128)} %pad_add_fusion.1.side_ref, bf16[2,128,128]{2,1,0:T(8,128)(2,1)} %get-tuple-element.44.refs_0_.refs_1_, bf16[2,128,128]{2,1,0:T(8,128)(2,1)} %copy-done.25, bf16[2,128,128]{2,1,0:T(8,128)(2,1)} %copy-done.26, bf16[2,128,128]{2,1,0:T(8,128)(2,1)} %copy-done.27, ...), custom_call_target="tpu_custom_call" | custom-call | flops 1 | bytes 1 | tf_op jit(solution)/shard_map/unpack/pallas_call | solution.py:368
  (157 shorter events, 30.4 us)
Async XLA Ops:
  12.2 18.7 %collective-permute-start.4 = (bf16[960,128]{1,0:T(8,128)(2,1)}, bf16[960,128]{1,0:T(8,128)(2,1)S(1)}, u32[]{:S(2)}, u32[]{:S(2)}) collective-permute-start(bf16[960,128]{1,0:T(8,128)(2,1)} %get-tuple-element.36), channel_id=1, source_target_pairs={{0,2},{1,3},{2,0},{3,1},{4,6},{5,7},{6,4},{7,5},{8,10},{9,11},{10,... | collective-permute-start | bytes 737288 | tf_op jit(solution)/shard_map/ppermute | solution.py:392
  13.8 20.8 %collective-permute-start.5 = (bf16[960,128]{1,0:T(8,128)(2,1)}, bf16[960,128]{1,0:T(8,128)(2,1)S(1)}, u32[]{:S(2)}, u32[]{:S(2)}) collective-permute-start(bf16[960,128]{1,0:T(8,128)(2,1)} %get-tuple-element.37), channel_id=1, source_target_pairs={{0,3},{1,2},{2,1},{3,0},{4,7},{5,6},{6,5},{7,4},{8,11},{9,10},{10,... | collective-permute-start | bytes 737288 | tf_op jit(solution)/shard_map/ppermute | solution.py:392
  13.8 24.2 %collective-permute-start.6 = (bf16[960,128]{1,0:T(8,128)(2,1)}, bf16[960,128]{1,0:T(8,128)(2,1)S(1)}, u32[]{:S(2)}, u32[]{:S(2)}) collective-permute-start(bf16[960,128]{1,0:T(8,128)(2,1)} %get-tuple-element.38), channel_id=1, source_target_pairs={{0,4},{1,5},{2,6},{3,7},{4,0},{5,1},{6,2},{7,3},{8,12},{9,13},{10,... | collective-permute-start | bytes 737288 | tf_op jit(solution)/shard_map/ppermute | solution.py:392
  16.7 34.7 %collective-permute-start.7 = (bf16[960,128]{1,0:T(8,128)(2,1)}, bf16[960,128]{1,0:T(8,128)(2,1)S(1)}, u32[]{:S(2)}, u32[]{:S(2)}) collective-permute-start(bf16[960,128]{1,0:T(8,128)(2,1)} %get-tuple-element.39), channel_id=1, source_target_pairs={{0,5},{1,4},{2,7},{3,6},{4,1},{5,0},{6,3},{7,2},{8,13},{9,12},{10,... | collective-permute-start | bytes 737288 | tf_op jit(solution)/shard_map/ppermute | solution.py:392
  18.3 33.1 %collective-permute-start.8 = (bf16[960,128]{1,0:T(8,128)(2,1)}, bf16[960,128]{1,0:T(8,128)(2,1)S(1)}, u32[]{:S(2)}, u32[]{:S(2)}) collective-permute-start(bf16[960,128]{1,0:T(8,128)(2,1)} %get-tuple-element.40), channel_id=1, source_target_pairs={{0,6},{1,7},{2,4},{3,5},{4,2},{5,3},{6,0},{7,1},{8,14},{9,15},{10,... | collective-permute-start | bytes 737288 | tf_op jit(solution)/shard_map/ppermute | solution.py:392
  30.9 20.6 %collective-permute-start.9 = (bf16[960,128]{1,0:T(8,128)(2,1)}, bf16[960,128]{1,0:T(8,128)(2,1)S(1)}, u32[]{:S(2)}, u32[]{:S(2)}) collective-permute-start(bf16[960,128]{1,0:T(8,128)(2,1)} %get-tuple-element.41), channel_id=1, source_target_pairs={{0,7},{1,6},{2,5},{3,4},{4,3},{5,2},{6,1},{7,0},{8,15},{9,14},{10,... | collective-permute-start | bytes 737288 | tf_op jit(solution)/shard_map/ppermute | solution.py:392
  34.5 43.5 %collective-permute-start.1 = (bf16[128,2048]{1,0:T(8,128)(2,1)S(1)}, bf16[128,2048]{1,0:T(8,128)(2,1)S(1)}, u32[]{:S(2)}, u32[]{:S(2)}) collective-permute-start(bf16[128,2048]{1,0:T(8,128)(2,1)S(1)} %copy-done.23), channel_id=1, source_target_pairs={{0,1},{1,0},{2,3},{3,2},{4,5},{5,4},{6,7},{7,6},{8,9},{9,8},{10,11... | collective-permute-start | bytes 1572872 | tf_op jit(solution)/shard_map/ppermute | solution.py:420
  54.2 12.6 %collective-permute-start.11 = (bf16[8,192,128]{2,1,0:T(8,128)(2,1)}, bf16[8,192,128]{2,1,0:T(8,128)(2,1)S(1)}, u32[]{:S(2)}, u32[]{:S(2)}) collective-permute-start(bf16[8,192,128]{2,1,0:T(8,128)(2,1)} %gather.1.refs_24_), channel_id=1, source_target_pairs={{0,16},{8,24},{16,0},{24,8},{1,17},{9,25},{17,1},{25,9},{2,18},{10... | collective-permute-start | bytes 1179656 | tf_op jit(solution)/shard_map/ppermute | solution.py:396
  55.7 18.9 %collective-permute-start.13 = (bf16[768,128]{1,0:T(8,128)(2,1)}, bf16[768,128]{1,0:T(8,128)(2,1)S(1)}, u32[]{:S(2)}, u32[]{:S(2)}) collective-permute-start(bf16[768,128]{1,0:T(8,128)(2,1)} %get-tuple-element.42), channel_id=1, source_target_pairs={{0,4},{1,5},{2,6},{3,7},{4,0},{5,1},{6,2},{7,3},{8,12},{9,13},{10,... | collective-permute-start | bytes 589832 | tf_op jit(solution)/shard_map/ppermute | solution.py:392
  66.7 18.6 %collective-permute-start.10 = (bf16[8,192,128]{2,1,0:T(8,128)(2,1)}, bf16[8,192,128]{2,1,0:T(8,128)(2,1)S(1)}, u32[]{:S(2)}, u32[]{:S(2)}) collective-permute-start(bf16[8,192,128]{2,1,0:T(8,128)(2,1)} %gather.1.refs_24_), channel_id=1, source_target_pairs={{0,8},{8,0},{16,24},{24,16},{1,9},{9,1},{17,25},{25,17},{2,10},{10... | collective-permute-start | bytes 1179656 | tf_op jit(solution)/shard_map/ppermute | solution.py:396
  66.7 22.8 %collective-permute-start.12 = (bf16[8,192,128]{2,1,0:T(8,128)(2,1)S(1)}, bf16[8,192,128]{2,1,0:T(8,128)(2,1)S(1)}, u32[]{:S(2)}, u32[]{:S(2)}) collective-permute-start(bf16[8,192,128]{2,1,0:T(8,128)(2,1)S(1)} %collective-permute-done.11.refs_26_), channel_id=1, source_target_pairs={{0,8},{8,0},{16,24},{24,16},{1,9},{9,1},{17,25},{25,17},{2,10},{10... | collective-permute-start | bytes 1179656 | tf_op jit(solution)/shard_map/ppermute | solution.py:396
  67.2 17.3 %collective-permute-start.14 = (bf16[768,128]{1,0:T(8,128)(2,1)}, bf16[768,128]{1,0:T(8,128)(2,1)S(1)}, u32[]{:S(2)}, u32[]{:S(2)}) collective-permute-start(bf16[768,128]{1,0:T(8,128)(2,1)} %get-tuple-element.43), channel_id=1, source_target_pairs={{0,5},{1,4},{2,7},{3,6},{4,1},{5,0},{6,3},{7,2},{8,13},{9,12},{10,... | collective-permute-start | bytes 589832 | tf_op jit(solution)/shard_map/ppermute | solution.py:392
  74.5 32.4 %collective-permute-start = (bf16[128,2048]{1,0:T(8,128)(2,1)S(1)}, bf16[128,2048]{1,0:T(8,128)(2,1)S(1)}, u32[]{:S(2)}, u32[]{:S(2)}) collective-permute-start(bf16[128,2048]{1,0:T(8,128)(2,1)S(1)} %copy-done.22), channel_id=1, source_target_pairs={{0,1},{1,2},{2,3},{3,4},{4,5},{5,6},{6,7},{8,9},{9,10},{10,11},{11... | collective-permute-start | bytes 1572872 | tf_op jit(solution)/shard_map/ppermute | solution.py:419
  78.0 30.1 %collective-permute-start.2 = (bf16[128,2048]{1,0:T(8,128)(2,1)S(1)}, bf16[128,2048]{1,0:T(8,128)(2,1)}, u32[]{:S(2)}, u32[]{:S(2)}) collective-permute-start(bf16[128,2048]{1,0:T(8,128)(2,1)S(1)} %collective-permute-done.1.odd_ref), channel_id=1, source_target_pairs={{0,2},{2,4},{4,6},{8,10},{10,12},{12,14},{16,18},{18,20},{20,22},{... | collective-permute-start | bytes 1572872 | tf_op jit(solution)/shard_map/ppermute | solution.py:421
  84.5 14.8 %collective-permute-start.25 = (bf16[768,128]{1,0:T(8,128)(2,1)S(1)}, bf16[768,128]{1,0:T(8,128)(2,1)S(1)}, u32[]{:S(2)}, u32[]{:S(2)}) collective-permute-start(bf16[768,128]{1,0:T(8,128)(2,1)S(1)} %copy-done.40), channel_id=1, source_target_pairs={{0,6},{1,7},{2,4},{3,5},{4,2},{5,3},{6,0},{7,1},{8,14},{9,15},{10,... | collective-permute-start | bytes 589832 | tf_op jit(solution)/shard_map/ppermute | solution.py:392
  85.3 20.7 %collective-permute-start.26 = (bf16[768,128]{1,0:T(8,128)(2,1)S(1)}, bf16[768,128]{1,0:T(8,128)(2,1)S(1)}, u32[]{:S(2)}, u32[]{:S(2)}) collective-permute-start(bf16[768,128]{1,0:T(8,128)(2,1)S(1)} %copy-done.39), channel_id=1, source_target_pairs={{0,7},{1,6},{2,5},{3,4},{4,3},{5,2},{6,1},{7,0},{8,15},{9,14},{10,... | collective-permute-start | bytes 589832 | tf_op jit(solution)/shard_map/ppermute | solution.py:392
  99.2 13.0 %collective-permute-start.24 = (bf16[768,128]{1,0:T(8,128)(2,1)}, bf16[768,128]{1,0:T(8,128)(2,1)S(1)}, u32[]{:S(2)}, u32[]{:S(2)}) collective-permute-start(bf16[768,128]{1,0:T(8,128)(2,1)} %gate.5), channel_id=1, source_target_pairs={{0,3},{1,2},{2,1},{3,0},{4,7},{5,6},{6,5},{7,4},{8,11},{9,10},{10,... | collective-permute-start | bytes 589832 | tf_op jit(solution)/shard_map/ppermute | solution.py:392
  99.3 13.3 %collective-permute-start.23 = (bf16[768,128]{1,0:T(8,128)(2,1)}, bf16[768,128]{1,0:T(8,128)(2,1)S(1)}, u32[]{:S(2)}, u32[]{:S(2)}) collective-permute-start(bf16[768,128]{1,0:T(8,128)(2,1)} %gate.4), channel_id=1, source_target_pairs={{0,2},{1,3},{2,0},{3,1},{4,6},{5,7},{6,4},{7,5},{8,10},{9,11},{10,... | collective-permute-start | bytes 589832 | tf_op jit(solution)/shard_map/ppermute | solution.py:392
  106.0 24.2 %collective-permute-start.22 = (bf16[768,128]{1,0:T(8,128)(2,1)}, bf16[768,128]{1,0:T(8,128)(2,1)S(1)}, u32[]{:S(2)}, u32[]{:S(2)}) collective-permute-start(bf16[768,128]{1,0:T(8,128)(2,1)} %gate.3), channel_id=1, source_target_pairs={{0,1},{1,0},{2,3},{3,2},{4,5},{5,4},{6,7},{7,6},{8,9},{9,8},{10,11... | collective-permute-start | bytes 589832 | tf_op jit(solution)/shard_map/ppermute | solution.py:392
  107.0 32.9 %collective-permute-start.15 = (bf16[2,128,128]{2,1,0:T(8,128)(2,1)S(1)}, bf16[2,128,128]{2,1,0:T(8,128)(2,1)S(1)}, u32[]{:S(2)}, u32[]{:S(2)}) collective-permute-start(bf16[2,128,128]{2,1,0:T(8,128)(2,1)S(1)} %copy-done.47), channel_id=1, source_target_pairs={{0,1},{1,0},{2,3},{3,2},{4,5},{5,4},{6,7},{7,6},{8,9},{9,8},{10,11... | collective-permute-start | bytes 196616 | tf_op jit(solution)/shard_map/ppermute | solution.py:392
  108.2 34.0 %collective-permute-start.16 = (bf16[2,128,128]{2,1,0:T(8,128)(2,1)S(1)}, bf16[2,128,128]{2,1,0:T(8,128)(2,1)S(1)}, u32[]{:S(2)}, u32[]{:S(2)}) collective-permute-start(bf16[2,128,128]{2,1,0:T(8,128)(2,1)S(1)} %copy-done.46), channel_id=1, source_target_pairs={{0,2},{1,3},{2,0},{3,1},{4,6},{5,7},{6,4},{7,5},{8,10},{9,11},{10,... | collective-permute-start | bytes 196616 | tf_op jit(solution)/shard_map/ppermute | solution.py:392
  112.2 32.0 %collective-permute-start.17 = (bf16[2,128,128]{2,1,0:T(8,128)(2,1)S(1)}, bf16[2,128,128]{2,1,0:T(8,128)(2,1)S(1)}, u32[]{:S(2)}, u32[]{:S(2)}) collective-permute-start(bf16[2,128,128]{2,1,0:T(8,128)(2,1)S(1)} %copy-done.45), channel_id=1, source_target_pairs={{0,3},{1,2},{2,1},{3,0},{4,7},{5,6},{6,5},{7,4},{8,11},{9,10},{10,... | collective-permute-start | bytes 196616 | tf_op jit(solution)/shard_map/ppermute | solution.py:392
  112.6 32.8 %collective-permute-start.18 = (bf16[2,128,128]{2,1,0:T(8,128)(2,1)S(1)}, bf16[2,128,128]{2,1,0:T(8,128)(2,1)S(1)}, u32[]{:S(2)}, u32[]{:S(2)}) collective-permute-start(bf16[2,128,128]{2,1,0:T(8,128)(2,1)S(1)} %copy-done.44), channel_id=1, source_target_pairs={{0,4},{1,5},{2,6},{3,7},{4,0},{5,1},{6,2},{7,3},{8,12},{9,13},{10,... | collective-permute-start | bytes 196616 | tf_op jit(solution)/shard_map/ppermute | solution.py:392
  130.3 15.1 %collective-permute-start.19 = (bf16[2,128,128]{2,1,0:T(8,128)(2,1)S(1)}, bf16[2,128,128]{2,1,0:T(8,128)(2,1)S(1)}, u32[]{:S(2)}, u32[]{:S(2)}) collective-permute-start(bf16[2,128,128]{2,1,0:T(8,128)(2,1)S(1)} %copy-done.43), channel_id=1, source_target_pairs={{0,5},{1,4},{2,7},{3,6},{4,1},{5,0},{6,3},{7,2},{8,13},{9,12},{10,... | collective-permute-start | bytes 196616 | tf_op jit(solution)/shard_map/ppermute | solution.py:392
  (58 other events, 645.5 us)

commit v5 on v4

--- a/solution.py
+++ b/solution.py
@@ -40,6 +40,7 @@
     tiles = []
     for tile in range(lanes // LANES):
         columns = extended[:, tile * LANES : (tile + 1) * LANES]
+        twice = jnp.concatenate([columns, columns], axis=0)
         convolved = jnp.zeros((rows, LANES), f32)
         for group in range(groups):
             line = tile * groups + group
@@ -47,9 +48,7 @@
             taps = pltpu.roll(wave, 0, 1, stride=1, stride_axis=0)
             high = taps.astype(bf16)
             low = (taps - high.astype(f32)).astype(bf16)
-            term = jnp.dot(high, columns, preferred_element_type=f32) + jnp.dot(
-                low, columns, preferred_element_type=f32
-            )
+            term = jnp.dot(jnp.concatenate([high, low], axis=1), twice, preferred_element_type=f32)
             convolved = jnp.where(channel == group, term, convolved)
         tiles.append(convolved)
     convolved = jnp.concatenate(tiles, axis=1)

time: 165 us -> 165 us (level)
  no operation moved by 1% of the time
where the time goes in v5:
time: 165 us
  starting transfers between devices  79.9 us (48%)
  Pallas kernels  42.7 us (26%)
  waiting for transfers between devices  32.9 us (20%)
  local copies, waits for them, and re-layouts  5.97 us (4%)
  between operations  1.89 us (1%)
    ppermute x28, starting transfers between devices, exchange(): parts[k] = lax.ppermute(parts[k], 'seq', [(i, i ^ k) for i in range(peers)])  69.8 us
    ppermute x28, waiting for transfers between devices, exchange(): parts[k] = lax.ppermute(parts[k], 'seq', [(i, i ^ k) for i in range(peers)])  32.8 us
    pallas_call x2, Pallas kernels, attend_wave(): pl.pallas_call(functools.partial(wave_kernel, wave, peers), grid_spec=plt...  17.9 us
    pallas_call x1, Pallas kernels, hyena(): pl.pallas_call(hyena_kernel, grid=(channels // lanes,), out_shape=jax.Sha...  12.4 us
    pallas_call x1, Pallas kernels, pack(): pl.pallas_call(functools.partial(pack_kernel, peers), grid_spec=pltpu.Pre...  7.29 us
    ppermute x1, starting transfers between devices, brought(): near = lax.ppermute(near, 'seq', [(i, i + 1) for i in range(peers - 1)])  3.45 us
  transfers between devices with their start and end apart: 34, of which 8 were waited for; matrix products, arithmetic and copies ran while one was open for 3% of the time, Pallas kernels for 20%

profile of v5, /device:TPU:0, one launch (start us, length us, event | category | flops | bytes accessed | tf_op | source)
XLA Modules:
  0.0 164.8 jit_solution(6979274464468586950)
XLA Ops:
  1.8 7.3 %pack.1 = (bf16[960,128]{1,0:T(8,128)(2,1)}, bf16[960,128]{1,0:T(8,128)(2,1)}, bf16[960,128]{1,0:T(8,128)(2,1)}, bf16[960,128]{1,0:T(8,128)(2,1)}, bf16[960,128]...) custom-call(s32[3]{0:T(128)} %pad_add_fusion.1.side_ref, ...), custom_call_target="tpu_custom_call" | custom-call | flops 1 | bytes 1 | tf_op jit(solution)/shard_map/pack/pallas_call | solution.py:203
  9.1 3.0 %collective-permute-start.3 = (bf16[960,128]{1,0:T(8,128)(2,1)}, bf16[960,128]{1,0:T(8,128)(2,1)S(1)}, u32[]{:S(2)}, u32[]{:S(2)}) collective-permute-start(bf16[960,128]{1,0:T(8,128)(2,1)} %get-tuple-element.35), channel_id=1, source_target_pairs={{0,1},{1,0},{2,3},{3,2},{4,5},{5,4},{6,7},{7,6},{8,9},{9,8},{10,11... | collective-permute-start | bytes 737288 | tf_op jit(solution)/shard_map/ppermute | solution.py:391
  13.8 3.0 %collective-permute-start.6 = (bf16[960,128]{1,0:T(8,128)(2,1)}, bf16[960,128]{1,0:T(8,128)(2,1)S(1)}, u32[]{:S(2)}, u32[]{:S(2)}) collective-permute-start(bf16[960,128]{1,0:T(8,128)(2,1)} %get-tuple-element.38), channel_id=1, source_target_pairs={{0,4},{1,5},{2,6},{3,7},{4,0},{5,1},{6,2},{7,3},{8,12},{9,13},{10,... | collective-permute-start | bytes 737288 | tf_op jit(solution)/shard_map/ppermute | solution.py:391
  18.3 3.8 %collective-permute-start.8 = (bf16[960,128]{1,0:T(8,128)(2,1)}, bf16[960,128]{1,0:T(8,128)(2,1)S(1)}, u32[]{:S(2)}, u32[]{:S(2)}) collective-permute-start(bf16[960,128]{1,0:T(8,128)(2,1)} %get-tuple-element.40), channel_id=1, source_target_pairs={{0,6},{1,7},{2,4},{3,5},{4,2},{5,3},{6,0},{7,1},{8,14},{9,15},{10,... | collective-permute-start | bytes 737288 | tf_op jit(solution)/shard_map/ppermute | solution.py:391
  22.2 8.7 %collective-permute-done.4.refs_2_.refs_6_.refs_7_.refs_8_ = bf16[960,128]{1,0:T(8,128)(2,1)S(1)} collective-permute-done((bf16[960,128]{1,0:T(8,128)(2,1)}, bf16[960,128]{1,0:T(8,128)(2,1)S(1)}, u32[]{:S(2)}, u32[]{:S(2)}) %collective-permute-start.4) | collective-permute-done | bytes 245792 | tf_op jit(solution)/shard_map/ppermute | solution.py:391
  34.5 2.6 %collective-permute-start.1 = (bf16[128,2048]{1,0:T(8,128)(2,1)S(1)}, bf16[128,2048]{1,0:T(8,128)(2,1)S(1)}, u32[]{:S(2)}, u32[]{:S(2)}) collective-permute-start(bf16[128,2048]{1,0:T(8,128)(2,1)S(1)} %copy-done.23), channel_id=1, source_target_pairs={{0,1},{1,0},{2,3},{3,2},{4,5},{5,4},{6,7},{7,6},{8,9},{9,8},{10,11... | collective-permute-start | bytes 1572872 | tf_op jit(solution)/shard_map/ppermute | solution.py:419
  37.9 13.5 %collective-permute-done.7.refs_5_.refs_15_.refs_16_.refs_17_ = bf16[960,128]{1,0:T(8,128)(2,1)S(1)} collective-permute-done((bf16[960,128]{1,0:T(8,128)(2,1)}, bf16[960,128]{1,0:T(8,128)(2,1)S(1)}, u32[]{:S(2)}, u32[]{:S(2)}) %collective-permute-start.7) | collective-permute-done | bytes 245792 | tf_op jit(solution)/shard_map/ppermute | solution.py:391
  55.7 11.1 %collective-permute-start.13 = (bf16[768,128]{1,0:T(8,128)(2,1)}, bf16[768,128]{1,0:T(8,128)(2,1)S(1)}, u32[]{:S(2)}, u32[]{:S(2)}) collective-permute-start(bf16[768,128]{1,0:T(8,128)(2,1)} %get-tuple-element.42), channel_id=1, source_target_pairs={{0,4},{1,5},{2,6},{3,7},{4,0},{5,1},{6,2},{7,3},{8,12},{9,13},{10,... | collective-permute-start | bytes 589832 | tf_op jit(solution)/shard_map/ppermute | solution.py:391
  67.2 7.3 %collective-permute-start.14 = (bf16[768,128]{1,0:T(8,128)(2,1)}, bf16[768,128]{1,0:T(8,128)(2,1)S(1)}, u32[]{:S(2)}, u32[]{:S(2)}) collective-permute-start(bf16[768,128]{1,0:T(8,128)(2,1)} %get-tuple-element.43), channel_id=1, source_target_pairs={{0,5},{1,4},{2,7},{3,6},{4,1},{5,0},{6,3},{7,2},{8,13},{9,12},{10,... | collective-permute-start | bytes 589832 | tf_op jit(solution)/shard_map/ppermute | solution.py:391
  74.5 3.5 %collective-permute-start = (bf16[128,2048]{1,0:T(8,128)(2,1)S(1)}, bf16[128,2048]{1,0:T(8,128)(2,1)S(1)}, u32[]{:S(2)}, u32[]{:S(2)}) collective-permute-start(bf16[128,2048]{1,0:T(8,128)(2,1)S(1)} %copy-done.22), channel_id=1, source_target_pairs={{0,1},{1,2},{2,3},{3,4},{4,5},{5,6},{6,7},{8,9},{9,10},{10,11},{11... | collective-permute-start | bytes 1572872 | tf_op jit(solution)/shard_map/ppermute | solution.py:418
  78.0 2.1 %collective-permute-start.2 = (bf16[128,2048]{1,0:T(8,128)(2,1)S(1)}, bf16[128,2048]{1,0:T(8,128)(2,1)}, u32[]{:S(2)}, u32[]{:S(2)}) collective-permute-start(bf16[128,2048]{1,0:T(8,128)(2,1)S(1)} %collective-permute-done.1.odd_ref), channel_id=1, source_target_pairs={{0,2},{2,4},{4,6},{8,10},{10,12},{12,14},{16,18},{18,20},{20,22},{... | collective-permute-start | bytes 1572872 | tf_op jit(solution)/shard_map/ppermute | solution.py:420
  80.1 4.4 %collective-permute-done.14.refs_29_.refs_15_.refs_16_.refs_17_ = bf16[768,128]{1,0:T(8,128)(2,1)S(1)} collective-permute-done((bf16[768,128]{1,0:T(8,128)(2,1)}, bf16[768,128]{1,0:T(8,128)(2,1)S(1)}, u32[]{:S(2)}, u32[]{:S(2)}) %collective-permute-start.14) | collective-permute-done | bytes 196640 | tf_op jit(solution)/shard_map/ppermute | solution.py:391
  85.3 4.2 %collective-permute-start.26 = (bf16[768,128]{1,0:T(8,128)(2,1)S(1)}, bf16[768,128]{1,0:T(8,128)(2,1)S(1)}, u32[]{:S(2)}, u32[]{:S(2)}) collective-permute-start(bf16[768,128]{1,0:T(8,128)(2,1)S(1)} %copy-done.39), channel_id=1, source_target_pairs={{0,7},{1,6},{2,5},{3,4},{4,3},{5,2},{6,1},{7,0},{8,15},{9,14},{10,... | collective-permute-start | bytes 589832 | tf_op jit(solution)/shard_map/ppermute | solution.py:391
  90.3 8.9 %attend_wave.2 = (bf16[2,128,128]{2,1,0:T(8,128)(2,1)}, bf16[2,128,128]{2,1,0:T(8,128)(2,1)}, bf16[2,128,128]{2,1,0:T(8,128)(2,1)}, bf16[2,128,128]{2,1,0:T(8,12...) custom-call(s32[3]{0:T(128)} %pad_add_fusion.1.side_ref, ...), custom_call_target="tpu_custom_call" | custom-call | flops 1 | bytes 1 | tf_op jit(solution)/shard_map/attend_wave/pallas_call | solution.py:334
  99.3 6.7 %collective-permute-start.23 = (bf16[768,128]{1,0:T(8,128)(2,1)}, bf16[768,128]{1,0:T(8,128)(2,1)S(1)}, u32[]{:S(2)}, u32[]{:S(2)}) collective-permute-start(bf16[768,128]{1,0:T(8,128)(2,1)} %gate.4), channel_id=1, source_target_pairs={{0,2},{1,3},{2,0},{3,1},{4,6},{5,7},{6,4},{7,5},{8,10},{9,11},{10,... | collective-permute-start | bytes 589832 | tf_op jit(solution)/shard_map/ppermute | solution.py:391
  108.2 4.0 %collective-permute-start.16 = (bf16[2,128,128]{2,1,0:T(8,128)(2,1)S(1)}, bf16[2,128,128]{2,1,0:T(8,128)(2,1)S(1)}, u32[]{:S(2)}, u32[]{:S(2)}) collective-permute-start(bf16[2,128,128]{2,1,0:T(8,128)(2,1)S(1)} %copy-done.46), channel_id=1, source_target_pairs={{0,2},{1,3},{2,0},{3,1},{4,6},{5,7},{6,4},{7,5},{8,10},{9,11},{10,... | collective-permute-start | bytes 196616 | tf_op jit(solution)/shard_map/ppermute | solution.py:391
  112.6 4.5 %collective-permute-start.18 = (bf16[2,128,128]{2,1,0:T(8,128)(2,1)S(1)}, bf16[2,128,128]{2,1,0:T(8,128)(2,1)S(1)}, u32[]{:S(2)}, u32[]{:S(2)}) collective-permute-start(bf16[2,128,128]{2,1,0:T(8,128)(2,1)S(1)} %copy-done.44), channel_id=1, source_target_pairs={{0,4},{1,5},{2,6},{3,7},{4,0},{5,1},{6,2},{7,3},{8,12},{9,13},{10,... | collective-permute-start | bytes 196616 | tf_op jit(solution)/shard_map/ppermute | solution.py:391
  117.8 12.4 %hyena.1.refs_28_ = bf16[1,128,4096]{2,1,0:T(8,128)(2,1)} custom-call(s32[2]{0:T(128)} %pad_add_fusion.place_ref, bf16[1,128,4096]{2,1,0:T(8,128)(2,1)} %query_ref.1, bf16[1,128,4096]{2,1,0:T(8,128)(2,1)} %key_ref.1, bf16[1,128,4096]{2,1,0:T(8,128)(2,1)} %value_ref.1, bf16[128,2048]{1,0:T(8,128)(2,1)} %copy-done.21, ...), custom_call_target="tpu_custom_call" | custom-call | flops 1 | bytes 1 | tf_op jit(solution)/shard_map/hyena/pallas_call | solution.py:68
  130.9 9.0 %attend_wave.3 = (bf16[2,128,128]{2,1,0:T(8,128)(2,1)}, bf16[2,128,128]{2,1,0:T(8,128)(2,1)}, bf16[2,128,128]{2,1,0:T(8,128)(2,1)}, bf16[2,128,128]{2,1,0:T(8,12...) custom-call(s32[3]{0:T(128)} %pad_add_fusion.1.side_ref, ...), custom_call_target="tpu_custom_call" | custom-call | flops 1 | bytes 1 | tf_op jit(solution)/shard_map/attend_wave/pallas_call | solution.py:334
  140.0 2.2 %collective-permute-start.20 = (bf16[2,128,128]{2,1,0:T(8,128)(2,1)S(1)}, bf16[2,128,128]{2,1,0:T(8,128)(2,1)S(1)}, u32[]{:S(2)}, u32[]{:S(2)}) collective-permute-start(bf16[2,128,128]{2,1,0:T(8,128)(2,1)S(1)} %copy-done.42), channel_id=1, source_target_pairs={{0,6},{1,7},{2,4},{3,5},{4,2},{5,3},{6,0},{7,1},{8,14},{9,15},{10,... | collective-permute-start | bytes 196616 | tf_op jit(solution)/shard_map/ppermute | solution.py:391
  145.4 2.3 %collective-permute-start.29 = (bf16[2,128,128]{2,1,0:T(8,128)(2,1)}, bf16[2,128,128]{2,1,0:T(8,128)(2,1)S(1)}, u32[]{:S(2)}, u32[]{:S(2)}) collective-permute-start(bf16[2,128,128]{2,1,0:T(8,128)(2,1)} %get-tuple-element.61), channel_id=1, source_target_pairs={{0,3},{1,2},{2,1},{3,0},{4,7},{5,6},{6,5},{7,4},{8,11},{9,10},{10,... | collective-permute-start | bytes 196616 | tf_op jit(solution)/shard_map/ppermute | solution.py:391
  151.3 2.1 %collective-permute-start.32 = (bf16[2,128,128]{2,1,0:T(8,128)(2,1)}, bf16[2,128,128]{2,1,0:T(8,128)(2,1)S(1)}, u32[]{:S(2)}, u32[]{:S(2)}) collective-permute-start(bf16[2,128,128]{2,1,0:T(8,128)(2,1)} %get-tuple-element.64), channel_id=1, source_target_pairs={{0,6},{1,7},{2,4},{3,5},{4,2},{5,3},{6,0},{7,1},{8,14},{9,15},{10,... | collective-permute-start | bytes 196616 | tf_op jit(solution)/shard_map/ppermute | solution.py:391
  156.6 2.6 %collective-permute-done.31.refs_13_ = bf16[2,128,128]{2,1,0:T(8,128)(2,1)S(1)} collective-permute-done((bf16[2,128,128]{2,1,0:T(8,128)(2,1)}, bf16[2,128,128]{2,1,0:T(8,128)(2,1)S(1)}, u32[]{:S(2)}, u32[]{:S(2)}) %collective-permute-start.31) | collective-permute-done | bytes 65568 | tf_op jit(solution)/shard_map/ppermute | solution.py:391
  161.3 3.3 %unpack.1 = bf16[128,32,128]{2,1,0:T(8,128)(2,1)} custom-call(s32[3]{0:T(128)} %pad_add_fusion.1.side_ref, bf16[2,128,128]{2,1,0:T(8,128)(2,1)} %get-tuple-element.44.refs_0_.refs_1_, bf16[2,128,128]{2,1,0:T(8,128)(2,1)} %copy-done.25, bf16[2,128,128]{2,1,0:T(8,128)(2,1)} %copy-done.26, bf16[2,128,128]{2,1,0:T(8,128)(2,1)} %copy-done.27, ...), custom_call_target="tpu_custom_call" | custom-call | flops 1 | bytes 1 | tf_op jit(solution)/shard_map/unpack/pallas_call | solution.py:367
  (157 shorter events, 30.4 us)
Async XLA Ops:
  12.2 18.7 %collective-permute-start.4 = (bf16[960,128]{1,0:T(8,128)(2,1)}, bf16[960,128]{1,0:T(8,128)(2,1)S(1)}, u32[]{:S(2)}, u32[]{:S(2)}) collective-permute-start(bf16[960,128]{1,0:T(8,128)(2,1)} %get-tuple-element.36), channel_id=1, source_target_pairs={{0,2},{1,3},{2,0},{3,1},{4,6},{5,7},{6,4},{7,5},{8,10},{9,11},{10,... | collective-permute-start | bytes 737288 | tf_op jit(solution)/shard_map/ppermute | solution.py:391
  13.8 20.8 %collective-permute-start.5 = (bf16[960,128]{1,0:T(8,128)(2,1)}, bf16[960,128]{1,0:T(8,128)(2,1)S(1)}, u32[]{:S(2)}, u32[]{:S(2)}) collective-permute-start(bf16[960,128]{1,0:T(8,128)(2,1)} %get-tuple-element.37), channel_id=1, source_target_pairs={{0,3},{1,2},{2,1},{3,0},{4,7},{5,6},{6,5},{7,4},{8,11},{9,10},{10,... | collective-permute-start | bytes 737288 | tf_op jit(solution)/shard_map/ppermute | solution.py:391
  13.8 24.2 %collective-permute-start.6 = (bf16[960,128]{1,0:T(8,128)(2,1)}, bf16[960,128]{1,0:T(8,128)(2,1)S(1)}, u32[]{:S(2)}, u32[]{:S(2)}) collective-permute-start(bf16[960,128]{1,0:T(8,128)(2,1)} %get-tuple-element.38), channel_id=1, source_target_pairs={{0,4},{1,5},{2,6},{3,7},{4,0},{5,1},{6,2},{7,3},{8,12},{9,13},{10,... | collective-permute-start | bytes 737288 | tf_op jit(solution)/shard_map/ppermute | solution.py:391
  16.7 34.7 %collective-permute-start.7 = (bf16[960,128]{1,0:T(8,128)(2,1)}, bf16[960,128]{1,0:T(8,128)(2,1)S(1)}, u32[]{:S(2)}, u32[]{:S(2)}) collective-permute-start(bf16[960,128]{1,0:T(8,128)(2,1)} %get-tuple-element.39), channel_id=1, source_target_pairs={{0,5},{1,4},{2,7},{3,6},{4,1},{5,0},{6,3},{7,2},{8,13},{9,12},{10,... | collective-permute-start | bytes 737288 | tf_op jit(solution)/shard_map/ppermute | solution.py:391
  18.3 33.1 %collective-permute-start.8 = (bf16[960,128]{1,0:T(8,128)(2,1)}, bf16[960,128]{1,0:T(8,128)(2,1)S(1)}, u32[]{:S(2)}, u32[]{:S(2)}) collective-permute-start(bf16[960,128]{1,0:T(8,128)(2,1)} %get-tuple-element.40), channel_id=1, source_target_pairs={{0,6},{1,7},{2,4},{3,5},{4,2},{5,3},{6,0},{7,1},{8,14},{9,15},{10,... | collective-permute-start | bytes 737288 | tf_op jit(solution)/shard_map/ppermute | solution.py:391
  30.9 20.6 %collective-permute-start.9 = (bf16[960,128]{1,0:T(8,128)(2,1)}, bf16[960,128]{1,0:T(8,128)(2,1)S(1)}, u32[]{:S(2)}, u32[]{:S(2)}) collective-permute-start(bf16[960,128]{1,0:T(8,128)(2,1)} %get-tuple-element.41), channel_id=1, source_target_pairs={{0,7},{1,6},{2,5},{3,4},{4,3},{5,2},{6,1},{7,0},{8,15},{9,14},{10,... | collective-permute-start | bytes 737288 | tf_op jit(solution)/shard_map/ppermute | solution.py:391
  34.5 43.5 %collective-permute-start.1 = (bf16[128,2048]{1,0:T(8,128)(2,1)S(1)}, bf16[128,2048]{1,0:T(8,128)(2,1)S(1)}, u32[]{:S(2)}, u32[]{:S(2)}) collective-permute-start(bf16[128,2048]{1,0:T(8,128)(2,1)S(1)} %copy-done.23), channel_id=1, source_target_pairs={{0,1},{1,0},{2,3},{3,2},{4,5},{5,4},{6,7},{7,6},{8,9},{9,8},{10,11... | collective-permute-start | bytes 1572872 | tf_op jit(solution)/shard_map/ppermute | solution.py:419
  54.2 12.6 %collective-permute-start.11 = (bf16[8,192,128]{2,1,0:T(8,128)(2,1)}, bf16[8,192,128]{2,1,0:T(8,128)(2,1)S(1)}, u32[]{:S(2)}, u32[]{:S(2)}) collective-permute-start(bf16[8,192,128]{2,1,0:T(8,128)(2,1)} %gather.1.refs_24_), channel_id=1, source_target_pairs={{0,16},{8,24},{16,0},{24,8},{1,17},{9,25},{17,1},{25,9},{2,18},{10... | collective-permute-start | bytes 1179656 | tf_op jit(solution)/shard_map/ppermute | solution.py:395
  55.7 18.9 %collective-permute-start.13 = (bf16[768,128]{1,0:T(8,128)(2,1)}, bf16[768,128]{1,0:T(8,128)(2,1)S(1)}, u32[]{:S(2)}, u32[]{:S(2)}) collective-permute-start(bf16[768,128]{1,0:T(8,128)(2,1)} %get-tuple-element.42), channel_id=1, source_target_pairs={{0,4},{1,5},{2,6},{3,7},{4,0},{5,1},{6,2},{7,3},{8,12},{9,13},{10,... | collective-permute-start | bytes 589832 | tf_op jit(solution)/shard_map/ppermute | solution.py:391
  66.7 18.6 %collective-permute-start.10 = (bf16[8,192,128]{2,1,0:T(8,128)(2,1)}, bf16[8,192,128]{2,1,0:T(8,128)(2,1)S(1)}, u32[]{:S(2)}, u32[]{:S(2)}) collective-permute-start(bf16[8,192,128]{2,1,0:T(8,128)(2,1)} %gather.1.refs_24_), channel_id=1, source_target_pairs={{0,8},{8,0},{16,24},{24,16},{1,9},{9,1},{17,25},{25,17},{2,10},{10... | collective-permute-start | bytes 1179656 | tf_op jit(solution)/shard_map/ppermute | solution.py:395
  66.7 22.8 %collective-permute-start.12 = (bf16[8,192,128]{2,1,0:T(8,128)(2,1)S(1)}, bf16[8,192,128]{2,1,0:T(8,128)(2,1)S(1)}, u32[]{:S(2)}, u32[]{:S(2)}) collective-permute-start(bf16[8,192,128]{2,1,0:T(8,128)(2,1)S(1)} %collective-permute-done.11.refs_26_), channel_id=1, source_target_pairs={{0,8},{8,0},{16,24},{24,16},{1,9},{9,1},{17,25},{25,17},{2,10},{10... | collective-permute-start | bytes 1179656 | tf_op jit(solution)/shard_map/ppermute | solution.py:395
  67.2 17.3 %collective-permute-start.14 = (bf16[768,128]{1,0:T(8,128)(2,1)}, bf16[768,128]{1,0:T(8,128)(2,1)S(1)}, u32[]{:S(2)}, u32[]{:S(2)}) collective-permute-start(bf16[768,128]{1,0:T(8,128)(2,1)} %get-tuple-element.43), channel_id=1, source_target_pairs={{0,5},{1,4},{2,7},{3,6},{4,1},{5,0},{6,3},{7,2},{8,13},{9,12},{10,... | collective-permute-start | bytes 589832 | tf_op jit(solution)/shard_map/ppermute | solution.py:391
  74.5 32.4 %collective-permute-start = (bf16[128,2048]{1,0:T(8,128)(2,1)S(1)}, bf16[128,2048]{1,0:T(8,128)(2,1)S(1)}, u32[]{:S(2)}, u32[]{:S(2)}) collective-permute-start(bf16[128,2048]{1,0:T(8,128)(2,1)S(1)} %copy-done.22), channel_id=1, source_target_pairs={{0,1},{1,2},{2,3},{3,4},{4,5},{5,6},{6,7},{8,9},{9,10},{10,11},{11... | collective-permute-start | bytes 1572872 | tf_op jit(solution)/shard_map/ppermute | solution.py:418
  78.0 30.1 %collective-permute-start.2 = (bf16[128,2048]{1,0:T(8,128)(2,1)S(1)}, bf16[128,2048]{1,0:T(8,128)(2,1)}, u32[]{:S(2)}, u32[]{:S(2)}) collective-permute-start(bf16[128,2048]{1,0:T(8,128)(2,1)S(1)} %collective-permute-done.1.odd_ref), channel_id=1, source_target_pairs={{0,2},{2,4},{4,6},{8,10},{10,12},{12,14},{16,18},{18,20},{20,22},{... | collective-permute-start | bytes 1572872 | tf_op jit(solution)/shard_map/ppermute | solution.py:420
  84.5 14.8 %collective-permute-start.25 = (bf16[768,128]{1,0:T(8,128)(2,1)S(1)}, bf16[768,128]{1,0:T(8,128)(2,1)S(1)}, u32[]{:S(2)}, u32[]{:S(2)}) collective-permute-start(bf16[768,128]{1,0:T(8,128)(2,1)S(1)} %copy-done.40), channel_id=1, source_target_pairs={{0,6},{1,7},{2,4},{3,5},{4,2},{5,3},{6,0},{7,1},{8,14},{9,15},{10,... | collective-permute-start | bytes 589832 | tf_op jit(solution)/shard_map/ppermute | solution.py:391
  85.3 20.7 %collective-permute-start.26 = (bf16[768,128]{1,0:T(8,128)(2,1)S(1)}, bf16[768,128]{1,0:T(8,128)(2,1)S(1)}, u32[]{:S(2)}, u32[]{:S(2)}) collective-permute-start(bf16[768,128]{1,0:T(8,128)(2,1)S(1)} %copy-done.39), channel_id=1, source_target_pairs={{0,7},{1,6},{2,5},{3,4},{4,3},{5,2},{6,1},{7,0},{8,15},{9,14},{10,... | collective-permute-start | bytes 589832 | tf_op jit(solution)/shard_map/ppermute | solution.py:391
  99.2 13.0 %collective-permute-start.24 = (bf16[768,128]{1,0:T(8,128)(2,1)}, bf16[768,128]{1,0:T(8,128)(2,1)S(1)}, u32[]{:S(2)}, u32[]{:S(2)}) collective-permute-start(bf16[768,128]{1,0:T(8,128)(2,1)} %gate.5), channel_id=1, source_target_pairs={{0,3},{1,2},{2,1},{3,0},{4,7},{5,6},{6,5},{7,4},{8,11},{9,10},{10,... | collective-permute-start | bytes 589832 | tf_op jit(solution)/shard_map/ppermute | solution.py:391
  99.3 13.3 %collective-permute-start.23 = (bf16[768,128]{1,0:T(8,128)(2,1)}, bf16[768,128]{1,0:T(8,128)(2,1)S(1)}, u32[]{:S(2)}, u32[]{:S(2)}) collective-permute-start(bf16[768,128]{1,0:T(8,128)(2,1)} %gate.4), channel_id=1, source_target_pairs={{0,2},{1,3},{2,0},{3,1},{4,6},{5,7},{6,4},{7,5},{8,10},{9,11},{10,... | collective-permute-start | bytes 589832 | tf_op jit(solution)/shard_map/ppermute | solution.py:391
  106.0 24.2 %collective-permute-start.22 = (bf16[768,128]{1,0:T(8,128)(2,1)}, bf16[768,128]{1,0:T(8,128)(2,1)S(1)}, u32[]{:S(2)}, u32[]{:S(2)}) collective-permute-start(bf16[768,128]{1,0:T(8,128)(2,1)} %gate.3), channel_id=1, source_target_pairs={{0,1},{1,0},{2,3},{3,2},{4,5},{5,4},{6,7},{7,6},{8,9},{9,8},{10,11... | collective-permute-start | bytes 589832 | tf_op jit(solution)/shard_map/ppermute | solution.py:391
  107.0 32.9 %collective-permute-start.15 = (bf16[2,128,128]{2,1,0:T(8,128)(2,1)S(1)}, bf16[2,128,128]{2,1,0:T(8,128)(2,1)S(1)}, u32[]{:S(2)}, u32[]{:S(2)}) collective-permute-start(bf16[2,128,128]{2,1,0:T(8,128)(2,1)S(1)} %copy-done.47), channel_id=1, source_target_pairs={{0,1},{1,0},{2,3},{3,2},{4,5},{5,4},{6,7},{7,6},{8,9},{9,8},{10,11... | collective-permute-start | bytes 196616 | tf_op jit(solution)/shard_map/ppermute | solution.py:391
  108.2 34.0 %collective-permute-start.16 = (bf16[2,128,128]{2,1,0:T(8,128)(2,1)S(1)}, bf16[2,128,128]{2,1,0:T(8,128)(2,1)S(1)}, u32[]{:S(2)}, u32[]{:S(2)}) collective-permute-start(bf16[2,128,128]{2,1,0:T(8,128)(2,1)S(1)} %copy-done.46), channel_id=1, source_target_pairs={{0,2},{1,3},{2,0},{3,1},{4,6},{5,7},{6,4},{7,5},{8,10},{9,11},{10,... | collective-permute-start | bytes 196616 | tf_op jit(solution)/shard_map/ppermute | solution.py:391
  112.2 32.0 %collective-permute-start.17 = (bf16[2,128,128]{2,1,0:T(8,128)(2,1)S(1)}, bf16[2,128,128]{2,1,0:T(8,128)(2,1)S(1)}, u32[]{:S(2)}, u32[]{:S(2)}) collective-permute-start(bf16[2,128,128]{2,1,0:T(8,128)(2,1)S(1)} %copy-done.45), channel_id=1, source_target_pairs={{0,3},{1,2},{2,1},{3,0},{4,7},{5,6},{6,5},{7,4},{8,11},{9,10},{10,... | collective-permute-start | bytes 196616 | tf_op jit(solution)/shard_map/ppermute | solution.py:391
  112.6 32.8 %collective-permute-start.18 = (bf16[2,128,128]{2,1,0:T(8,128)(2,1)S(1)}, bf16[2,128,128]{2,1,0:T(8,128)(2,1)S(1)}, u32[]{:S(2)}, u32[]{:S(2)}) collective-permute-start(bf16[2,128,128]{2,1,0:T(8,128)(2,1)S(1)} %copy-done.44), channel_id=1, source_target_pairs={{0,4},{1,5},{2,6},{3,7},{4,0},{5,1},{6,2},{7,3},{8,12},{9,13},{10,... | collective-permute-start | bytes 196616 | tf_op jit(solution)/shard_map/ppermute | solution.py:391
  130.3 15.1 %collective-permute-start.19 = (bf16[2,128,128]{2,1,0:T(8,128)(2,1)S(1)}, bf16[2,128,128]{2,1,0:T(8,128)(2,1)S(1)}, u32[]{:S(2)}, u32[]{:S(2)}) collective-permute-start(bf16[2,128,128]{2,1,0:T(8,128)(2,1)S(1)} %copy-done.43), channel_id=1, source_target_pairs={{0,5},{1,4},{2,7},{3,6},{4,1},{5,0},{6,3},{7,2},{8,13},{9,12},{10,... | collective-permute-start | bytes 196616 | tf_op jit(solution)/shard_map/ppermute | solution.py:391
  (58 other events, 645.6 us)
